TPU v7x, 32 devices: a whole 2x2x4 slice. The times are simulated.
32 devices in a mesh: fsdp: 8 (over y, x, core), blk: 4 (over z).
Axes of the slice: x: 2, y: 2, z: 4, core: 2. Of those that a mesh axis runs over, the one named last changes fastest.
Arguments:
- block_input: bfloat16 [32, 256, 2048], P('fsdp', 'blk'), may hold values from -6 to 6
- cotangent: bfloat16 [32, 256, 2048], P('fsdp', 'blk'), may hold values from -6 to 6
- bin_ids: int32 [32], P('fsdp'), may hold values from 0 to 63
- image_counts: int32 [8], P('fsdp'), may hold values from 1 to 4, as said below
- attn_weight: float32 [2048, 8192], P('fsdp')
- mlp_weight: float32 [2048, 16384], P('fsdp')
- noise_table: float32 [64, 2048], P(None, 'fsdp'), may hold values from -6 to 6
- mod_weight: float32 [2048, 12288], P('fsdp'), may hold values from -0.125 to 0.125
- mod_bias: float32 [12288], P('fsdp'), may hold values from -3 to 3
Outputs:
- block_out: bfloat16 [32, 256, 2048], P('fsdp', 'blk')
- input_grad: float32 [32, 256, 2048], P('fsdp', 'blk')
- attn_weight_grad: float32 [2048, 8192], P('fsdp')
- mlp_weight_grad: float32 [2048, 16384], P('fsdp')
- noise_grad: float32 [64, 2048], P(None, 'fsdp')
- mod_weight_grad: float32 [2048, 12288], P('fsdp')
- mod_bias_grad: float32 [12288], P('fsdp')
Inputs may be any that keep to these rules, and one draw needn't show every extreme that they name: `image_counts`: slots at and beyond the count hold no image; some index of fsdp holds all 4.
All inputs are finite; a program needn't handle non-finite values.
Results may differ from a plain program's by a relative error of at most 0.017.
Values may be sent and summed in bfloat16 or wider, within the bound.
A program may use at most 576 MiB of HBM per device.

v0:
```python
import jax
import jax.numpy as jnp
from jax import lax
from jax.sharding import PartitionSpec as P

HD = 128


EPSILON = 1e-06
PRECISE = lax.Precision.HIGHEST


def norm_mod(features, scaling, shifting):
    normed = features * lax.rsqrt(jnp.mean(features * features, axis=-1, keepdims=True) + EPSILON)
    return normed * (1.0 + scaling) + shifting


def rows_product(left_rows, right_rows):
    return lax.dot_general(
        left_rows, right_rows, (((0,), (0,)), ((), ())), preferred_element_type=jnp.float32
    )


def body(
    block_input,
    cotangent,
    bin_ids,
    image_counts,
    attn_weight,
    mlp_weight,
    noise_table,
    mod_weight,
    mod_bias,
):
    slot_count, local_tok, model_width = block_input.shape
    row_count = slot_count * local_tok
    feed_width = mlp_weight.shape[1] // 2
    head_count = model_width // HD
    blk_size = lax.axis_size("blk")
    image_tok = local_tok * blk_size
    score_scale = HD ** (-0.5)
    bias_piece = mod_bias.shape[0]
    activated = jax.nn.silu(noise_table)
    partial_mod = jnp.dot(activated, mod_weight, precision=PRECISE)
    bias_full = lax.dynamic_update_slice_in_dim(
        jnp.zeros((6 * model_width,), jnp.float32), mod_bias, lax.axis_index("fsdp") * bias_piece, 0
    )
    mod_table = lax.psum(partial_mod + bias_full[None, :], "fsdp")
    onehot = (
        bin_ids[:, None] == jnp.arange(noise_table.shape[0], dtype=jnp.int32)[None, :]
    ).astype(jnp.float32)
    mod_image = jnp.dot(onehot, mod_table, precision=PRECISE)
    shift_one, scale_one, gate_one, shift_two, scale_two, gate_two = [
        member[:, None, :] for member in jnp.split(mod_image, 6, axis=-1)
    ]
    live_mask = (jnp.arange(slot_count) < image_counts[0]).astype(jnp.float32)[:, None, None]
    features = block_input.astype(jnp.float32)
    h_one = (
        norm_mod(features, scale_one, shift_one)
        .astype(jnp.bfloat16)
        .reshape(row_count, model_width)
    )
    attn_full = lax.all_gather(attn_weight.astype(jnp.bfloat16), "fsdp", axis=0, tiled=True)
    projected = jnp.dot(
        h_one, attn_full[:, : 3 * model_width], preferred_element_type=jnp.float32
    ).astype(jnp.bfloat16)
    queries = projected[:, :model_width].reshape(slot_count, local_tok, head_count, HD)
    key_rows = projected[:, model_width : 2 * model_width].reshape(
        slot_count, local_tok, model_width
    )
    value_rows = projected[:, 2 * model_width :].reshape(slot_count, local_tok, model_width)
    all_keys, all_values = (
        lax.all_gather(key_rows, "blk", axis=1, tiled=True),
        lax.all_gather(value_rows, "blk", axis=1, tiled=True),
    )
    all_keys = all_keys.reshape(slot_count, image_tok, head_count, HD)
    all_values = all_values.reshape(slot_count, image_tok, head_count, HD)

    def scores_of(query_rows):
        return (
            jnp.einsum("sqhd,skhd->shqk", query_rows, all_keys, preferred_element_type=jnp.float32)
            * score_scale
        )

    scores = scores_of(queries)
    maximum = jnp.max(scores, axis=-1, keepdims=True)
    exponent = jnp.exp(scores - maximum)
    denominator = jnp.sum(exponent, axis=-1, keepdims=True)
    attention = exponent / denominator
    log_total = maximum + jnp.log(denominator)
    attended = (
        jnp.einsum(
            "shqk,skhd->sqhd",
            attention.astype(jnp.bfloat16),
            all_values,
            preferred_element_type=jnp.float32,
        )
        .astype(jnp.bfloat16)
        .reshape(row_count, model_width)
    )
    attn_out = jnp.dot(
        attended, attn_full[:, 3 * model_width :], preferred_element_type=jnp.float32
    ).reshape(slot_count, local_tok, model_width)
    first_sum = features + gate_one * attn_out
    h_two = (
        norm_mod(first_sum, scale_two, shift_two)
        .astype(jnp.bfloat16)
        .reshape(row_count, model_width)
    )
    mlp_full = lax.all_gather(mlp_weight.astype(jnp.bfloat16), "fsdp", axis=0, tiled=True)
    pre_gelu = jnp.dot(h_two, mlp_full[:, :feed_width], preferred_element_type=jnp.float32)
    hidden = jax.nn.gelu(pre_gelu).astype(jnp.bfloat16)
    mlp_out = jnp.einsum(
        "rf,df->rd", hidden, mlp_full[:, feed_width:], preferred_element_type=jnp.float32
    ).reshape(slot_count, local_tok, model_width)
    second_sum = first_sum + gate_two * mlp_out
    block_out = (live_mask * second_sum).astype(jnp.bfloat16)
    grad_out = cotangent.astype(jnp.float32) * live_mask
    grad_mlp = (gate_two * grad_out).astype(jnp.bfloat16).reshape(row_count, model_width)
    grad_gate_two = jnp.sum(grad_out * mlp_out, axis=1)
    grad_hidden = jnp.dot(grad_mlp, mlp_full[:, feed_width:], preferred_element_type=jnp.float32)
    grad_pre = jax.vjp(jax.nn.gelu, pre_gelu)[1](grad_hidden)[0].astype(jnp.bfloat16)
    grad_h_two = jnp.einsum(
        "rf,df->rd", grad_pre, mlp_full[:, :feed_width], preferred_element_type=jnp.float32
    ).reshape(slot_count, local_tok, model_width)
    grad_first, grad_scale_two, grad_shift_two = jax.vjp(norm_mod, first_sum, scale_two, shift_two)[
        1
    ](grad_h_two)
    grad_first = grad_first + grad_out
    grad_attn_out = (gate_one * grad_first).astype(jnp.bfloat16).reshape(row_count, model_width)
    grad_gate_one = jnp.sum(grad_first * attn_out, axis=1)
    grad_attended = jnp.einsum(
        "rd,ed->re",
        grad_attn_out,
        attn_full[:, 3 * model_width :],
        preferred_element_type=jnp.float32,
    ).astype(jnp.bfloat16)
    grad_heads = grad_attended.reshape(slot_count, local_tok, head_count, HD)
    recomputed = jnp.exp(scores_of(queries) - log_total)
    grad_weights = jnp.einsum(
        "sqhd,skhd->shqk", grad_heads, all_values, preferred_element_type=jnp.float32
    )
    row_delta = jnp.sum(recomputed * grad_weights, axis=-1, keepdims=True)
    grad_scores = (recomputed * (grad_weights - row_delta)).astype(jnp.bfloat16)
    grad_queries = (
        jnp.einsum("shqk,skhd->sqhd", grad_scores, all_keys, preferred_element_type=jnp.float32)
        * score_scale
    )
    grad_keys_all = (
        jnp.einsum("shqk,sqhd->skhd", grad_scores, queries, preferred_element_type=jnp.float32)
        * score_scale
    )
    grad_values_all = jnp.einsum(
        "shqk,sqhd->skhd",
        recomputed.astype(jnp.bfloat16),
        grad_heads,
        preferred_element_type=jnp.float32,
    )
    grad_keys, grad_values = (
        lax.psum_scatter(
            grad_keys_all.reshape(slot_count, image_tok, model_width).astype(jnp.bfloat16),
            "blk",
            scatter_dimension=1,
            tiled=True,
        ).astype(jnp.float32),
        lax.psum_scatter(
            grad_values_all.reshape(slot_count, image_tok, model_width).astype(jnp.bfloat16),
            "blk",
            scatter_dimension=1,
            tiled=True,
        ).astype(jnp.float32),
    )
    grad_qkv = jnp.concatenate(
        [
            grad_queries.reshape(row_count, model_width).astype(jnp.bfloat16),
            grad_keys.reshape(row_count, model_width).astype(jnp.bfloat16),
            grad_values.reshape(row_count, model_width).astype(jnp.bfloat16),
        ],
        axis=1,
    )
    grad_h_one = jnp.einsum(
        "rc,dc->rd", grad_qkv, attn_full[:, : 3 * model_width], preferred_element_type=jnp.float32
    ).reshape(slot_count, local_tok, model_width)
    grad_input, grad_scale_one, grad_shift_one = jax.vjp(norm_mod, features, scale_one, shift_one)[
        1
    ](grad_h_one)
    input_grad = grad_input + grad_first
    grad_mod = jnp.concatenate(
        [
            grad_shift_one[:, 0, :],
            grad_scale_one[:, 0, :],
            grad_gate_one,
            grad_shift_two[:, 0, :],
            grad_scale_two[:, 0, :],
            grad_gate_two,
        ],
        axis=-1,
    )
    bin_terms = lax.dot_general(onehot, grad_mod, (((0,), (0,)), ((), ())), precision=PRECISE)
    grad_bins = lax.psum(bin_terms, ("fsdp", "blk"))
    table_term = jnp.einsum("be,de->bd", grad_bins, mod_weight, precision=PRECISE)
    noise_grad = jax.vjp(jax.nn.silu, noise_table)[1](table_term)[0]
    mod_weight_grad = lax.dot_general(
        activated, grad_bins, (((0,), (0,)), ((), ())), precision=PRECISE
    )
    mod_bias_grad = lax.dynamic_slice_in_dim(
        jnp.sum(grad_bins, axis=0), lax.axis_index("fsdp") * bias_piece, bias_piece
    )
    h_part = h_one
    attn_part = lax.psum_scatter(
        jnp.concatenate(
            [rows_product(h_part, grad_qkv), rows_product(attended, grad_attn_out)], axis=1
        ).astype(jnp.bfloat16),
        "fsdp",
        scatter_dimension=0,
        tiled=True,
    )
    h_part = h_two
    mlp_part = lax.psum_scatter(
        jnp.concatenate(
            [rows_product(h_part, grad_pre), rows_product(grad_mlp, hidden)], axis=1
        ).astype(jnp.bfloat16),
        "fsdp",
        scatter_dimension=0,
        tiled=True,
    )
    attn_weight_grad, mlp_weight_grad = (
        lax.psum(attn_part, "blk").astype(jnp.float32),
        lax.psum(mlp_part, "blk").astype(jnp.float32),
    )
    return (
        block_out,
        input_grad,
        attn_weight_grad,
        mlp_weight_grad,
        noise_grad,
        mod_weight_grad,
        mod_bias_grad,
    )


def solution(mesh):
    return jax.shard_map(
        body,
        mesh=mesh,
        in_specs=(
            P("fsdp", "blk", None),
            P("fsdp", "blk", None),
            P("fsdp"),
            P("fsdp"),
            P("fsdp", None),
            P("fsdp", None),
            P(None, "fsdp"),
            P("fsdp", None),
            P("fsdp"),
        ),
        out_specs=(
            P("fsdp", "blk", None),
            P("fsdp", "blk", None),
            P("fsdp", None),
            P("fsdp", None),
            P(None, "fsdp"),
            P("fsdp", None),
            P("fsdp"),
        ),
        check_vma=False,
    )
```

profile of v0, /device:TPU:0, one launch (start us, length us, event | category | flops | bytes accessed | tf_op | source)
XLA Modules:
  0.0 2220.2 jit_solution(969000613093661028)
XLA Ops:
  8.1 11.7 convolution_add_fusion
  27.4 64.8 %all-reduce.5.cloned.1.call-done = f32[64,12288]{1,0:T(8,128)} async-done(((f32[64,12288]{1,0:T(8,128)}), f32[64,12288]{1,0:T(8,128)}) %all-reduce.5.cloned.1.call-update) | async-done | bytes 3145744 | tf_op jit(solution)/shard_map/psum | solution.py:48
  95.7 160.0 %all-gather.5.cloned.1.call-done = bf16[2048,8192]{1,0:T(8,128)(2,1)} async-done(((bf16[256,8192]{1,0:T(8,128)(2,1)}), bf16[2048,8192]{1,0:T(8,128)(2,1)}) %all-gather.5.cloned.1.call-update) | async-done | bytes 33554448 | tf_op jit(solution)/shard_map/all_gather | solution.py:63
  255.7 11.6 fusion.21
  273.5 9.5 convert_element_type.116
  284.2 67.2 %all-gather.7.cloned.1.call-done = bf16[4,256,2048]{2,0,1:T(4,128)(2,1)} async-done(((bf16[4,64,2048]{2,0,1:T(4,128)(2,1)}), bf16[4,256,2048]{2,0,1:T(4,128)(2,1)}) %all-gather.7.cloned.1.call-update) | async-done | bytes 4194320 | tf_op jit(solution)/shard_map/all_gather | solution.py:74
  351.3 7.5 copy.38
  358.8 73.9 %all-gather.9.cloned.1.call-done = bf16[4,256,2048]{2,0,1:T(4,128)(2,1)} async-done(((bf16[4,64,2048]{2,0,1:T(4,128)(2,1)}), bf16[4,256,2048]{2,0,1:T(4,128)(2,1)}) %all-gather.9.cloned.1.call-update) | async-done | bytes 4194320 | tf_op jit(solution)/shard_map/all_gather | solution.py:73
  432.7 7.5 copy.40
  451.5 9.8 multiply_reduce_fusion.5
  463.1 273.5 %all-gather.11.cloned.1.call-done = bf16[2048,16384]{1,0:T(8,128)(2,1)} async-done(((bf16[256,16384]{1,0:T(8,128)(2,1)}), bf16[2048,16384]{1,0:T(8,128)(2,1)}) %all-gather.11.cloned.1.call-update) | async-done | bytes 67108880 | tf_op jit(solution)/shard_map/all_gather | solution.py:110
  736.6 17.1 fusion.6
  753.7 20.5 fusion.18
  774.2 17.2 fusion.4
  795.3 18.6 fusion.2
  830.3 6.3 copy.52
  866.5 47.1 %reduce-scatter.7.cloned.1.call-done = bf16[4,64,2048]{2,1,0:T(8,128)(2,1)} async-done(((bf16[4,256,2048]{2,1,0:T(8,128)(2,1)}), bf16[4,64,2048]{2,1,0:T(8,128)(2,1)}) %reduce-scatter.7.cloned.1.call-update) | async-done | bytes 1048592 | tf_op jit(solution)/shard_map/reduce_scatter | solution.py:166
  913.6 79.6 %reduce-scatter.5.cloned.1.call-done = bf16[4,64,2048]{2,1,0:T(8,128)(2,1)} async-done(((bf16[4,256,2048]{2,1,0:T(8,128)(2,1)}), bf16[4,64,2048]{2,1,0:T(8,128)(2,1)}) %reduce-scatter.5.cloned.1.call-update) | async-done | bytes 1048592 | tf_op jit(solution)/shard_map/reduce_scatter | solution.py:160
  993.2 13.3 convolution_convert_fusion.2
  1006.5 22.6 %pad_maximum_fusion.1 = bf16[2048,8192]{1,0:T(8,128)(2,1)} fusion(bf16[2048,2048]{1,0:T(8,128)(2,1)} %convolution_convert_fusion.3, bf16[2048,6144]{1,0:T(8,128)(2,1)} %convolution_convert_fusion.2), kind=kLoop, calls=%fused_computation.1 | loop fusion | flops 67108864 | bytes 67108864 | tf_op jit(solution)/shard_map/concatenate | solution.py:211
  1030.3 21.5 convolution_convert_fusion.1
  1051.9 23.0 %convolution_convert_fusion = bf16[2048,8192]{1,0:T(8,128)(2,1)} fusion(bf16[256,2048]{1,0:T(8,128)(2,1)S(1)} %bitcast.114, f32[256,8192]{1,0:T(8,128)} %fusion.6), kind=kOutput, calls=%fused_computation.2 | convolution fusion | flops 8625586176 | bytes 42991616 | tf_op jit(solution)/shard_map/dot_general | solution.py:19
  1074.9 46.9 %pad_maximum_fusion = bf16[2048,16384]{1,0:T(8,128)(2,1)} fusion(bf16[2048,8192]{1,0:T(8,128)(2,1)} %convolution_convert_fusion, bf16[2048,8192]{1,0:T(8,128)(2,1)} %convolution_convert_fusion.1), kind=kLoop, calls=%fused_computation | loop fusion | flops 134217728 | bytes 134217728 | tf_op jit(solution)/shard_map/concatenate | solution.py:220
  1121.9 13.6 fusion.8
  1140.5 94.6 %reduce-scatter.9.cloned.1.call-done = bf16[256,8192]{1,0:T(8,128)(2,1)} async-done(((bf16[2048,8192]{1,0:T(8,128)(2,1)}), bf16[256,8192]{1,0:T(8,128)(2,1)}) %reduce-scatter.9.cloned.1.call-update) | async-done | bytes 4194320 | tf_op jit(solution)/shard_map/reduce_scatter | solution.py:210
  1235.1 387.4 %reduce-scatter.11.cloned.1.call-done = bf16[256,16384]{1,0:T(8,128)(2,1)} async-done(((bf16[2048,16384]{1,0:T(8,128)(2,1)}), bf16[256,16384]{1,0:T(8,128)(2,1)}) %reduce-scatter.11.cloned.1.call-update) | async-done | bytes 8388624 | tf_op jit(solution)/shard_map/reduce_scatter | solution.py:219
  1626.7 140.2 %all-reduce.7.cloned.1.call-done = f32[64,12288]{1,0:T(8,128)} async-done(((f32[64,12288]{1,0:T(8,128)}), f32[64,12288]{1,0:T(8,128)}) %all-reduce.7.cloned.1.call-update) | async-done | bytes 3145744 | tf_op jit(solution)/shard_map/psum | solution.py:200
  1769.9 12.5 fusion.66
  1782.4 15.2 fusion.64
  1797.5 397.6 %all-reduce.9.cloned.1.call-done = (bf16[256,8192]{1,0:T(8,128)(2,1)}, bf16[256,16384]{1,0:T(8,128)(2,1)}) async-done(((bf16[256,8192]{1,0:T(8,128)(2,1)}, bf16[256,16384]{1,0:T(8,128)(2,1)}), (bf16[256,8192]{1,0:T(8,128)(2,1)}, bf16[256,16384]{1,0:T(8,128)(2,1)})) %all-reduce.9.cloned.1.call-update) | async-done | bytes 12582928 | tf_op jit(solution)/shard_map/psum | solution.py:228
  2195.1 6.6 convert_element_type.137
  2201.7 11.5 convert_element_type.138
  (133 shorter events, 94.8 us)
Async XLA Ops:
  7.2 85.0 %all-reduce.5.cloned.1.call-start = ((), (), s32[]{:S(2)}) async-start(), calls=%async_computation.4 | async-start | bytes 6291456 | tf_op jit(solution)/shard_map/psum | solution.py:48
  19.9 235.8 %all-gather.5.cloned.1.call-start = ((), (), s32[]{:S(2)}) async-start(), calls=%async_computation.5 | async-start | bytes 37748736 | tf_op jit(solution)/shard_map/all_gather | solution.py:63
  25.9 66.3 %copy-start.30 = (s32[4]{0:T(128)S(1)}, s32[4]{0:T(128)}, u32[]{:S(2)}) copy-start(s32[4]{0:T(128)} %param.11) | copy-start | bytes 52
  25.9 325.4 %all-gather.7.cloned.1.call-start = ((), (), s32[]{:S(2)}) async-start(), calls=%async_computation.6 | async-start | bytes 5242880 | tf_op jit(solution)/shard_map/all_gather | solution.py:74
  27.4 228.3 %copy-start.28 = (f32[4,64]{1,0:T(4,128)}, f32[4,64]{1,0:T(4,128)S(1)}, u32[]{:S(2)}) copy-start(f32[4,64]{1,0:T(4,128)S(1)} %fusion.42) | copy-start | bytes 3076
  27.4 228.3 %copy-start.26 = (f32[4,64]{1,0:T(4,128)}, f32[4,64]{1,0:T(4,128)S(1)}, u32[]{:S(2)}) copy-start(f32[4,64]{1,0:T(4,128)S(1)} %fusion.71) | copy-start | bytes 3076
  95.2 160.5 %copy-start.20 = (f32[4,2048]{1,0:T(4,128)}, f32[4,2048]{1,0:T(4,128)S(1)}, u32[]{:S(2)}) copy-start(f32[4,2048]{1,0:T(4,128)S(1)} %get-tuple-element.28) | copy-start | bytes 98308
  95.7 171.6 %copy-start.10 = (bf16[4,64,2048]{2,1,0:T(8,128)(2,1)}, bf16[4,64,2048]{2,1,0:T(8,128)(2,1)S(1)}, u32[]{:S(2)}) copy-start(bf16[4,64,2048]{2,1,0:T(8,128)(2,1)S(1)} %fusion.37) | copy-start | bytes 3145732
  270.4 162.3 %all-gather.9.cloned.1.call-start = ((), (), s32[]{:S(2)}) async-start(), calls=%async_computation.7 | async-start | bytes 5242880 | tf_op jit(solution)/shard_map/all_gather | solution.py:73
  273.5 463.1 %all-gather.11.cloned.1.call-start = ((), (), s32[]{:S(2)}) async-start(), calls=%async_computation.8 | async-start | bytes 75497472 | tf_op jit(solution)/shard_map/all_gather | solution.py:110
  283.0 630.6 %reduce-scatter.7.cloned.1.call-start = ((), (), s32[]{:S(2)}) async-start(), calls=%async_computation.10 | async-start | bytes 5242880 | tf_op jit(solution)/shard_map/reduce_scatter | solution.py:166
  284.2 156.0 %copy-start.8 = (bf16[32,8,16,128]{3,2,1,0:T(8,128)(2,1)}, bf16[32,8,16,128]{3,2,1,0:T(8,128)(2,1)S(1)}, u32[]{:S(2)}) copy-start(bf16[32,8,16,128]{3,2,1,0:T(8,128)(2,1)S(1)} %copy.61) | copy-start | bytes 3145732
  445.1 6.4 copy-start
  445.1 4.5 copy-start.5
  451.5 9.9 copy-start.18
  451.5 9.9 copy-start.14
  463.1 290.6 %copy-start.12 = (bf16[4,64,2048]{2,1,0:T(8,128)(2,1)}, bf16[4,64,2048]{2,1,0:T(8,128)(2,1)S(1)}, u32[]{:S(2)}) copy-start(bf16[4,64,2048]{2,1,0:T(8,128)(2,1)S(1)} %get-tuple-element.36) | copy-start | bytes 3145732
  795.3 18.6 copy-start.15
  821.0 6.1 copy-start.1
  836.7 156.5 %reduce-scatter.5.cloned.1.call-start = ((), (), s32[]{:S(2)}) async-start(), calls=%async_computation.9 | async-start | bytes 5242880 | tf_op jit(solution)/shard_map/reduce_scatter | solution.py:160
  836.8 5.9 copy-start.2
  853.8 381.3 %reduce-scatter.9.cloned.1.call-start = ((), (), s32[]{:S(2)}) async-start(), calls=%async_computation.11 | async-start | bytes 37748736 | tf_op jit(solution)/shard_map/reduce_scatter | solution.py:210
  860.7 132.5 %copy-start.16 = (bf16[32,8,16,128]{3,1,2,0:T(8,128)(2,1)}, bf16[32,8,16,128]{3,1,2,0:T(8,128)(2,1)S(1)}, u32[]{:S(2)}) copy-start(bf16[32,8,16,128]{3,1,2,0:T(8,128)(2,1)S(1)} %copy.88) | copy-start | bytes 3145732
  860.7 132.5 %copy-start.11 = (bf16[4,64,2048]{2,1,0:T(8,128)(2,1)S(1)}, bf16[4,64,2048]{2,1,0:T(8,128)(2,1)}, u32[]{:S(2)}) copy-start(bf16[4,64,2048]{2,1,0:T(8,128)(2,1)} %copy-done.10) | copy-start | bytes 3145732
  1029.2 22.7 %copy-start.17 = (bf16[4,64,2048]{2,1,0:T(8,128)(2,1)S(1)}, bf16[4,64,2048]{2,1,0:T(8,128)(2,1)}, u32[]{:S(2)}) copy-start(bf16[4,64,2048]{2,1,0:T(8,128)(2,1)} %get-tuple-element.35) | copy-start | bytes 3145732
  1029.2 593.3 %reduce-scatter.11.cloned.1.call-start = ((), (), s32[]{:S(2)}) async-start(), calls=%async_computation.12 | async-start | bytes 75497472 | tf_op jit(solution)/shard_map/reduce_scatter | solution.py:219
  1121.8 13.7 copy-start.7
  1121.8 13.7 copy-start.21
  1121.9 13.7 copy-start.27
  1121.9 645.0 %all-reduce.7.cloned.1.call-start = ((), (), s32[]{:S(2)}) async-start(), calls=%async_computation.13 | async-start | bytes 6291456 | tf_op jit(solution)/shard_map/psum | solution.py:200
  1140.2 1055.0 %all-reduce.9.cloned.1.call-start = ((), (), s32[]{:S(2)}) async-start(), calls=%async_computation.14 | async-start | bytes 25165824 | tf_op jit(solution)/shard_map/psum | solution.py:228
  1623.2 146.7 %copy-start.19 = (f32[64,256]{1,0:T(8,128)S(1)}, f32[64,256]{1,0:T(8,128)}, u32[]{:S(2)}) copy-start(f32[64,256]{1,0:T(8,128)} %param.15) | copy-start | bytes 196612
  (11 other events, 15.7 us)
Sparse Core Ops, SparseCore 0:
  20.0 72.1 all-reduce.4
  94.8 160.8 all-gather.4
  270.5 80.7 all-gather.6
  353.4 79.2 all-gather.8
  435.2 301.3 all-gather.10
  836.8 76.7 reduce-scatter.6
  915.9 77.2 reduce-scatter.4
  1029.3 205.7 reduce-scatter.8
  1238.7 383.7 reduce-scatter.10
  1629.3 137.5 all-reduce.6
  1769.5 425.5 all-reduce.8
where the time goes:
time: 2230 us; the launch traced here: 2220 us
  waiting for transfers between devices  1790 us (80%)
  matrix products  246 us (11%)
  other arithmetic  125 us (6%)
  local copies, waits for them, and re-layouts  45.8 us (2%)
    psum x1, waiting for transfers between devices, body(): lax.psum(attn_part, 'blk').astype(jnp.float32)  398 us
    reduce_scatter x1, waiting for transfers between devices, body(): lax.psum_scatter(jnp.concatenate([rows_product(h_part, grad_pre), rows_pr...  387 us
    all_gather x1, waiting for transfers between devices, body(): lax.all_gather(mlp_weight.astype(jnp.bfloat16), 'fsdp', axis=0, tiled=True)  274 us
    all_gather x1, waiting for transfers between devices, body(): lax.all_gather(attn_weight.astype(jnp.bfloat16), 'fsdp', axis=0, tiled=True)  160 us
    psum x1, waiting for transfers between devices, body(): grad_bins = lax.psum(bin_terms, ('fsdp', 'blk'))  140 us
    reduce_scatter x1, waiting for transfers between devices, body(): lax.psum_scatter(jnp.concatenate([rows_product(h_part, grad_qkv), rows_pr...  94.6 us
    reduce_scatter x1, waiting for transfers between devices, body(): lax.psum_scatter(grad_keys_all.reshape(slot_count, image_tok, model_width...  79.6 us
    all_gather x1, waiting for transfers between devices, body(): lax.all_gather(key_rows, 'blk', axis=1, tiled=True)  73.9 us
  transfers between devices with their start and end apart: 11, of which 11 were waited for; matrix products, arithmetic and copies ran while one was open for 10% of the time, Pallas kernels for 0%

commit v1 on v0

--- a/solution.py
+++ b/solution.py
@@ -1,6 +1,11 @@
+import functools
+import math
+
 import jax
 import jax.numpy as jnp
 from jax import lax
+from jax.experimental import pallas as pl
+from jax.experimental.pallas import tpu as pltpu
 from jax.sharding import PartitionSpec as P
 
 HD = 128
@@ -239,9 +244,629 @@
     )
 
 
+MESH_ID = pl.DeviceIdType.MESH
+VMEM_BYTES = 56 * 1024 * 1024
+
+
+def contract(left, right, left_dim, right_dim):
+    return lax.dot_general(
+        left, right, (((left_dim,), (right_dim,)), ((), ())), preferred_element_type=jnp.float32
+    )
+
+
+def plane_places():
+    mine = lax.axis_index("fsdp")
+    plane = lax.axis_index("blk")
+    core = lax.rem(mine, 2)
+    col = lax.rem(mine // 2, 2)
+    row = mine // 4
+
+    def at(flip):
+        flip_row, flip_col, flip_core = flip // 4, (flip // 2) % 2, flip % 2
+        new_row = 1 - row if flip_row else row
+        new_col = 1 - col if flip_col else col
+        new_core = 1 - core if flip_core else core
+        return new_row * 4 + new_col * 2 + new_core
+
+    return mine, plane, at
+
+
+def greet(places):
+    barrier = pltpu.get_barrier_semaphore()
+    for place in places:
+        pl.semaphore_signal(barrier, inc=1, device_id=place, device_id_type=MESH_ID)
+    pl.semaphore_wait(barrier, len(places))
+
+
+def remote(src, dst, send_sem, recv_sem, place):
+    return pltpu.make_async_remote_copy(
+        src_ref=src,
+        dst_ref=dst,
+        send_sem=send_sem,
+        recv_sem=recv_sem,
+        device_id=place,
+        device_id_type=MESH_ID,
+    )
+
+
+PIECES = 4
+
+
+def gather_kernel(block_ref, out_ref, own_sem, send_sems, recv_sems):
+    mine, plane, at = plane_places()
+    piece = block_ref.shape[0] // PIECES
+    greet([(at(flip), plane) for flip in (1, 2, 4)])
+    own = pltpu.make_async_copy(block_ref, out_ref.at[mine], own_sem)
+    own.start()
+    started = []
+
+    def send(src, owner, part, flip, slot):
+        copy = remote(
+            src,
+            out_ref.at[owner, pl.ds(part * piece, piece)],
+            send_sems.at[slot],
+            recv_sems.at[slot],
+            (at(flip), plane),
+        )
+        copy.start()
+        started.append(copy)
+
+    def arrived(owner, part, slot):
+        ref = out_ref.at[owner, pl.ds(part * piece, piece)]
+        remote(ref, ref, send_sems.at[slot], recv_sems.at[slot], (mine, plane)).wait_recv()
+        return ref
+
+    for part in range(PIECES):
+        src = block_ref.at[pl.ds(part * piece, piece)]
+        send(src, mine, part, 2, part)
+        send(src, mine, part, 4, PIECES + part)
+        send(src, mine, part, 1, 3 * PIECES + part)
+    for part in range(PIECES):
+        got = arrived(at(2), part, part)
+        if part < PIECES // 2:
+            send(got, at(2), part, 4, 2 * PIECES + part)
+        send(got, at(2), part, 1, 4 * PIECES + part)
+        got = arrived(at(4), part, PIECES + part)
+        if part >= PIECES // 2:
+            send(got, at(4), part, 2, 2 * PIECES + part)
+        send(got, at(4), part, 1, 5 * PIECES + part)
+    for part in range(PIECES):
+        got = arrived(at(6), part, 2 * PIECES + part)
+        send(got, at(6), part, 1, 6 * PIECES + part)
+    for number, flip in enumerate((1, 3, 5, 7)):
+        for part in range(PIECES):
+            arrived(at(flip), part, (3 + number) * PIECES + part)
+    own.wait()
+    for copy in started:
+        copy.wait_send()
+
+
+def plane_gather(block):
+    rows, width = block.shape
+    return pl.pallas_call(
+        gather_kernel,
+        out_shape=jax.ShapeDtypeStruct((8, rows, width), block.dtype),
+        in_specs=[pl.BlockSpec(memory_space=pl.ANY)],
+        out_specs=pl.BlockSpec(memory_space=pl.ANY),
+        scratch_shapes=[
+            pltpu.SemaphoreType.DMA,
+            pltpu.SemaphoreType.DMA((7 * PIECES,)),
+            pltpu.SemaphoreType.DMA((7 * PIECES,)),
+        ],
+        compiler_params=pltpu.CompilerParams(collective_id=0, has_side_effects=True),
+        name="plane_gather",
+    )(block)
+
+
+def scatter_kernel(
+    part_ref,
+    out_ref,
+    own,
+    peer,
+    far,
+    near,
+    load_sems,
+    core_send,
+    core_recv,
+    far_send,
+    far_recv,
+    near_send,
+    near_recv,
+):
+    mine, plane, at = plane_places()
+    rows = part_ref.shape[1]
+    half = rows // 2
+    greet([(at(flip), plane) for flip in (1, 2, 4)])
+    order = (6, 2, 4, 0)
+    loads, pairs = [], []
+    for slot, flip in enumerate(order):
+        copy = remote(
+            part_ref.at[at(flip ^ 1)],
+            peer.at[slot],
+            core_send.at[slot],
+            core_recv.at[slot],
+            (at(1), plane),
+        )
+        copy.start()
+        pairs.append(copy)
+        load = pltpu.make_async_copy(part_ref.at[at(flip)], own.at[slot], load_sems.at[slot])
+        load.start()
+        loads.append(load)
+
+    def pair_sum(slot, start, count):
+        rows_at = pl.ds(start, count)
+        total = own[slot, rows_at, :].astype(jnp.float32) + peer[slot, rows_at, :].astype(
+            jnp.float32
+        )
+        return total
+
+    low, high = pl.ds(0, half), pl.ds(half, half)
+    far_copies, near_copies = [], []
+    loads[0].wait()
+    pairs[0].wait_recv()
+    own[0] = pair_sum(0, 0, rows).astype(jnp.bfloat16)
+    for number, (flip, rows_at) in enumerate(((2, low), (4, high))):
+        copy = remote(
+            own.at[0, rows_at],
+            far.at[number],
+            far_send.at[number],
+            far_recv.at[number],
+            (at(flip), plane),
+        )
+        copy.start()
+        far_copies.append(copy)
+
+    def send_near(slot, flip, part, rows_at):
+        index = (slot - 1) * 2 + part
+        copy = remote(
+            own.at[slot, rows_at],
+            near.at[slot - 1, rows_at],
+            near_send.at[index],
+            near_recv.at[index],
+            (at(flip), plane),
+        )
+        copy.start()
+        near_copies.append(copy)
+
+    loads[1].wait()
+    pairs[1].wait_recv()
+    own[1, low, :] = pair_sum(1, 0, half).astype(jnp.bfloat16)
+    send_near(1, 2, 0, low)
+    loads[2].wait()
+    pairs[2].wait_recv()
+    own[2, high, :] = pair_sum(2, half, half).astype(jnp.bfloat16)
+    send_near(2, 4, 1, high)
+    far_copies[0].wait_recv()
+    own[2, low, :] = (pair_sum(2, 0, half) + far[0].astype(jnp.float32)).astype(jnp.bfloat16)
+    send_near(2, 4, 0, low)
+    far_copies[1].wait_recv()
+    own[1, high, :] = (pair_sum(1, half, half) + far[1].astype(jnp.float32)).astype(jnp.bfloat16)
+    send_near(1, 2, 1, high)
+    loads[3].wait()
+    pairs[3].wait_recv()
+    for copy in near_copies:
+        copy.wait_recv()
+    out_ref[...] = (
+        pair_sum(3, 0, rows) + near[0].astype(jnp.float32) + near[1].astype(jnp.float32)
+    )
+    for copy in pairs + far_copies + near_copies:
+        copy.wait_send()
+
+
+def plane_scatter(partial_sums):
+    _, rows, width = partial_sums.shape
+    kind = partial_sums.dtype
+    return pl.pallas_call(
+        scatter_kernel,
+        out_shape=jax.ShapeDtypeStruct((rows, width), jnp.float32),
+        in_specs=[pl.BlockSpec(memory_space=pl.ANY)],
+        out_specs=pl.BlockSpec(memory_space=pltpu.VMEM),
+        scratch_shapes=[
+            pltpu.VMEM((4, rows, width), kind),
+            pltpu.VMEM((4, rows, width), kind),
+            pltpu.VMEM((2, rows // 2, width), kind),
+            pltpu.VMEM((2, rows, width), kind),
+            pltpu.SemaphoreType.DMA((4,)),
+            pltpu.SemaphoreType.DMA((4,)),
+            pltpu.SemaphoreType.DMA((4,)),
+            pltpu.SemaphoreType.DMA((2,)),
+            pltpu.SemaphoreType.DMA((2,)),
+            pltpu.SemaphoreType.DMA((4,)),
+            pltpu.SemaphoreType.DMA((4,)),
+        ],
+        compiler_params=pltpu.CompilerParams(
+            collective_id=1, has_side_effects=True, vmem_limit_bytes=VMEM_BYTES
+        ),
+        name="plane_scatter",
+    )(partial_sums)
+
+
+def exchange_kernel(count, *refs):
+    sources, results = refs[:count], refs[count : 2 * count]
+    own_sems, send_sems, recv_sems = refs[2 * count :]
+    mine, plane, at = plane_places()
+    greet([(at(flip), plane) for flip in range(1, 8)])
+    waits = []
+    for number, (src, dst) in enumerate(zip(sources, results)):
+        own = pltpu.make_async_copy(src.at[mine], dst.at[mine], own_sems.at[number])
+        own.start()
+        waits.append(own)
+        for flip in (6, 7, 2, 4, 3, 5, 1):
+            copy = remote(
+                src.at[at(flip)],
+                dst.at[mine],
+                send_sems.at[number, flip],
+                recv_sems.at[number, flip],
+                (at(flip), plane),
+            )
+            copy.start()
+            waits.append(copy)
+    for copy in waits:
+        copy.wait()
+
+
+def plane_exchange(sources, number):
+    count = len(sources)
+    return pl.pallas_call(
+        functools.partial(exchange_kernel, count),
+        out_shape=[jax.ShapeDtypeStruct(source.shape, source.dtype) for source in sources],
+        in_specs=[pl.BlockSpec(memory_space=pl.ANY)] * count,
+        out_specs=[pl.BlockSpec(memory_space=pl.ANY)] * count,
+        scratch_shapes=[
+            pltpu.SemaphoreType.DMA((count,)),
+            pltpu.SemaphoreType.DMA((count, 8)),
+            pltpu.SemaphoreType.DMA((count, 8)),
+        ],
+        compiler_params=pltpu.CompilerParams(collective_id=number, has_side_effects=True),
+        name="plane_exchange",
+    )(*sources)
+
+
+def softmax_rows(queries, key_rows):
+    scores = contract(queries, key_rows, 1, 1) * HD ** (-0.5)
+    exponent = jnp.exp(scores - jnp.max(scores, axis=-1, keepdims=True))
+    return exponent / jnp.sum(exponent, axis=-1, keepdims=True)
+
+
+def attention_kernel(h_ref, qkv_weight_ref, out_weight_ref, qkv_ref, attended_ref, partial_ref):
+    width = qkv_ref.shape[-1] // 3
+    projected = contract(h_ref[0], qkv_weight_ref[...], 1, 0).astype(jnp.bfloat16)
+    qkv_ref[0] = projected
+    for head in range(width // HD):
+        at = head * HD
+        queries = projected[:, at : at + HD]
+        key_rows = projected[:, width + at : width + at + HD]
+        value_rows = projected[:, 2 * width + at : 2 * width + at + HD]
+        attention = softmax_rows(queries, key_rows).astype(jnp.bfloat16)
+        attended_ref[0, :, at : at + HD] = contract(attention, value_rows, 1, 0).astype(
+            jnp.bfloat16
+        )
+    partial_ref[0] = contract(attended_ref[0], out_weight_ref[...], 1, 0).astype(jnp.bfloat16)
+
+
+def whole(shape):
+    return pl.BlockSpec(shape, lambda image: (0,) * len(shape))
+
+
+def per_image(shape):
+    return pl.BlockSpec((1,) + shape, lambda image: (image,) + (0,) * len(shape))
+
+
+def attention_forward(h_all, qkv_weight, out_weight):
+    images, rows, width = h_all.shape
+    columns = qkv_weight.shape[1]
+    return pl.pallas_call(
+        attention_kernel,
+        grid=(images,),
+        out_shape=[
+            jax.ShapeDtypeStruct((images, rows, columns), jnp.bfloat16),
+            jax.ShapeDtypeStruct((images, rows, columns // 3), jnp.bfloat16),
+            jax.ShapeDtypeStruct((images, rows, width), jnp.bfloat16),
+        ],
+        in_specs=[
+            per_image((rows, width)),
+            whole(qkv_weight.shape),
+            whole(out_weight.shape),
+        ],
+        out_specs=[
+            per_image((rows, columns)),
+            per_image((rows, columns // 3)),
+            per_image((rows, width)),
+        ],
+        compiler_params=pltpu.CompilerParams(vmem_limit_bytes=VMEM_BYTES),
+        name="attention_forward",
+    )(h_all, qkv_weight, out_weight)
+
+
+def attention_back_kernel(
+    grad_ref, qkv_ref, qkv_weight_ref, out_weight_ref, grad_qkv_ref, partial_ref
+):
+    width = qkv_ref.shape[-1] // 3
+    scale = HD ** (-0.5)
+    grad_attended = contract(grad_ref[0], out_weight_ref[...], 1, 1).astype(jnp.bfloat16)
+    for head in range(width // HD):
+        at = head * HD
+        queries = qkv_ref[0, :, at : at + HD]
+        key_rows = qkv_ref[0, :, width + at : width + at + HD]
+        value_rows = qkv_ref[0, :, 2 * width + at : 2 * width + at + HD]
+        grad_head = grad_attended[:, at : at + HD]
+        attention = softmax_rows(queries, key_rows)
+        grad_weights = contract(grad_head, value_rows, 1, 1)
+        row_delta = jnp.sum(attention * grad_weights, axis=-1, keepdims=True)
+        grad_scores = (attention * (grad_weights - row_delta)).astype(jnp.bfloat16)
+        grad_qkv_ref[0, :, at : at + HD] = (contract(grad_scores, key_rows, 1, 0) * scale).astype(
+            jnp.bfloat16
+        )
+        grad_qkv_ref[0, :, width + at : width + at + HD] = (
+            contract(grad_scores, queries, 0, 0) * scale
+        ).astype(jnp.bfloat16)
+        grad_qkv_ref[0, :, 2 * width + at : 2 * width + at + HD] = contract(
+            attention.astype(jnp.bfloat16), grad_head, 0, 0
+        ).astype(jnp.bfloat16)
+    partial_ref[0] = contract(grad_qkv_ref[0], qkv_weight_ref[...], 1, 1).astype(jnp.bfloat16)
+
+
+def attention_backward(grad_all, qkv_all, qkv_weight, out_weight):
+    images, rows, width = grad_all.shape
+    columns = qkv_weight.shape[1]
+    return pl.pallas_call(
+        attention_back_kernel,
+        grid=(images,),
+        out_shape=[
+            jax.ShapeDtypeStruct((images, rows, columns), jnp.bfloat16),
+            jax.ShapeDtypeStruct((images, rows, width), jnp.bfloat16),
+        ],
+        in_specs=[
+            per_image((rows, width)),
+            per_image((rows, columns)),
+            whole(qkv_weight.shape),
+            whole(out_weight.shape),
+        ],
+        out_specs=[per_image((rows, columns)), per_image((rows, width))],
+        compiler_params=pltpu.CompilerParams(vmem_limit_bytes=VMEM_BYTES),
+        name="attention_backward",
+    )(grad_all, qkv_all, qkv_weight, out_weight)
+
+
+GELU_SCALE = (2.0 / math.pi) ** 0.5
+
+
+def feed_kernel(
+    h_ref, grad_ref, up_ref, down_ref, hidden_ref, grad_pre_ref, partial_out_ref, partial_grad_ref
+):
+    pre = contract(h_ref[0], up_ref[...], 1, 0)
+    grad_hidden = contract(grad_ref[0], down_ref[...], 1, 0)
+    squared = pre * pre
+    bend = jnp.tanh(GELU_SCALE * (pre + 0.044715 * (squared * pre)))
+    rise = 0.5 * (1.0 + bend)
+    hidden_ref[0] = (pre * rise).astype(jnp.bfloat16)
+    slope = rise + 0.5 * pre * (1.0 - bend * bend) * (
+        GELU_SCALE * (1.0 + 3.0 * 0.044715 * squared)
+    )
+    grad_pre_ref[0] = (grad_hidden * slope).astype(jnp.bfloat16)
+    partial_out_ref[0] = contract(hidden_ref[0], down_ref[...], 1, 1).astype(jnp.bfloat16)
+    partial_grad_ref[0] = contract(grad_pre_ref[0], up_ref[...], 1, 1).astype(jnp.bfloat16)
+
+
+def feed_both(h_all, grad_all, up_weight, down_weight):
+    images, rows, width = h_all.shape
+    columns = up_weight.shape[1]
+    return pl.pallas_call(
+        feed_kernel,
+        grid=(images,),
+        out_shape=[
+            jax.ShapeDtypeStruct((images, rows, columns), jnp.bfloat16),
+            jax.ShapeDtypeStruct((images, rows, columns), jnp.bfloat16),
+            jax.ShapeDtypeStruct((images, rows, width), jnp.bfloat16),
+            jax.ShapeDtypeStruct((images, rows, width), jnp.bfloat16),
+        ],
+        in_specs=[
+            per_image((rows, width)),
+            per_image((rows, width)),
+            whole(up_weight.shape),
+            whole(down_weight.shape),
+        ],
+        out_specs=[
+            per_image((rows, columns)),
+            per_image((rows, columns)),
+            per_image((rows, width)),
+            per_image((rows, width)),
+        ],
+        compiler_params=pltpu.CompilerParams(vmem_limit_bytes=VMEM_BYTES),
+        name="feed_both",
+    )(h_all, grad_all, up_weight, down_weight)
+
+
+def rms_scale(features):
+    return lax.rsqrt(jnp.mean(features * features, axis=-1, keepdims=True) + EPSILON)
+
+
+def norm_back(features, grad_h, scaling):
+    inverse = rms_scale(features)
+    unit = features * inverse
+    inner = grad_h * (1.0 + scaling)
+    grad = (inner - unit * jnp.mean(inner * unit, axis=-1, keepdims=True)) * inverse
+    grad_scaling = jnp.sum(grad_h * unit, axis=0)
+    grad_shifting = jnp.sum(grad_h, axis=0)
+    return grad, grad_scaling, grad_shifting
+
+
+def plane_sum(weight_part, number):
+    depth, columns = weight_part.shape
+    rows = depth // 8
+    place = lax.axis_index("blk")
+    received = lax.ppermute(weight_part, "blk", [(0, 1), (3, 2)])
+    total = (weight_part.astype(jnp.float32) + received.astype(jnp.float32)).astype(jnp.bfloat16)
+    halves = total.reshape(8, 2, rows // 2, columns)
+    kept = lax.dynamic_index_in_dim(halves, jnp.where(place == 1, 0, 1), 1, keepdims=False)
+    sent = lax.dynamic_index_in_dim(halves, jnp.where(place == 1, 1, 0), 1, keepdims=False)
+    received = lax.ppermute(sent, "blk", [(1, 2), (2, 1)])
+    total = (kept.astype(jnp.float32) + received.astype(jnp.float32)).astype(jnp.bfloat16)
+    (mine,) = plane_exchange([total], number)
+    other = lax.ppermute(mine, "blk", [(1, 2), (2, 1)])
+    both = jnp.where(place == 1, jnp.stack([mine, other]), jnp.stack([other, mine]))
+    given = lax.ppermute(both, "blk", [(1, 0), (2, 3)])
+    result = jnp.where((place == 1) | (place == 2), both, given)
+    return result.transpose(0, 2, 1, 3).reshape(rows, 8 * columns).astype(jnp.float32)
+
+
+def plane_body(
+    block_input,
+    cotangent,
+    bin_ids,
+    image_counts,
+    attn_weight,
+    mlp_weight,
+    noise_table,
+    mod_weight,
+    mod_bias,
+):
+    _, local_tok, model_width = block_input.shape
+    feed_width = mlp_weight.shape[1] // 2
+    rows = attn_weight.shape[0]
+    bins = noise_table.shape[0]
+    bias_piece = mod_bias.shape[0]
+    mine, place = lax.axis_index("fsdp"), lax.axis_index("blk")
+
+    def to_images(tokens):
+        return lax.all_to_all(tokens, "blk", split_axis=0, concat_axis=1, tiled=True)[0]
+
+    def to_tokens(image):
+        return lax.all_to_all(
+            image.reshape(1, -1, model_width), "blk", split_axis=1, concat_axis=0, tiled=True
+        )
+
+    features = to_images(block_input).astype(jnp.float32)
+    incoming = to_images(cotangent).astype(jnp.float32)
+    live = (place < image_counts[0]).astype(jnp.float32)
+
+    all_bins = lax.all_gather(bin_ids, "fsdp", axis=0)
+    plane_bins = lax.dynamic_index_in_dim(all_bins, place, 1, keepdims=False)
+    activated = jax.nn.silu(noise_table)
+    onehot = (plane_bins[:, None] == jnp.arange(bins, dtype=jnp.int32)[None, :]).astype(jnp.float32)
+    chosen = jnp.dot(onehot, activated, precision=PRECISE)
+    partial_mod = jnp.dot(chosen, mod_weight, precision=PRECISE)
+    bias_full = lax.dynamic_update_slice_in_dim(
+        jnp.zeros((6 * model_width,), jnp.float32), mod_bias, mine * bias_piece, 0
+    )
+    partial_mod = partial_mod + bias_full[None, :]
+    mod_parts, qkv_weight = plane_exchange(
+        [
+            partial_mod.reshape(8, 6, model_width),
+            attn_weight[:, : 3 * model_width]
+            .astype(jnp.bfloat16)
+            .reshape(rows, 3, 8, model_width // 8)
+            .transpose(2, 0, 1, 3)
+            .reshape(8, rows, 3 * model_width // 8),
+        ],
+        2,
+    )
+    mod_image = jnp.sum(mod_parts, axis=0)
+    shift_one, scale_one, gate_one, shift_two, scale_two, gate_two = [
+        mod_image[number][None, :] for number in range(6)
+    ]
+    qkv_weight = qkv_weight.reshape(model_width, 3 * model_width // 8)
+    out_weight = attn_weight[:, 3 * model_width :].astype(jnp.bfloat16)
+    feed_piece = feed_width // 8
+
+    def columns_apart(weight):
+        return weight.astype(jnp.bfloat16).reshape(rows, 8, feed_piece).transpose(1, 0, 2)
+
+    h_one = (features * rms_scale(features) * (1.0 + scale_one) + shift_one).astype(jnp.bfloat16)
+    h_one_all = plane_gather(h_one)
+    qkv_all, attended_all, partial = attention_forward(h_one_all, qkv_weight, out_weight)
+    attn_out = plane_scatter(partial)
+    up_weight, down_weight = plane_exchange(
+        [columns_apart(mlp_weight[:, :feed_width]), columns_apart(mlp_weight[:, feed_width:])], 3
+    )
+    up_weight = up_weight.reshape(model_width, feed_piece)
+    down_weight = down_weight.reshape(model_width, feed_piece)
+    first_sum = features + gate_one * attn_out
+    h_two = (first_sum * rms_scale(first_sum) * (1.0 + scale_two) + shift_two).astype(jnp.bfloat16)
+    grad_out = incoming * live
+    grad_mlp = (gate_two * grad_out).astype(jnp.bfloat16)
+    grad_mlp_all = plane_gather(grad_mlp)
+    h_two_all = plane_gather(h_two)
+    hidden_all, grad_pre_all, partial_out, partial_grad = feed_both(
+        h_two_all, grad_mlp_all, up_weight, down_weight
+    )
+
+    def flat(array):
+        return array.reshape(-1, array.shape[-1])
+
+    def rows_low(left, right):
+        return rows_product(flat(left), flat(right)).astype(jnp.bfloat16)
+
+    down_grad = plane_sum(rows_low(grad_mlp_all, hidden_all), 4)
+    up_grad = plane_sum(rows_low(h_two_all, grad_pre_all), 5)
+    grad_h_two = plane_scatter(partial_grad)
+    grad_first, grad_scale_two, grad_shift_two = norm_back(first_sum, grad_h_two, scale_two)
+    grad_first = grad_first + grad_out
+    grad_attn_out = (gate_one * grad_first).astype(jnp.bfloat16)
+    grad_gate_one = jnp.sum(grad_first * attn_out, axis=0)
+    grad_attn_all = plane_gather(grad_attn_out)
+    grad_qkv_all, partial_h_one = attention_backward(
+        grad_attn_all, qkv_all, qkv_weight, out_weight
+    )
+    qkv_grad = plane_sum(rows_low(h_one_all, grad_qkv_all), 6)
+    qkv_grad = (
+        qkv_grad.reshape(rows, 8, 3, model_width // 8)
+        .transpose(0, 2, 1, 3)
+        .reshape(rows, 3 * model_width)
+    )
+    out_grad = lax.psum(rows_low(attended_all, grad_attn_all), "blk").astype(jnp.float32)
+    attn_weight_grad = jnp.concatenate([qkv_grad, out_grad], axis=1)
+    mlp_weight_grad = jnp.concatenate([up_grad, down_grad], axis=1)
+    grad_h_one = plane_scatter(partial_h_one)
+    grad_input, grad_scale_one, grad_shift_one = norm_back(features, grad_h_one, scale_one)
+    input_grad = to_tokens((grad_input + grad_first).astype(jnp.bfloat16)).astype(jnp.float32)
+    mlp_out = plane_scatter(partial_out)
+    block_out = to_tokens((live * (first_sum + gate_two * mlp_out)).astype(jnp.bfloat16))
+    grad_gate_two = jnp.sum(grad_out * mlp_out, axis=0)
+
+    grad_mod = jnp.concatenate(
+        [
+            grad_shift_one,
+            grad_scale_one,
+            grad_gate_one,
+            grad_shift_two,
+            grad_scale_two,
+            grad_gate_two,
+        ]
+    )
+    grad_images = lax.all_gather(
+        lax.all_gather(grad_mod, "blk", axis=0), "fsdp", axis=0, tiled=True
+    )
+    onehot_all = (
+        all_bins.reshape(-1)[:, None] == jnp.arange(bins, dtype=jnp.int32)[None, :]
+    ).astype(jnp.float32)
+    chosen_all = jnp.dot(onehot_all, activated, precision=PRECISE)
+    mod_weight_grad = lax.dot_general(
+        chosen_all, grad_images, (((0,), (0,)), ((), ())), precision=PRECISE
+    )
+    image_term = lax.dot_general(
+        grad_images, mod_weight, (((1,), (1,)), ((), ())), precision=PRECISE
+    )
+    table_term = lax.dot_general(onehot_all, image_term, (((0,), (0,)), ((), ())), precision=PRECISE)
+    noise_grad = jax.vjp(jax.nn.silu, noise_table)[1](table_term)[0]
+    mod_bias_grad = lax.dynamic_slice_in_dim(
+        jnp.sum(grad_images, axis=0), mine * bias_piece, bias_piece
+    )
+    return (
+        block_out,
+        input_grad,
+        attn_weight_grad,
+        mlp_weight_grad,
+        noise_grad,
+        mod_weight_grad,
+        mod_bias_grad,
+    )
+
+
 def solution(mesh):
+    fits = mesh.shape["fsdp"] == 8 and mesh.shape["blk"] == 4
     return jax.shard_map(
-        body,
+        plane_body if fits else body,
         mesh=mesh,
         in_specs=(
             P("fsdp", "blk", None),

time: 2230 us -> 1420 us (0.64)
  waiting for transfers between devices: 1790 us -> 299 us
  Pallas kernels: 0 us -> 629 us
  matrix products: 246 us -> 80.2 us
  blocking collectives: 0 us -> 91 us
  local copies, waits for them, and re-layouts: 45.8 us -> 131 us
  starting transfers between devices: 1.27 us -> 50.5 us
    pallas_call x0 -> x16, Pallas kernels: none -> 629 us  [the longest x5 214 us: plane_exchange(): pl.pallas_call(functools.partial(exchange_kernel, count), out_shape=[jax....]
    reduce_scatter x4 -> x0, waiting for transfers between devices: 609 us -> none  [the longest x1 387 us: body(): lax.psum_scatter(jnp.concatenate([rows_product(h_part, grad_pre), rows_pr...]
    psum x3 -> x1, waiting for transfers between devices: 603 us -> 0.02 us  [plane_body(): lax.psum(rows_low(attended_all, grad_attn_all), 'blk').astype(jnp.float32)]
    all_gather x4 -> x1, waiting for transfers between devices: 575 us -> 0.01 us  [plane_body(): lax.all_gather(lax.all_gather(grad_mod, 'blk', axis=0), 'fsdp', axis=0, t...]
    ppermute x0 -> x12, waiting for transfers between devices: none -> 252 us  [the longest x3 160 us: plane_sum(): received = lax.ppermute(weight_part, 'blk', [(0, 1), (3, 2)])]
    dot_general x19 -> x6, matrix products: 183 us -> 37.1 us  [the longest x1 14.3 us: plane_body(): lax.dot_general(grad_images, mod_weight, (((1,), (1,)), ((), ())), precis...]
    all_gather x0 -> x1, blocking collectives: none -> 83 us  [plane_body(): lax.all_gather(grad_mod, 'blk', axis=0)]
    unnamed x73 -> x76, local copies, waits for them, and re-layouts: 9.18 us -> 66.6 us
  transfers between devices with their start and end apart: 11 -> 18, of which waited for: 11 -> 5; matrix products, arithmetic and copies ran while one was open for 10% -> 19% of each run, Pallas kernels for 0% -> 30%
where the time goes in v1:
time: 1420 us; the launch traced here: 1410 us
  Pallas kernels  629 us (44%)
  waiting for transfers between devices  299 us (21%)
  local copies, waits for them, and re-layouts  131 us (9%)
  other arithmetic  110 us (8%)
  blocking collectives  91 us (6%)
  matrix products  80.2 us (6%)
  starting transfers between devices  50.5 us (4%)
  between operations  17.9 us (1%)
    pallas_call x5, Pallas kernels, plane_exchange(): pl.pallas_call(functools.partial(exchange_kernel, count), out_shape=[jax....  214 us
    pallas_call x4, Pallas kernels, plane_scatter(): pl.pallas_call(scatter_kernel, out_shape=jax.ShapeDtypeStruct((rows, widt...  167 us
    ppermute x3, waiting for transfers between devices, plane_sum(): received = lax.ppermute(weight_part, 'blk', [(0, 1), (3, 2)])  160 us
    pallas_call x4, Pallas kernels, plane_gather(): pl.pallas_call(gather_kernel, out_shape=jax.ShapeDtypeStruct((8, rows, wi...  158 us
    ppermute x3, waiting for transfers between devices, plane_sum(): given = lax.ppermute(both, 'blk', [(1, 0), (2, 3)])  91.8 us
    all_gather x1, blocking collectives, plane_body(): lax.all_gather(grad_mod, 'blk', axis=0)  83 us
    unnamed x76, local copies, waits for them, and re-layouts  66.6 us
    all_to_all x2, waiting for transfers between devices, to_tokens(): lax.all_to_all(image.reshape(1, -1, model_width), 'blk', split_axis=1, co...  47.1 us
  transfers between devices with their start and end apart: 18, of which 5 were waited for; matrix products, arithmetic and copies ran while one was open for 19% of the time, Pallas kernels for 30%

profile of v1, /device:TPU:0, one launch (start us, length us, event | category | flops | bytes accessed | tf_op | source)
XLA Modules:
  0.0 1407.0 jit_solution(15285635893597770810)
XLA Ops:
  31.7 9.1 convolution_add_fusion
  54.0 42.8 %plane_exchange.5 = (f32[8,6,2048]{2,1,0:T(8,128)}, bf16[8,256,768]{2,1,0:T(8,128)(2,1)}) custom-call(f32[8,6,2048]{2,1,0:T(8,128)} %copy.78.refs_0_, bf16[8,256,768]{2,1,0:T(8,128)(2,1)} %copy.79.refs_1_), custom_call_target="tpu_custom_call" | custom-call | tf_op jit(solution)/shard_map/plane_exchange/pallas_call | solution.py:510
  98.5 13.8 copy.80
  131.0 94.0 %plane_exchange.6 = (bf16[8,256,1024]{2,1,0:T(8,128)(2,1)}, bf16[8,256,1024]{2,1,0:T(8,128)(2,1)}) custom-call(bf16[8,256,1024]{2,1,0:T(8,128)(2,1)} %bitcast.155, bf16[8,256,1024]{2,1,0:T(8,128)(2,1)} %bitcast.156), custom_call_target="tpu_custom_call" | custom-call | tf_op jit(solution)/shard_map/plane_exchange/pallas_call | solution.py:510
  232.1 39.3 %plane_gather.4.h_ref = bf16[8,256,2048]{2,1,0:T(8,128)(2,1)} custom-call(bf16[256,2048]{1,0:T(8,128)(2,1)} %fusion.11.block_ref), custom_call_target="tpu_custom_call" | custom-call | tf_op jit(solution)/shard_map/plane_gather/pallas_call | solution.py:346
  271.4 22.2 %attention_forward.1 = (bf16[8,256,768]{2,1,0:T(8,128)(2,1)}, bf16[8,256,256]{2,1,0:T(8,128)(2,1)}, bf16[8,256,2048]{2,1,0:T(8,128)(2,1)}) custom-call(bf16[8,256,2048]{2,1,0:T(8,128)(2,1)} %plane_gather.4.h_ref, bf16[2048,768]{1,0:T(8,128)(2,1)} %bitcast.171, bf16[256,2048]{1,0:T(8,128)(2,1)} %slice.48.out_weight_ref), custom_call_target="tpu_custom_call" | custom-call | tf_op jit(solution)/shard_map/attention_forward/pallas_call | solution.py:558
  293.6 41.7 %plane_scatter.4 = f32[256,2048]{1,0:T(8,128)} custom-call(bf16[8,256,2048]{2,1,0:T(8,128)(2,1)} %get-tuple-element.22.part_ref), custom_call_target="tpu_custom_call" | custom-call | tf_op jit(solution)/shard_map/plane_scatter/pallas_call | solution.py:459
  338.7 39.2 %plane_gather.5.h_ref = bf16[8,256,2048]{2,1,0:T(8,128)(2,1)} custom-call(bf16[256,2048]{1,0:T(8,128)(2,1)} %add_convert_fusion.3.block_ref), custom_call_target="tpu_custom_call" | custom-call | tf_op jit(solution)/shard_map/plane_gather/pallas_call | solution.py:346
  381.9 39.8 %plane_gather.6.grad_ref = bf16[8,256,2048]{2,1,0:T(8,128)(2,1)} custom-call(bf16[256,2048]{1,0:T(8,128)(2,1)} %fusion.4.block_ref), custom_call_target="tpu_custom_call" | custom-call | tf_op jit(solution)/shard_map/plane_gather/pallas_call | solution.py:346
  421.7 42.1 %feed_both.1 = (bf16[8,256,1024]{2,1,0:T(8,128)(2,1)}, bf16[8,256,1024]{2,1,0:T(8,128)(2,1)}, bf16[8,256,2048]{2,1,0:T(8,128)(2,1)}, bf16[8,256,2048]{2,1,0:T(8,128)(2,1)}) custom-call(bf16[8,256,2048]{2,1,0:T(8,128)(2,1)} %plane_gather.5.h_ref, bf16[8,256,2048]{2,1,0:T(8,128)(2,1)} %plane_gather.6.grad_ref, bf16[2048,1024]{1,0:T(8,128)(2,1)} %bitcast.178, ...), custom_call_target="tpu_custom_call" | custom-call | tf_op jit(solution)/shard_map/feed_both/pallas_call | solution.py:654
  463.8 41.8 %plane_scatter.6 = f32[256,2048]{1,0:T(8,128)} custom-call(bf16[8,256,2048]{2,1,0:T(8,128)(2,1)} %get-tuple-element.26.part_ref), custom_call_target="tpu_custom_call" | custom-call | tf_op jit(solution)/shard_map/plane_scatter/pallas_call | solution.py:459
  507.9 41.2 %plane_scatter.5 = f32[256,2048]{1,0:T(8,128)} custom-call(bf16[8,256,2048]{2,1,0:T(8,128)(2,1)} %get-tuple-element.25.part_ref), custom_call_target="tpu_custom_call" | custom-call | tf_op jit(solution)/shard_map/plane_scatter/pallas_call | solution.py:459
  556.1 39.6 %plane_gather.7.grad_ref = bf16[8,256,2048]{2,1,0:T(8,128)(2,1)} custom-call(bf16[256,2048]{1,0:T(8,128)(2,1)} %multiply_convert_fusion.block_ref), custom_call_target="tpu_custom_call" | custom-call | tf_op jit(solution)/shard_map/plane_gather/pallas_call | solution.py:346
  595.7 14.1 bitcast_convert_fusion.1
  615.6 25.7 %attention_backward.1 = (bf16[8,256,768]{2,1,0:T(8,128)(2,1)}, bf16[8,256,2048]{2,1,0:T(8,128)(2,1)}) custom-call(bf16[8,256,2048]{2,1,0:T(8,128)(2,1)} %plane_gather.7.grad_ref, bf16[8,256,768]{2,1,0:T(8,128)(2,1)} %get-tuple-element.27.qkv_ref, bf16[2048,768]{1,0:T(8,128)(2,1)} %bitcast.172, bf16[256,2048]{1,0:T(8,128)(2,1)} %slice.48.out_weight_ref), custom_call_target="tpu_custom_call" | custom-call | tf_op jit(solution)/shard_map/attention_backward/pallas_call | solution.py:612
  641.3 11.5 bitcast_convert_fusion.2
  655.7 10.7 bitcast_convert_fusion
  669.8 41.8 %plane_scatter.7 = f32[256,2048]{1,0:T(8,128)} custom-call(bf16[8,256,2048]{2,1,0:T(8,128)(2,1)} %get-tuple-element.28.part_ref), custom_call_target="tpu_custom_call" | custom-call | tf_op jit(solution)/shard_map/plane_scatter/pallas_call | solution.py:459
  719.3 86.6 %collective-permute-done = bf16[2048,768]{1,0:T(8,128)(2,1)} collective-permute-done((bf16[2048,768]{1,0:T(8,128)(2,1)}, bf16[2048,768]{1,0:T(8,128)(2,1)}, u32[]{:S(2)}, u32[]{:S(2)}) %collective-permute-start) | collective-permute-done | bytes 3145760 | tf_op jit(solution)/shard_map/ppermute | solution.py:698
  822.2 73.1 %collective-permute-done.8 = bf16[2048,1024]{1,0:T(8,128)(2,1)} collective-permute-done((bf16[2048,1024]{1,0:T(8,128)(2,1)}, bf16[2048,1024]{1,0:T(8,128)(2,1)}, u32[]{:S(2)}, u32[]{:S(2)}) %collective-permute-start.8) | collective-permute-done | bytes 4194336 | tf_op jit(solution)/shard_map/ppermute | solution.py:698
  925.0 20.4 %plane_exchange.7 = bf16[8,128,768]{2,1,0:T(8,128)(2,1)} custom-call(bf16[8,128,768]{2,1,0:T(8,128)(2,1)} %fusion.2.refs_0_), custom_call_target="tpu_custom_call" | custom-call | tf_op jit(solution)/shard_map/plane_exchange/pallas_call | solution.py:510
  951.8 26.0 %plane_exchange.8 = bf16[8,128,1024]{2,1,0:T(8,128)(2,1)} custom-call(bf16[8,128,1024]{2,1,0:T(8,128)(2,1)} %fusion.1.refs_0_), custom_call_target="tpu_custom_call" | custom-call | tf_op jit(solution)/shard_map/plane_exchange/pallas_call | solution.py:510
  979.9 83.0 %all-gather.1 = f32[49152]{0:T(1024)S(1)} all-gather(f32[12288]{0:T(1024)S(1)} %constant_dynamic-update-slice_fusion), channel_id=3, replica_groups=mesh['fsdp'=8,'blk'=4] {'blk'}, dimensions={0}, use_global_device_ids=true | all-gather | bytes 245760 | tf_op jit(solution)/shard_map/all_gather | solution.py:838
  1068.2 31.0 %plane_exchange.9 = bf16[8,128,1024]{2,1,0:T(8,128)(2,1)} custom-call(bf16[8,128,1024]{2,1,0:T(8,128)(2,1)} %fusion.refs_0_), custom_call_target="tpu_custom_call" | custom-call | tf_op jit(solution)/shard_map/plane_exchange/pallas_call | solution.py:510
  1147.8 47.1 %all-to-all-done.2 = bf16[4,2,65536]{2,1,0:T(2,128)(2,1)} async-done(((bf16[4,2,65536]{2,1,0:T(2,128)(2,1)}), bf16[4,2,65536]{2,1,0:T(2,128)(2,1)}, u32[]{:S(2)}, u32[]{:S(2)}) %all-to-all-start.2) | async-done | bytes 1048608 | tf_op jit(solution)/shard_map/all_to_all | solution.py:735
  1207.2 14.3 %fusion.34 = f32[32,256]{1,0:T(8,128)S(1)} fusion(f32[32,12288]{1,0:T(8,128)} %reshape.173, f32[256,12288]{1,0:T(8,128)} %param.16), kind=kOutput, calls=%fused_computation.87 | convolution fusion | flops 1207959552 | bytes 14188544 | tf_op jit(solution)/shard_map/dot_general | solution.py:847
  1222.4 12.4 fusion.35
  1239.6 8.7 copy.87
  1260.6 8.9 copy.97
  1269.5 15.2 %collective-permute-done.7 = bf16[2,8,128,1024]{3,2,1,0:T(8,128)(2,1)} collective-permute-done((bf16[2,8,128,1024]{3,2,1,0:T(8,128)(2,1)}, bf16[2,8,128,1024]{3,2,1,0:T(8,128)(2,1)}, u32[]{:S(2)}, u32[]{:S(2)}) %collective-permute-start.7) | collective-permute-done | bytes 4194336 | tf_op jit(solution)/shard_map/ppermute | solution.py:708
  1297.6 76.6 %collective-permute-done.11 = bf16[2,8,128,1024]{3,2,1,0:T(8,128)(2,1)} collective-permute-done((bf16[2,8,128,1024]{3,2,1,0:T(8,128)(2,1)}, bf16[2,8,128,1024]{3,2,1,0:T(8,128)(2,1)}, u32[]{:S(2)}, u32[]{:S(2)}) %collective-permute-start.11) | collective-permute-done | bytes 4194336 | tf_op jit(solution)/shard_map/ppermute | solution.py:708
  1387.5 11.6 maximum_convert_fusion
  (173 shorter events, 264.0 us)
Async XLA Ops:
  8.0 217.1 %all-to-all-start = ((bf16[4,64,2048]{2,1,0:T(8,128)(2,1)}), bf16[4,64,2048]{2,1,0:T(8,128)(2,1)S(1)}, u32[]{:S(2)}, u32[]{:S(2)}) async-start(bf16[4,64,2048]{2,1,0:T(8,128)(2,1)} %param.9), calls=%async_computation | async-start | bytes 2097152 | tf_op jit(solution)/shard_map/all_to_all | solution.py:732
  18.3 12.8 copy-start.21
  18.3 13.1 copy-start.17
  31.7 10.1 slice-start.2
  225.1 152.8 %all-to-all-start.1 = ((bf16[4,64,2048]{2,1,0:T(8,128)(2,1)}), bf16[4,64,2048]{2,1,0:T(8,128)(2,1)}, u32[]{:S(2)}, u32[]{:S(2)}) async-start(bf16[4,64,2048]{2,1,0:T(8,128)(2,1)} %param.10), calls=%async_computation.1 | async-start | bytes 2097152 | tf_op jit(solution)/shard_map/all_to_all | solution.py:732
  230.2 908.3 %all-reduce.3.cloned.1.call-start = ((), (), s32[]{:S(2)}) async-start(), calls=%async_computation.4 | async-start | bytes 2097152 | tf_op jit(solution)/shard_map/psum | solution.py:817
  507.9 41.2 %copy-start.5 = (f32[256,2048]{1,0:T(8,128)S(1)}, f32[256,2048]{1,0:T(8,128)}, u32[]{:S(2)}) copy-start(f32[256,2048]{1,0:T(8,128)} %plane_scatter.4) | copy-start | bytes 6291460
  507.9 41.2 %copy-start.7 = (f32[4,64,2048]{2,1,0:T(8,128)S(1)}, f32[4,64,2048]{2,1,0:T(8,128)}, u32[]{:S(2)}) copy-start(f32[4,64,2048]{2,1,0:T(8,128)} %copy-done.6) | copy-start | bytes 6291460
  609.8 203.0 %collective-permute-start.4 = (bf16[2048,1024]{1,0:T(8,128)(2,1)}, bf16[2048,1024]{1,0:T(8,128)(2,1)}, u32[]{:S(2)}, u32[]{:S(2)}) collective-permute-start(bf16[2048,1024]{1,0:T(8,128)(2,1)} %bitcast_convert_fusion.1), channel_id=1, source_target_pairs={{0,1},{3,2},{4,5},{7,6},{8,9},{11,10},{12,13},{15,14},{16,17},{19,... | collective-permute-start | bytes 12582920 | tf_op jit(solution)/shard_map/ppermute | solution.py:698
  615.6 40.2 %slice-start = ((s8[8388608]{0:T(1024)(128)(4,1)}), s8[4194304]{0:T(1024)(128)(4,1)S(1)}, s32[]{:S(2)}) async-start(s8[8388608]{0:T(1024)(128)(4,1)} %bitcast.144), calls=%async_computation.6 | async-start | bytes 8388608
  641.3 14.5 %slice-start.1 = ((s8[8388608]{0:T(1024)(128)(4,1)}), s8[4194304]{0:T(1024)(128)(4,1)S(1)}, s32[]{:S(2)}) async-start(s8[8388608]{0:T(1024)(128)(4,1)} %bitcast.144), calls=%async_computation.7 | async-start | bytes 8388608
  641.3 14.5 %copy-start.20 = (bf16[8,256,1024]{2,1,0:T(8,128)(2,1)S(1)}, bf16[8,256,1024]{2,1,0:T(8,128)(2,1)}, u32[]{:S(2)}) copy-start(bf16[8,256,1024]{2,1,0:T(8,128)(2,1)} %get-tuple-element.32) | copy-start | bytes 12582916
  652.8 153.1 %collective-permute-start = (bf16[2048,768]{1,0:T(8,128)(2,1)}, bf16[2048,768]{1,0:T(8,128)(2,1)}, u32[]{:S(2)}, u32[]{:S(2)}) collective-permute-start(bf16[2048,768]{1,0:T(8,128)(2,1)} %bitcast_convert_fusion.2), channel_id=1, source_target_pairs={{0,1},{3,2},{4,5},{7,6},{8,9},{11,10},{12,13},{15,14},{16,17},{19,... | collective-permute-start | bytes 9437192 | tf_op jit(solution)/shard_map/ppermute | solution.py:698
  666.4 228.9 %collective-permute-start.8 = (bf16[2048,1024]{1,0:T(8,128)(2,1)}, bf16[2048,1024]{1,0:T(8,128)(2,1)}, u32[]{:S(2)}, u32[]{:S(2)}) collective-permute-start(bf16[2048,1024]{1,0:T(8,128)(2,1)} %bitcast_convert_fusion), channel_id=1, source_target_pairs={{0,1},{3,2},{4,5},{7,6},{8,9},{11,10},{12,13},{15,14},{16,17},{19,... | collective-permute-start | bytes 12582920 | tf_op jit(solution)/shard_map/ppermute | solution.py:698
  669.8 41.9 %copy-start.16 = (bf16[8,256,256]{2,1,0:T(8,128)(2,1)S(1)}, bf16[8,256,256]{2,1,0:T(8,128)(2,1)}, u32[]{:S(2)}) copy-start(bf16[8,256,256]{2,1,0:T(8,128)(2,1)} %get-tuple-element.30) | copy-start | bytes 3145732
  811.0 110.6 %collective-permute-start.1 = (bf16[8,128,768]{2,1,0:T(8,128)(2,1)}, bf16[8,128,768]{2,1,0:T(8,128)(2,1)}, u32[]{:S(2)}, u32[]{:S(2)}) collective-permute-start(bf16[8,128,768]{2,1,0:T(8,128)(2,1)} %dynamic-slice_bitcast_fusion.2), channel_id=1, source_target_pairs={{1,2},{2,1},{5,6},{6,5},{9,10},{10,9},{13,14},{14,13},{17,18},{18,... | collective-permute-start | bytes 4718600 | tf_op jit(solution)/shard_map/ppermute | solution.py:703
  820.2 127.1 %collective-permute-start.5 = (bf16[8,128,1024]{2,1,0:T(8,128)(2,1)}, bf16[8,128,1024]{2,1,0:T(8,128)(2,1)}, u32[]{:S(2)}, u32[]{:S(2)}) collective-permute-start(bf16[8,128,1024]{2,1,0:T(8,128)(2,1)} %dynamic-slice_bitcast_fusion.1), channel_id=1, source_target_pairs={{1,2},{2,1},{5,6},{6,5},{9,10},{10,9},{13,14},{14,13},{17,18},{18,... | collective-permute-start | bytes 6291464 | tf_op jit(solution)/shard_map/ppermute | solution.py:703
  902.5 161.2 %collective-permute-start.9 = (bf16[8,128,1024]{2,1,0:T(8,128)(2,1)}, bf16[8,128,1024]{2,1,0:T(8,128)(2,1)}, u32[]{:S(2)}, u32[]{:S(2)}) collective-permute-start(bf16[8,128,1024]{2,1,0:T(8,128)(2,1)} %dynamic-slice_bitcast_fusion), channel_id=1, source_target_pairs={{1,2},{2,1},{5,6},{6,5},{9,10},{10,9},{13,14},{14,13},{17,18},{18,... | collective-permute-start | bytes 6291464 | tf_op jit(solution)/shard_map/ppermute | solution.py:703
  916.5 202.8 %all-to-all-start.3 = ((bf16[4,2,65536]{2,1,0:T(2,128)(2,1)}), bf16[4,2,65536]{2,1,0:T(2,128)(2,1)}, u32[]{:S(2)}, u32[]{:S(2)}) async-start(bf16[4,2,65536]{2,1,0:T(2,128)(2,1)} %reshape.182), calls=%async_computation.3 | async-start | bytes 2097152 | tf_op jit(solution)/shard_map/all_to_all | solution.py:735
  921.6 280.4 %all-gather.5.cloned.1.call-start = ((), (), s32[]{:S(2)}) async-start(), calls=%async_computation.5 | async-start | bytes 1769472 | tf_op jit(solution)/shard_map/all_gather | solution.py:837
  945.4 155.9 %collective-permute-start.2 = (bf16[8,128,768]{2,1,0:T(8,128)(2,1)}, bf16[8,128,768]{2,1,0:T(8,128)(2,1)}, u32[]{:S(2)}, u32[]{:S(2)}) collective-permute-start(bf16[8,128,768]{2,1,0:T(8,128)(2,1)} %plane_exchange.7), channel_id=1, source_target_pairs={{1,2},{2,1},{5,6},{6,5},{9,10},{10,9},{13,14},{14,13},{17,18},{18,... | collective-permute-start | bytes 4718600 | tf_op jit(solution)/shard_map/ppermute | solution.py:706
  977.8 147.1 %collective-permute-start.6 = (bf16[8,128,1024]{2,1,0:T(8,128)(2,1)}, bf16[8,128,1024]{2,1,0:T(8,128)(2,1)}, u32[]{:S(2)}, u32[]{:S(2)}) collective-permute-start(bf16[8,128,1024]{2,1,0:T(8,128)(2,1)} %plane_exchange.8), channel_id=1, source_target_pairs={{1,2},{2,1},{5,6},{6,5},{9,10},{10,9},{13,14},{14,13},{17,18},{18,... | collective-permute-start | bytes 6291464 | tf_op jit(solution)/shard_map/ppermute | solution.py:706
  1068.2 33.0 %copy-start.12 = (bf16[8,128,768]{2,1,0:T(8,128)(2,1)S(1)}, bf16[8,128,768]{2,1,0:T(8,128)(2,1)}, u32[]{:S(2)}) copy-start(bf16[8,128,768]{2,1,0:T(8,128)(2,1)} %plane_exchange.7) | copy-start | bytes 4718596
  1099.2 31.5 %collective-permute-start.10 = (bf16[8,128,1024]{2,1,0:T(8,128)(2,1)}, bf16[8,128,1024]{2,1,0:T(8,128)(2,1)}, u32[]{:S(2)}, u32[]{:S(2)}) collective-permute-start(bf16[8,128,1024]{2,1,0:T(8,128)(2,1)} %plane_exchange.9), channel_id=1, source_target_pairs={{1,2},{2,1},{5,6},{6,5},{9,10},{10,9},{13,14},{14,13},{17,18},{18,... | collective-permute-start | bytes 6291464 | tf_op jit(solution)/shard_map/ppermute | solution.py:706
  1104.9 129.9 %collective-permute-start.3 = (bf16[2,8,128,768]{3,2,1,0:T(8,128)(2,1)}, bf16[2,8,128,768]{3,2,1,0:T(8,128)(2,1)}, u32[]{:S(2)}, u32[]{:S(2)}) collective-permute-start(bf16[2,8,128,768]{3,2,1,0:T(8,128)(2,1)} %maximum_select_fusion.2), channel_id=1, source_target_pairs={{1,0},{2,3},{5,4},{6,7},{9,8},{10,11},{13,12},{14,15},{17,16},{18,... | collective-permute-start | bytes 9437192 | tf_op jit(solution)/shard_map/ppermute | solution.py:708
  1109.1 15.8 %copy-start.1 = (bf16[8,128,1024]{2,1,0:T(8,128)(2,1)S(1)}, bf16[8,128,1024]{2,1,0:T(8,128)(2,1)}, u32[]{:S(2)}) copy-start(bf16[8,128,1024]{2,1,0:T(8,128)(2,1)} %plane_exchange.8) | copy-start | bytes 6291460
  1119.3 75.5 %all-to-all-start.2 = ((bf16[4,2,65536]{2,1,0:T(2,128)(2,1)}), bf16[4,2,65536]{2,1,0:T(2,128)(2,1)}, u32[]{:S(2)}, u32[]{:S(2)}) async-start(bf16[4,2,65536]{2,1,0:T(2,128)(2,1)} %reshape.184), calls=%async_computation.2 | async-start | bytes 2097152 | tf_op jit(solution)/shard_map/all_to_all | solution.py:735
  1129.4 155.3 %collective-permute-start.7 = (bf16[2,8,128,1024]{3,2,1,0:T(8,128)(2,1)}, bf16[2,8,128,1024]{3,2,1,0:T(8,128)(2,1)}, u32[]{:S(2)}, u32[]{:S(2)}) collective-permute-start(bf16[2,8,128,1024]{3,2,1,0:T(8,128)(2,1)} %maximum_select_fusion), channel_id=1, source_target_pairs={{1,0},{2,3},{5,4},{6,7},{9,8},{10,11},{13,12},{14,15},{17,16},{18,... | collective-permute-start | bytes 12582920 | tf_op jit(solution)/shard_map/ppermute | solution.py:708
  1136.8 237.4 %collective-permute-start.11 = (bf16[2,8,128,1024]{3,2,1,0:T(8,128)(2,1)}, bf16[2,8,128,1024]{3,2,1,0:T(8,128)(2,1)}, u32[]{:S(2)}, u32[]{:S(2)}) collective-permute-start(bf16[2,8,128,1024]{3,2,1,0:T(8,128)(2,1)} %maximum_select_fusion.1), channel_id=1, source_target_pairs={{1,0},{2,3},{5,4},{6,7},{9,8},{10,11},{13,12},{14,15},{17,16},{18,... | collective-permute-start | bytes 12582920 | tf_op jit(solution)/shard_map/ppermute | solution.py:708
  1207.2 15.2 %copy-start.11 = (f32[32,12288]{1,0:T(8,128)S(1)}, f32[32,12288]{1,0:T(8,128)}, u32[]{:S(2)}) copy-start(f32[32,12288]{1,0:T(8,128)} %reshape.173) | copy-start | bytes 4718596
  1222.4 12.4 copy-start.13
  1291.2 83.0 %copy-start.2 = (bf16[8,128,1024]{2,1,0:T(8,128)(2,1)S(1)}, bf16[8,128,1024]{2,1,0:T(8,128)(2,1)}, u32[]{:S(2)}) copy-start(bf16[8,128,1024]{2,1,0:T(8,128)(2,1)} %plane_exchange.9) | copy-start | bytes 6291460
  (14 other events, 55.1 us)
Sparse Core Ops, SparseCore 0:
  718.7 81.7 all-reduce.2
Sparse Core Ops, SparseCore 1:
  1063.7 38.5 all-gather.4

commit v2 on v1

--- a/solution.py
+++ b/solution.py
@@ -681,33 +681,801 @@
     return lax.rsqrt(jnp.mean(features * features, axis=-1, keepdims=True) + EPSILON)
 
 
-def norm_back(features, grad_h, scaling):
-    inverse = rms_scale(features)
-    unit = features * inverse
-    inner = grad_h * (1.0 + scaling)
-    grad = (inner - unit * jnp.mean(inner * unit, axis=-1, keepdims=True)) * inverse
-    grad_scaling = jnp.sum(grad_h * unit, axis=0)
-    grad_shifting = jnp.sum(grad_h, axis=0)
-    return grad, grad_scaling, grad_shifting
-
-
-def plane_sum(weight_part, number):
-    depth, columns = weight_part.shape
-    rows = depth // 8
-    place = lax.axis_index("blk")
-    received = lax.ppermute(weight_part, "blk", [(0, 1), (3, 2)])
-    total = (weight_part.astype(jnp.float32) + received.astype(jnp.float32)).astype(jnp.bfloat16)
-    halves = total.reshape(8, 2, rows // 2, columns)
-    kept = lax.dynamic_index_in_dim(halves, jnp.where(place == 1, 0, 1), 1, keepdims=False)
-    sent = lax.dynamic_index_in_dim(halves, jnp.where(place == 1, 1, 0), 1, keepdims=False)
-    received = lax.ppermute(sent, "blk", [(1, 2), (2, 1)])
-    total = (kept.astype(jnp.float32) + received.astype(jnp.float32)).astype(jnp.bfloat16)
-    (mine,) = plane_exchange([total], number)
-    other = lax.ppermute(mine, "blk", [(1, 2), (2, 1)])
-    both = jnp.where(place == 1, jnp.stack([mine, other]), jnp.stack([other, mine]))
-    given = lax.ppermute(both, "blk", [(1, 0), (2, 3)])
-    result = jnp.where((place == 1) | (place == 2), both, given)
-    return result.transpose(0, 2, 1, 3).reshape(rows, 8 * columns).astype(jnp.float32)
+CHUNKS = 12
+EARLY = 8
+HALF_ROWS = 128
+BAND = 32
+
+
+def flipped(mine, flip):
+    total = 0
+    for bit in (1, 2, 4):
+        total = total + lax.rem(mine // bit + flip // bit, 2) * bit
+    return total
+
+
+def bands(count, step):
+    @pl.loop(0, count // BAND)
+    def _(index):
+        step(pl.ds(pl.multiple_of(index * BAND, BAND), BAND))
+
+
+def plain(ref, rows):
+    return ref[rows, :].astype(jnp.float32)
+
+
+class Plane:
+    def __init__(self):
+        self.mine, self.place, self.at = plane_places()
+
+    def to(self, flip):
+        return (self.at(flip), self.place)
+
+    def got(self, ref, sem):
+        remote(ref, ref, sem, sem, (self.mine, self.place)).wait_recv()
+
+    def gone(self, ref, sem):
+        remote(ref, ref, sem, sem, (self.mine, self.place)).wait_send()
+
+
+def scatter_flow(plane, own_of, fetch, peer, far, near, sems, finish):
+    core_recv, far_send, far_recv, near_send, near_recv = sems
+    rows = near.shape[1]
+    half = rows // 2
+    sent = []
+
+    def add(slot, start, count, extra=None):
+        own = own_of(slot)
+
+        def step(band):
+            at = pl.ds(pl.multiple_of(start + band.start, BAND), BAND)
+            total = plain(own, at) + plain(peer.at[slot], at)
+            if extra is not None:
+                total = total + plain(extra, band)
+            peer[slot, at, :] = total.astype(jnp.bfloat16)
+
+        bands(count, step)
+
+    def send(src, dst, flip, send_sem, recv_sem):
+        copy = remote(src, dst, send_sem, recv_sem, plane.to(flip))
+        copy.start()
+        sent.append(copy)
+
+    def send_near(slot, part):
+        at = pl.ds(part * half, half)
+        index = (slot - 1) * 2 + part
+        send(
+            peer.at[slot, at],
+            near.at[slot - 1, at],
+            2 * slot,
+            near_send.at[index],
+            near_recv.at[index],
+        )
+
+    fetch(3)
+    plane.got(peer.at[3], core_recv.at[3])
+    add(3, 0, rows)
+    send(peer.at[3, pl.ds(0, half)], far.at[0], 2, far_send.at[0], far_recv.at[0])
+    send(peer.at[3, pl.ds(half, half)], far.at[1], 4, far_send.at[1], far_recv.at[1])
+    fetch(1)
+    plane.got(peer.at[1], core_recv.at[1])
+    add(1, 0, half)
+    send_near(1, 0)
+    fetch(2)
+    plane.got(peer.at[2], core_recv.at[2])
+    add(2, half, half)
+    send_near(2, 1)
+    yield
+    plane.got(far.at[0], far_recv.at[0])
+    add(2, 0, half, far.at[0])
+    send_near(2, 0)
+    plane.got(far.at[1], far_recv.at[1])
+    add(1, half, half, far.at[1])
+    send_near(1, 1)
+    fetch(0)
+    plane.got(peer.at[0], core_recv.at[0])
+    yield
+    for slot in (1, 2):
+        for part in (0, 1):
+            at = pl.ds(part * half, half)
+            plane.got(near.at[slot - 1, at], near_recv.at[(slot - 1) * 2 + part])
+    own = own_of(0)
+
+    def step(at):
+        finish(
+            at,
+            plain(own, at)
+            + plain(peer.at[0], at)
+            + plain(near.at[0], at)
+            + plain(near.at[1], at),
+        )
+
+    bands(rows, step)
+    for copy in sent:
+        copy.wait_send()
+
+
+def back_kernel(
+    partial_grad,
+    partial_out,
+    early,
+    h_all,
+    qkv_all,
+    attended_all,
+    qkv_weight,
+    out_weight,
+    features,
+    first_sum,
+    attn_out,
+    grad_out,
+    mod,
+    shares,
+    token_out,
+    token_grad,
+    mod_out,
+    late,
+    land_a,
+    land_b,
+    first_buf,
+    second_buf,
+    stage,
+    own_grad,
+    grad_all,
+    grad_first,
+    image_out,
+    image_grad,
+    grad_qkv,
+    h_cols,
+    qkv_buf,
+    attended_buf,
+    late_buf,
+    out_sum,
+    sum_buf,
+    in_buf,
+    half_buf,
+    half_in,
+    mod_sum,
+    mod_land,
+    core_send,
+    core_recv,
+    far_send,
+    far_recv,
+    near_send,
+    near_recv,
+    stage_sems,
+    gather_send,
+    gather_recv,
+    load_sems,
+    late_sems,
+    z_sems,
+    x_sems,
+    zload_sems,
+    token_sems,
+    mod_sems,
+):
+    plane = Plane()
+    mine, place = plane.mine, plane.place
+    rows, width = features.shape
+    at = plane.at
+    is_mid = (place == 1) | (place == 2)
+    my_half = pl.ds(pl.multiple_of(jnp.where(place == 2, HALF_ROWS, 0), HALF_ROWS), HALF_ROWS)
+    other_half = pl.ds(pl.multiple_of(jnp.where(place == 2, 0, HALF_ROWS), HALF_ROWS), HALF_ROWS)
+    partner = (mine, 3 - place)
+    outer = (mine, jnp.where(place == 1, 0, 3))
+    inner = (mine, jnp.where(place == 0, 1, 2))
+    others = [lax.rem(place + step, 4) for step in (1, 2, 3)]
+    greet([plane.to(flip) for flip in range(1, 8)] + [(mine, other) for other in others])
+
+    def z_copy(kind, chunk, src, dst, target):
+        return remote(src, dst, z_sems.at[0, kind, chunk], z_sems.at[1, kind, chunk], target)
+
+    def start_outward(chunk):
+        if isinstance(chunk, int) and chunk >= EARLY:
+            src = late.at[chunk - EARLY]
+        else:
+            src = early.at[chunk]
+        z_copy(0, chunk, src, land_a.at[chunk], inner).start()
+
+    def stage_d(k):
+        region = shares.at[k, :, other_half]
+        plane.got(region, z_sems.at[1, 2, k])
+        z_copy(4, k, region, region, outer).start()
+
+    def stage_x(k):
+        region = shares.at[k, :, my_half]
+        plane.got(region, x_sems.at[1, k])
+        z_copy(2, k, region, region, partner).start()
+        z_copy(3, k, region, region, outer).start()
+
+    def stage_f(k):
+        slot = k % 2
+        load = pltpu.make_async_copy(land_b.at[k], half_in, zload_sems.at[2])
+        plane.got(land_b.at[k], z_sems.at[1, 1, k])
+        load.start()
+        if k >= 2:
+            plane.gone(half_buf.at[slot, pl.ds(0, 7)], x_sems.at[0, k - 2])
+        load.wait()
+
+        @pl.loop(0, 8)
+        def _(block):
+            half_buf[slot, block] = (
+                sum_buf[slot, block, my_half, :].astype(jnp.float32)
+                + half_in[block].astype(jnp.float32)
+            ).astype(jnp.bfloat16)
+
+        if k == CHUNKS - 1:
+            pltpu.make_async_copy(
+                half_buf.at[slot], shares.at[k, :, my_half], x_sems.at[1, k]
+            ).start()
+            return
+        pltpu.make_async_copy(
+            half_buf.at[slot, mine], shares.at[k, mine, my_half], x_sems.at[1, k]
+        ).start()
+        for flip in (6, 7, 2, 4, 3, 5, 1):
+            remote(
+                half_buf.at[slot, at(flip)],
+                shares.at[k, mine, my_half],
+                x_sems.at[0, k],
+                x_sems.at[1, k],
+                plane.to(flip),
+            ).start()
+
+    def stage_s(k):
+        slot = k % 2
+        if k >= 2:
+            plane.gone(sum_buf.at[slot, :, other_half], z_sems.at[0, 1, k - 2])
+        src = late.at[k - EARLY] if k >= EARLY else early.at[k]
+        own_load = pltpu.make_async_copy(src, sum_buf.at[slot], zload_sems.at[0])
+        own_load.start()
+        in_load = pltpu.make_async_copy(land_a.at[k], in_buf, zload_sems.at[1])
+        plane.got(land_a.at[k], z_sems.at[1, 0, k])
+        in_load.start()
+        own_load.wait()
+        in_load.wait()
+
+        @pl.loop(0, 8)
+        def _(block):
+            sum_buf[slot, block] = (
+                sum_buf[slot, block].astype(jnp.float32) + in_buf[block].astype(jnp.float32)
+            ).astype(jnp.bfloat16)
+
+        z_copy(1, k, sum_buf.at[slot, :, other_half], land_b.at[k], partner).start()
+
+    def tick(now):
+        @pl.when(jnp.logical_not(is_mid))
+        def _():
+            if now < CHUNKS:
+                plane.gone(land_a.at[now], z_sems.at[0, 0, now])
+            if now + 2 < CHUNKS:
+                start_outward(now + 2)
+
+        @pl.when(is_mid)
+        def _():
+            if 0 <= now - 3 < CHUNKS:
+                stage_d(now - 3)
+            if 0 <= now - 2 < CHUNKS:
+                stage_x(now - 2)
+            if 0 <= now - 1 < CHUNKS:
+                stage_f(now - 1)
+            if now < CHUNKS:
+                stage_s(now)
+
+    @pl.when(jnp.logical_not(is_mid))
+    def _():
+        start_outward(0)
+        start_outward(1)
+
+    attended_load = pltpu.make_async_copy(attended_all, attended_buf, load_sems.at[0])
+    attended_load.start()
+    mod_sum[...] = jnp.zeros_like(mod_sum)
+    row = {
+        name: number
+        for number, name in enumerate(
+            ("shift_one", "scale_one", "gate_one", "shift_two", "scale_two", "gate_two", "live")
+        )
+    }
+
+    def mod_row(name):
+        return mod[pl.ds(row[name], 1), :]
+
+    def accumulate(name, value):
+        mod_sum[pl.ds(row[name], 1), :] += jnp.sum(value, axis=0, keepdims=True)
+
+    def sems(number):
+        return (
+            core_recv.at[number],
+            far_send.at[number],
+            far_recv.at[number],
+            near_send.at[number],
+            near_recv.at[number],
+        )
+
+    class Halves:
+        def __init__(self, ref):
+            self.ref = ref
+
+        @property
+        def at(self):
+            return self
+
+        def __getitem__(self, number):
+            return self.ref.at[pl.ds(number * (rows // 2), rows // 2)]
+
+    def give(src, buf, number, slot):
+        remote(
+            src, buf.at[slot], core_send.at[number, slot], core_recv.at[number, slot], plane.to(1)
+        ).start()
+
+    def staged_flow(source, buf, number, finish):
+        for slot in (3, 1, 2, 0):
+            give(source.at[at((2 * slot) ^ 1)], buf, number, slot)
+        order = {3: 0, 1: 1, 2: 0, 0: 1}
+
+        def load(slot):
+            return pltpu.make_async_copy(
+                source.at[at(2 * slot)], stage.at[order[slot]], stage_sems.at[number, slot]
+            )
+
+        load(3).start()
+        load(1).start()
+
+        def fetch(slot):
+            if slot == 2:
+                load(2).start()
+            if slot == 0:
+                load(0).start()
+            load(slot).wait()
+
+        return scatter_flow(
+            plane,
+            lambda slot: stage.at[order[slot]],
+            fetch,
+            buf.at[pl.ds(0, 4)],
+            Halves(buf.at[6]),
+            buf.at[pl.ds(4, 2)],
+            sems(number),
+            finish,
+        )
+
+    def run(flow, first_tick):
+        for step, _ in enumerate(flow):
+            tick(first_tick + step)
+
+    def finish_out(where, value):
+        base = first_sum[where, :]
+        image_out[where, :] = (
+            mod_row("live") * (base + mod_row("gate_two") * value)
+        ).astype(jnp.bfloat16)
+        accumulate("gate_two", plain(grad_out, where) * value)
+
+    token_copies = []
+
+    def return_tokens(image, result, number):
+        piece = rows // 4
+        own = pltpu.make_async_copy(
+            image.at[pl.ds(pl.multiple_of(place * piece, piece), piece)],
+            result.at[place],
+            token_sems.at[0, number, 0],
+        )
+        own.start()
+        token_copies.append(own)
+        for step, other in enumerate(others):
+            copy = remote(
+                image.at[pl.ds(pl.multiple_of(other * piece, piece), piece)],
+                result.at[place],
+                token_sems.at[0, number, step + 1],
+                token_sems.at[1, number, step + 1],
+                (mine, other),
+            )
+            copy.start()
+            token_copies.append(copy)
+
+    run(staged_flow(partial_out, first_buf, 0, finish_out), 0)
+    return_tokens(image_out, token_out, 0)
+
+    def back_norm(source, value, scale_name, shift_name):
+        inverse = rms_scale(source)
+        unit = source * inverse
+        inner = value * (1.0 + mod_row(scale_name))
+        accumulate(scale_name, value * unit)
+        accumulate(shift_name, value)
+        return (inner - unit * jnp.mean(inner * unit, axis=-1, keepdims=True)) * inverse
+
+    def finish_feed(where, value):
+        total = back_norm(first_sum[where, :], value, "scale_two", "shift_two") + plain(
+            grad_out, where
+        )
+        grad_first[where, :] = total
+        accumulate("gate_one", total * attn_out[where, :])
+        low_grad = (mod_row("gate_one") * total).astype(jnp.bfloat16)
+        own_grad[where, :] = low_grad
+        grad_all[mine, where, :] = low_grad
+
+    run(staged_flow(partial_grad, second_buf, 1, finish_feed), 2)
+
+    piece = rows // PIECES
+
+    def forward(src, owner, part, flip, slot):
+        copy = remote(
+            src,
+            grad_all.at[owner, pl.ds(part * piece, piece)],
+            gather_send.at[slot],
+            gather_recv.at[slot],
+            plane.to(flip),
+        )
+        copy.start()
+
+    def arrived(owner, part, slot):
+        ref = grad_all.at[owner, pl.ds(part * piece, piece)]
+        plane.got(ref, gather_recv.at[slot])
+        return ref
+
+    for part in range(PIECES):
+        src = own_grad.at[pl.ds(part * piece, piece)]
+        forward(src, mine, part, 2, part)
+        forward(src, mine, part, 4, PIECES + part)
+        forward(src, mine, part, 1, 3 * PIECES + part)
+
+    def arrive(step):
+        if step == 2:
+            for part in range(PIECES):
+                got = arrived(at(2), part, part)
+                if part < PIECES // 2:
+                    forward(got, at(2), part, 4, 2 * PIECES + part)
+                forward(got, at(2), part, 1, 4 * PIECES + part)
+                got = arrived(at(4), part, PIECES + part)
+                if part >= PIECES // 2:
+                    forward(got, at(4), part, 2, 2 * PIECES + part)
+                forward(got, at(4), part, 1, 5 * PIECES + part)
+        if step == 6:
+            for part in range(PIECES):
+                got = arrived(at(6), part, 2 * PIECES + part)
+                forward(got, at(6), part, 1, 6 * PIECES + part)
+        if step % 2:
+            for part in range(PIECES):
+                arrived(at(step), part, (3 + step // 2) * PIECES + part)
+
+    def qkv_load(step):
+        return pltpu.make_async_copy(
+            qkv_all.at[flipped(mine, step)], qkv_buf.at[lax.rem(step, 2)], load_sems.at[1 + lax.rem(step, 2)]
+        )
+
+    qkv_load(0).start()
+    attended_load.wait()
+    out_sum[...] = jnp.zeros_like(out_sum)
+    columns = qkv_buf.shape[-1]
+    third = columns // 3
+    scale = HD ** (-0.5)
+
+    @pl.loop(0, 8)
+    def _(step):
+        for number in range(8):
+
+            @pl.when(step == number)
+            def _(number=number):
+                arrive(number)
+
+        image = flipped(mine, step)
+        slot = lax.rem(step, 2)
+        qkv_load(step).wait()
+
+        @pl.when(step < 7)
+        def _():
+            qkv_load(step + 1).start()
+
+        grad = grad_all[image]
+        grad_attended = contract(grad, out_weight[...], 1, 1).astype(jnp.bfloat16)
+        image_rows = pl.ds(pl.multiple_of(image * rows, rows), rows)
+        for head in range(third // HD):
+            begin = head * HD
+            queries = qkv_buf[slot, :, begin : begin + HD]
+            key_rows = qkv_buf[slot, :, third + begin : third + begin + HD]
+            value_rows = qkv_buf[slot, :, 2 * third + begin : 2 * third + begin + HD]
+            grad_head = grad_attended[:, begin : begin + HD]
+            attention = softmax_rows(queries, key_rows)
+            grad_weights = contract(grad_head, value_rows, 1, 1)
+            row_delta = jnp.sum(attention * grad_weights, axis=-1, keepdims=True)
+            grad_scores = (attention * (grad_weights - row_delta)).astype(jnp.bfloat16)
+            grad_qkv[image_rows, begin : begin + HD] = (
+                contract(grad_scores, key_rows, 1, 0) * scale
+            ).astype(jnp.bfloat16)
+            grad_qkv[image_rows, third + begin : third + begin + HD] = (
+                contract(grad_scores, queries, 0, 0) * scale
+            ).astype(jnp.bfloat16)
+            grad_qkv[image_rows, 2 * third + begin : 2 * third + begin + HD] = contract(
+                attention.astype(jnp.bfloat16), grad_head, 0, 0
+            ).astype(jnp.bfloat16)
+        out_sum[...] += contract(attended_buf[image], grad, 0, 0)
+        second_buf[step] = contract(grad_qkv[image_rows, :], qkv_weight[...], 1, 1).astype(
+            jnp.bfloat16
+        )
+        for number in (1, 3, 5, 7):
+
+            @pl.when(step == number)
+            def _(number=number):
+                give(second_buf.at[number], first_buf, 2, number // 2)
+
+        for number, now in ((2, 4), (5, 5)):
+
+            @pl.when(step == number)
+            def _(now=now):
+                tick(now)
+
+    for slot in range(7 * PIECES):
+        plane.gone(own_grad.at[pl.ds(0, piece)], gather_send.at[slot])
+
+    def cols_load(block):
+        return pltpu.make_async_copy(
+            h_all.at[:, :, pl.ds(pl.multiple_of(block * rows, rows), rows)],
+            h_cols.at[lax.rem(block, 2)],
+            load_sems.at[3 + lax.rem(block, 2)],
+        )
+
+    cols_load(0).start()
+    for block in range(8):
+        late_buf[3, block] = out_sum[:, block * rows : (block + 1) * rows].astype(jnp.bfloat16)
+
+    @pl.loop(0, 8)
+    def _(block):
+        cols_load(block).wait()
+
+        @pl.when(block < 7)
+        def _():
+            cols_load(block + 1).start()
+
+        cols = h_cols[lax.rem(block, 2)].reshape(8 * rows, rows)
+        product = contract(cols, grad_qkv[...], 0, 0)
+        for number in range(3):
+            late_buf[number, block] = product[:, number * third : (number + 1) * third].astype(
+                jnp.bfloat16
+            )
+
+    late_copy = pltpu.make_async_copy(late_buf, late, late_sems)
+    late_copy.start()
+
+    def finish_input(where, value):
+        total = back_norm(plain(features, where), value, "scale_one", "shift_one")
+        image_grad[where, :] = (total + grad_first[where, :]).astype(jnp.bfloat16)
+
+    late_copy.wait()
+    run(
+        scatter_flow(
+            plane,
+            lambda slot: second_buf.at[2 * slot],
+            lambda slot: None,
+            first_buf.at[pl.ds(0, 4)],
+            Halves(first_buf.at[6]),
+            first_buf.at[pl.ds(4, 2)],
+            sems(2),
+            finish_input,
+        ),
+        6,
+    )
+    return_tokens(image_grad, token_grad, 1)
+
+    mod_copies = []
+    mod_land[place] = mod_sum[...]
+    for step, other in enumerate(others):
+        copy = remote(
+            mod_sum, mod_land.at[place], mod_sems.at[0, step], mod_sems.at[1, step], (mine, other)
+        )
+        copy.start()
+        mod_copies.append(copy)
+    tick(8)
+    for copy in mod_copies:
+        copy.wait_recv()
+    own = pltpu.make_async_copy(mod_land, mod_out.at[mine], mod_sems.at[0, 3])
+    own.start()
+    plane_copies = []
+    for flip in range(1, 8):
+        copy = remote(
+            mod_land,
+            mod_out.at[mine],
+            mod_sems.at[0, 3 + flip],
+            mod_sems.at[1, 3 + flip],
+            plane.to(flip),
+        )
+        copy.start()
+        plane_copies.append(copy)
+    for now in range(9, CHUNKS + 3):
+        tick(now)
+    own.wait()
+    for copy in mod_copies:
+        copy.wait_send()
+    for copy in plane_copies:
+        copy.wait()
+    for copy in token_copies:
+        copy.wait()
+    for number in range(3):
+        for slot in range(4):
+            plane.gone(second_buf.at[slot], core_send.at[number, slot])
+
+    @pl.when(is_mid)
+    def _():
+        for k in (CHUNKS - 2, CHUNKS - 1):
+            plane.gone(sum_buf.at[k % 2, :, other_half], z_sems.at[0, 1, k])
+        plane.gone(half_buf.at[0, pl.ds(0, 7)], x_sems.at[0, CHUNKS - 2])
+        for k in range(CHUNKS):
+            plane.gone(shares.at[k, :, my_half], z_sems.at[0, 2, k])
+            plane.gone(shares.at[k, :, my_half], z_sems.at[0, 3, k])
+            plane.gone(shares.at[k, :, other_half], z_sems.at[0, 4, k])
+
+    @pl.when(jnp.logical_not(is_mid))
+    def _():
+        first = pl.ds(pl.multiple_of(jnp.where(place == 0, 0, HALF_ROWS), HALF_ROWS), HALF_ROWS)
+        second = pl.ds(pl.multiple_of(jnp.where(place == 0, HALF_ROWS, 0), HALF_ROWS), HALF_ROWS)
+        for k in range(CHUNKS):
+            plane.got(shares.at[k, :, first], z_sems.at[1, 3, k])
+            plane.got(shares.at[k, :, second], z_sems.at[1, 4, k])
+
+
+def back_part(
+    partial_grad,
+    partial_out,
+    early,
+    h_all,
+    qkv_all,
+    attended_all,
+    qkv_weight,
+    out_weight,
+    features,
+    first_sum,
+    attn_out,
+    grad_out,
+    mod,
+):
+    images, rows, width = h_all.shape
+    columns = qkv_weight.shape[1]
+    low, full = jnp.bfloat16, jnp.float32
+    dma = pltpu.SemaphoreType.DMA
+    anywhere, inside = pl.BlockSpec(memory_space=pl.ANY), pl.BlockSpec(memory_space=pltpu.VMEM)
+    return pl.pallas_call(
+        back_kernel,
+        out_shape=[
+            jax.ShapeDtypeStruct((CHUNKS, 8, rows, rows), low),
+            jax.ShapeDtypeStruct((4, rows // 4, width), low),
+            jax.ShapeDtypeStruct((4, rows // 4, width), low),
+            jax.ShapeDtypeStruct((8, 4, 8, width), full),
+            jax.ShapeDtypeStruct((CHUNKS - EARLY, 8, rows, rows), low),
+            jax.ShapeDtypeStruct((CHUNKS, 8, rows, rows), low),
+            jax.ShapeDtypeStruct((CHUNKS, 8, HALF_ROWS, rows), low),
+        ],
+        in_specs=[anywhere] * 6 + [inside] * 7,
+        out_specs=[anywhere] * 7,
+        scratch_shapes=[
+            pltpu.VMEM((7, rows, width), low),
+            pltpu.VMEM((8, rows, width), low),
+            pltpu.VMEM((2, rows, width), low),
+            pltpu.VMEM((rows, width), low),
+            pltpu.VMEM((8, rows, width), low),
+            pltpu.VMEM((rows, width), full),
+            pltpu.VMEM((rows, width), low),
+            pltpu.VMEM((rows, width), low),
+            pltpu.VMEM((8 * rows, columns), low),
+            pltpu.VMEM((2, 8, rows, rows), low),
+            pltpu.VMEM((2, rows, columns), low),
+            pltpu.VMEM((8, rows, columns // 3), low),
+            pltpu.VMEM((4, 8, rows, rows), low),
+            pltpu.VMEM((columns // 3, width), full),
+            pltpu.VMEM((2, 8, rows, rows), low),
+            pltpu.VMEM((8, rows, rows), low),
+            pltpu.VMEM((2, 8, HALF_ROWS, rows), low),
+            pltpu.VMEM((8, HALF_ROWS, rows), low),
+            pltpu.VMEM((8, width), full),
+            pltpu.VMEM((4, 8, width), full),
+            dma((3, 4)),
+            dma((3, 4)),
+            dma((3, 2)),
+            dma((3, 2)),
+            dma((3, 4)),
+            dma((3, 4)),
+            dma((2, 4)),
+            dma((7 * PIECES,)),
+            dma((7 * PIECES,)),
+            dma((5,)),
+            dma,
+            dma((2, 5, CHUNKS)),
+            dma((2, CHUNKS)),
+            dma((3,)),
+            dma((2, 2, 4)),
+            dma((2, 11)),
+        ],
+        compiler_params=pltpu.CompilerParams(
+            collective_id=4, has_side_effects=True, vmem_limit_bytes=63 * 1024 * 1024
+        ),
+        name="back_part",
+    )(
+        partial_grad,
+        partial_out,
+        early,
+        h_all,
+        qkv_all,
+        attended_all,
+        qkv_weight,
+        out_weight,
+        features,
+        first_sum,
+        attn_out,
+        grad_out,
+        mod,
+    )
+
+
+def early_kernel(grad_mlp, h_two, hidden, grad_pre, out_ref):
+    step = pl.program_id(0)
+
+    def product(left, right):
+        for block in range(8):
+            size = out_ref.shape[-1]
+            out_ref[0, block] = contract(
+                left[:, block * size : (block + 1) * size], right[...], 0, 0
+            ).astype(jnp.bfloat16)
+
+    @pl.when(step < 4)
+    def _():
+        product(grad_mlp, hidden)
+
+    @pl.when(step >= 4)
+    def _():
+        product(h_two, grad_pre)
+
+
+def early_grads(grad_mlp, h_two, hidden, grad_pre):
+    tokens, width = grad_mlp.shape
+    size = width // 8
+    once = pl.Buffered(1)
+    return pl.pallas_call(
+        early_kernel,
+        grid=(EARLY,),
+        out_shape=jax.ShapeDtypeStruct((EARLY, 8, size, size), jnp.bfloat16),
+        in_specs=[
+            pl.BlockSpec((tokens, width), lambda step: (0, 0), pipeline_mode=once),
+            pl.BlockSpec((tokens, width), lambda step: (0, 0), pipeline_mode=once),
+            pl.BlockSpec((tokens, size), lambda step: (0, jnp.minimum(step, 3))),
+            pl.BlockSpec((tokens, size), lambda step: (0, jnp.maximum(step - 4, 0))),
+        ],
+        out_specs=pl.BlockSpec((1, 8, size, size), lambda step: (step, 0, 0, 0)),
+        compiler_params=pltpu.CompilerParams(vmem_limit_bytes=VMEM_BYTES),
+        name="early_grads",
+    )(grad_mlp, h_two, hidden, grad_pre)
+
+
+def mlp_spread_kernel(share_ref, out_ref):
+    size = share_ref.shape[-1]
+    for number in range(4):
+        out_ref[:, number * size : (number + 1) * size] = share_ref[number, 0].astype(jnp.float32)
+
+
+def mlp_spread(shares):
+    rows = shares.shape[2]
+    return pl.pallas_call(
+        mlp_spread_kernel,
+        grid=(2, 8),
+        out_shape=jax.ShapeDtypeStruct((rows, 64 * rows), jnp.float32),
+        in_specs=[pl.BlockSpec((4, 1, rows, rows), lambda part, block: (1 - part, block, 0, 0))],
+        out_specs=pl.BlockSpec((rows, 4 * rows), lambda part, block: (0, part * 8 + block)),
+        compiler_params=pltpu.CompilerParams(vmem_limit_bytes=VMEM_BYTES),
+        name="mlp_spread",
+    )(shares)
+
+
+def attn_spread_kernel(share_ref, out_ref):
+    size = share_ref.shape[-1]
+    for number in range(8):
+        out_ref[:, number * size : (number + 1) * size] = share_ref[0, number].astype(jnp.float32)
+
+
+def attn_spread(shares):
+    rows = shares.shape[2]
+    return pl.pallas_call(
+        attn_spread_kernel,
+        grid=(4,),
+        out_shape=jax.ShapeDtypeStruct((rows, 32 * rows), jnp.float32),
+        in_specs=[pl.BlockSpec((1, 8, rows, rows), lambda part: (EARLY + part, 0, 0, 0))],
+        out_specs=pl.BlockSpec((rows, 8 * rows), lambda part: (0, part)),
+        compiler_params=pltpu.CompilerParams(vmem_limit_bytes=VMEM_BYTES),
+        name="attn_spread",
+    )(shares)
 
 
 def plane_body(
@@ -731,11 +1499,6 @@
     def to_images(tokens):
         return lax.all_to_all(tokens, "blk", split_axis=0, concat_axis=1, tiled=True)[0]
 
-    def to_tokens(image):
-        return lax.all_to_all(
-            image.reshape(1, -1, model_width), "blk", split_axis=1, concat_axis=0, tiled=True
-        )
-
     features = to_images(block_input).astype(jnp.float32)
     incoming = to_images(cotangent).astype(jnp.float32)
     live = (place < image_counts[0]).astype(jnp.float32)
@@ -772,20 +1535,21 @@
     def columns_apart(weight):
         return weight.astype(jnp.bfloat16).reshape(rows, 8, feed_piece).transpose(1, 0, 2)
 
+    up_weight, down_weight = [
+        lax.all_to_all(
+            columns_apart(weight), "fsdp", split_axis=0, concat_axis=0, tiled=True
+        ).reshape(model_width, feed_piece)
+        for weight in (mlp_weight[:, :feed_width], mlp_weight[:, feed_width:])
+    ]
+    grad_out = incoming * live
+    grad_mlp = (gate_two * grad_out).astype(jnp.bfloat16)
+    grad_mlp_all = lax.all_gather(grad_mlp, "fsdp", axis=0)
     h_one = (features * rms_scale(features) * (1.0 + scale_one) + shift_one).astype(jnp.bfloat16)
     h_one_all = plane_gather(h_one)
     qkv_all, attended_all, partial = attention_forward(h_one_all, qkv_weight, out_weight)
     attn_out = plane_scatter(partial)
-    up_weight, down_weight = plane_exchange(
-        [columns_apart(mlp_weight[:, :feed_width]), columns_apart(mlp_weight[:, feed_width:])], 3
-    )
-    up_weight = up_weight.reshape(model_width, feed_piece)
-    down_weight = down_weight.reshape(model_width, feed_piece)
     first_sum = features + gate_one * attn_out
     h_two = (first_sum * rms_scale(first_sum) * (1.0 + scale_two) + shift_two).astype(jnp.bfloat16)
-    grad_out = incoming * live
-    grad_mlp = (gate_two * grad_out).astype(jnp.bfloat16)
-    grad_mlp_all = plane_gather(grad_mlp)
     h_two_all = plane_gather(h_two)
     hidden_all, grad_pre_all, partial_out, partial_grad = feed_both(
         h_two_all, grad_mlp_all, up_weight, down_weight
@@ -794,49 +1558,33 @@
     def flat(array):
         return array.reshape(-1, array.shape[-1])
 
-    def rows_low(left, right):
-        return rows_product(flat(left), flat(right)).astype(jnp.bfloat16)
-
-    down_grad = plane_sum(rows_low(grad_mlp_all, hidden_all), 4)
-    up_grad = plane_sum(rows_low(h_two_all, grad_pre_all), 5)
-    grad_h_two = plane_scatter(partial_grad)
-    grad_first, grad_scale_two, grad_shift_two = norm_back(first_sum, grad_h_two, scale_two)
-    grad_first = grad_first + grad_out
-    grad_attn_out = (gate_one * grad_first).astype(jnp.bfloat16)
-    grad_gate_one = jnp.sum(grad_first * attn_out, axis=0)
-    grad_attn_all = plane_gather(grad_attn_out)
-    grad_qkv_all, partial_h_one = attention_backward(
-        grad_attn_all, qkv_all, qkv_weight, out_weight
-    )
-    qkv_grad = plane_sum(rows_low(h_one_all, grad_qkv_all), 6)
-    qkv_grad = (
-        qkv_grad.reshape(rows, 8, 3, model_width // 8)
-        .transpose(0, 2, 1, 3)
-        .reshape(rows, 3 * model_width)
-    )
-    out_grad = lax.psum(rows_low(attended_all, grad_attn_all), "blk").astype(jnp.float32)
-    attn_weight_grad = jnp.concatenate([qkv_grad, out_grad], axis=1)
-    mlp_weight_grad = jnp.concatenate([up_grad, down_grad], axis=1)
-    grad_h_one = plane_scatter(partial_h_one)
-    grad_input, grad_scale_one, grad_shift_one = norm_back(features, grad_h_one, scale_one)
-    input_grad = to_tokens((grad_input + grad_first).astype(jnp.bfloat16)).astype(jnp.float32)
-    mlp_out = plane_scatter(partial_out)
-    block_out = to_tokens((live * (first_sum + gate_two * mlp_out)).astype(jnp.bfloat16))
-    grad_gate_two = jnp.sum(grad_out * mlp_out, axis=0)
-
-    grad_mod = jnp.concatenate(
+    early = early_grads(
+        flat(grad_mlp_all), flat(h_two_all), flat(hidden_all), flat(grad_pre_all)
+    )
+    mod_rows = jnp.concatenate(
         [
-            grad_shift_one,
-            grad_scale_one,
-            grad_gate_one,
-            grad_shift_two,
-            grad_scale_two,
-            grad_gate_two,
+            mod_image.reshape(6, model_width),
+            jnp.full((2, model_width), live, jnp.float32),
         ]
     )
-    grad_images = lax.all_gather(
-        lax.all_gather(grad_mod, "blk", axis=0), "fsdp", axis=0, tiled=True
-    )
+    shares, token_out, token_grad, mod_out, _, _, _ = back_part(
+        partial_grad,
+        partial_out,
+        early,
+        h_one_all,
+        qkv_all,
+        attended_all,
+        qkv_weight,
+        out_weight,
+        features.astype(jnp.bfloat16),
+        first_sum,
+        attn_out,
+        grad_out.astype(jnp.bfloat16),
+        mod_rows,
+    )
+    block_out, input_grad = token_out, token_grad.astype(jnp.float32)
+    attn_weight_grad, mlp_weight_grad = attn_spread(shares), mlp_spread(shares)
+    grad_images = mod_out[:, :, :6].reshape(-1, 6 * model_width)
     onehot_all = (
         all_bins.reshape(-1)[:, None] == jnp.arange(bins, dtype=jnp.int32)[None, :]
     ).astype(jnp.float32)

time: 1420 us -> 950 us (0.67)
  waiting for transfers between devices: 299 us -> 72.1 us
  Pallas kernels: 629 us -> 733 us
  local copies, waits for them, and re-layouts: 131 us -> 32.3 us
  other arithmetic: 110 us -> 19.5 us
  blocking collectives: 91 us -> 8.01 us
  matrix products: 80.2 us -> 37.6 us
  starting transfers between devices: 50.5 us -> 20.9 us
    pallas_call x1 -> x4, Pallas kernels: 25.7 us -> 466 us  [the longest x1 419 us: back_part(): pl.pallas_call(back_kernel, out_shape=[jax.ShapeDtypeStruct((CHUNKS, 8, r...]
    ppermute x12 -> x0, waiting for transfers between devices: 252 us -> none  [the longest x3 160 us: plane_sum(): received = lax.ppermute(weight_part, 'blk', [(0, 1), (3, 2)])]
    pallas_call x5 -> x1, Pallas kernels: 214 us -> 42.8 us  [plane_exchange(): pl.pallas_call(functools.partial(exchange_kernel, count), out_shape=[jax....]
    pallas_call x4 -> x1, Pallas kernels: 167 us -> 41.7 us  [plane_scatter(): pl.pallas_call(scatter_kernel, out_shape=jax.ShapeDtypeStruct((rows, widt...]
    all_gather x1 -> x0, blocking collectives: 83 us -> none  [plane_body(): lax.all_gather(grad_mod, 'blk', axis=0)]
    unnamed x76 -> x22, local copies, waits for them, and re-layouts: 66.6 us -> 7.97 us
    dot_general x4 -> x0, matrix products: 43.1 us -> none  [rows_product(): lax.dot_general(left_rows, right_rows, (((0,), (0,)), ((), ())), preferre...]
    convert_element_type x11 -> x2, other arithmetic: 42.8 us -> 4.09 us  [the longest x1 2.53 us: plane_body(): grad_out.astype(jnp.bfloat16)]
  transfers between devices with their start and end apart: 18 -> 5, of which waited for: 5 -> 2; matrix products, arithmetic and copies ran while one was open for 19% -> 5% of each run, Pallas kernels for 30% -> 24%
where the time goes in v2:
time: 950 us; the launch traced here: 940 us
  Pallas kernels  733 us (77%)
  waiting for transfers between devices  72.1 us (8%)
  matrix products  37.6 us (4%)
  local copies, waits for them, and re-layouts  32.3 us (3%)
  starting transfers between devices  20.9 us (2%)
  other arithmetic  19.5 us (2%)
  between operations  16 us (2%)
    pallas_call x1, Pallas kernels, back_part(): pl.pallas_call(back_kernel, out_shape=[jax.ShapeDtypeStruct((CHUNKS, 8, r...  419 us
    pallas_call x2, Pallas kernels, plane_gather(): pl.pallas_call(gather_kernel, out_shape=jax.ShapeDtypeStruct((8, rows, wi...  119 us
    all_to_all x2, waiting for transfers between devices, plane_body(): lax.all_to_all(columns_apart(weight), 'fsdp', split_axis=0, concat_axis=0...  58.2 us
    pallas_call x1, Pallas kernels, plane_exchange(): pl.pallas_call(functools.partial(exchange_kernel, count), out_shape=[jax....  42.8 us
    pallas_call x1, Pallas kernels, plane_scatter(): pl.pallas_call(scatter_kernel, out_shape=jax.ShapeDtypeStruct((rows, widt...  41.7 us
    pallas_call x1, Pallas kernels, feed_both(): pl.pallas_call(feed_kernel, grid=(images,), out_shape=[jax.ShapeDtypeStru...  41.7 us
    pallas_call x1, Pallas kernels, early_grads(): pl.pallas_call(early_kernel, grid=(EARLY,), out_shape=jax.ShapeDtypeStruc...  27.3 us
    pallas_call x1, Pallas kernels, attention_forward(): pl.pallas_call(attention_kernel, grid=(images,), out_shape=[jax.ShapeDtyp...  22.2 us
  transfers between devices with their start and end apart: 5, of which 2 were waited for; matrix products, arithmetic and copies ran while one was open for 5% of the time, Pallas kernels for 24%

profile of v2, /device:TPU:0, one launch (start us, length us, event | category | flops | bytes accessed | tf_op | source)
XLA Modules:
  0.0 939.6 jit_solution(6794284284973771272)
XLA Ops:
  7.2 6.3 all-to-all-start.1
  16.3 8.0 all-reduce.1
  26.5 9.1 convolution_add_fusion
  37.5 1.7 copy-done.2
  40.2 3.4 copy.24
  43.6 4.6 copy.26.refs_1_
  48.2 42.8 %plane_exchange.1 = (f32[8,6,2048]{2,1,0:T(8,128)}, bf16[8,256,768]{2,1,0:T(8,128)(2,1)}) custom-call(f32[8,6,2048]{2,1,0:T(8,128)} %copy.25.refs_0_, bf16[8,256,768]{2,1,0:T(8,128)(2,1)} %copy.26.refs_1_), custom_call_target="tpu_custom_call" | custom-call | tf_op jit(solution)/shard_map/plane_exchange/pallas_call | solution.py:510
  92.8 2.5 fusion.4
  96.5 5.1 all-to-all-start
  101.6 7.3 convert.9
  109.0 2.5 fusion.17
  111.4 2.5 copy.36
  113.9 13.9 %all-to-all-done = bf16[4,64,2048]{2,1,0:T(8,128)(2,1)S(1)} async-done(((bf16[4,64,2048]{2,1,0:T(8,128)(2,1)}), bf16[4,64,2048]{2,1,0:T(8,128)(2,1)S(1)}, u32[]{:S(2)}, u32[]{:S(2)}) %all-to-all-start) | async-done | bytes 1048608 | tf_op jit(solution)/shard_map/all_to_all | solution.py:1500
  127.8 4.6 all-to-all-start.2
  132.4 5.0 copy.35
  137.4 58.2 %all-to-all-done.2 = bf16[8,256,1024]{2,1,0:T(8,128)(2,1)} async-done(((bf16[8,256,1024]{2,1,0:T(8,128)(2,1)}), bf16[8,256,1024]{2,1,0:T(8,128)(2,1)}, u32[]{:S(2)}, u32[]{:S(2)}) %all-to-all-start.2) | async-done | bytes 4194336 | tf_op jit(solution)/shard_map/all_to_all | solution.py:1539
  195.6 4.9 all-to-all-start.3
  200.5 2.3 slice.52.out_weight_ref.out_weight
  204.0 1.4 fusion.2.block_ref
  205.4 79.7 %plane_gather.2.h_ref.h_all = bf16[8,256,2048]{2,1,0:T(8,128)(2,1)} custom-call(bf16[256,2048]{1,0:T(8,128)(2,1)} %fusion.2.block_ref), custom_call_target="tpu_custom_call" | custom-call | tf_op jit(solution)/shard_map/plane_gather/pallas_call | solution.py:346
  285.1 22.2 %attention_forward.1 = (bf16[8,256,768]{2,1,0:T(8,128)(2,1)}, bf16[8,256,256]{2,1,0:T(8,128)(2,1)}, bf16[8,256,2048]{2,1,0:T(8,128)(2,1)}) custom-call(bf16[8,256,2048]{2,1,0:T(8,128)(2,1)} %plane_gather.2.h_ref.h_all, bf16[2048,768]{1,0:T(8,128)(2,1)} %bitcast.66, bf16[256,2048]{1,0:T(8,128)(2,1)} %slice.52.out_weight_ref.out_weight), custom_call_target="tpu_custom_call" | custom-call | tf_op jit(solution)/shard_map/attention_forward/pallas_call | solution.py:558
  307.3 41.7 %plane_scatter.1.attn_out = f32[256,2048]{1,0:T(8,128)} custom-call(bf16[8,256,2048]{2,1,0:T(8,128)(2,1)} %get-tuple-element.22.part_ref), custom_call_target="tpu_custom_call" | custom-call | tf_op jit(solution)/shard_map/plane_scatter/pallas_call | solution.py:459
  349.0 2.0 multiply_reduce_fusion
  353.7 39.7 %plane_gather.3.h_ref = bf16[8,256,2048]{2,1,0:T(8,128)(2,1)} custom-call(bf16[256,2048]{1,0:T(8,128)(2,1)} %add_convert_fusion.block_ref), custom_call_target="tpu_custom_call" | custom-call | tf_op jit(solution)/shard_map/plane_gather/pallas_call | solution.py:346
  393.4 41.7 %feed_both.1 = (bf16[8,256,1024]{2,1,0:T(8,128)(2,1)}, bf16[8,256,1024]{2,1,0:T(8,128)(2,1)}, bf16[8,256,2048]{2,1,0:T(8,128)(2,1)}, bf16[8,256,2048]{2,1,0:T(8,128)(2,1)}) custom-call(bf16[8,256,2048]{2,1,0:T(8,128)(2,1)} %plane_gather.3.h_ref, bf16[8,256,2048]{2,1,0:T(8,128)(2,1)} %all-gather.3.cloned.1.call-done.grad_ref, ...), custom_call_target="tpu_custom_call" | custom-call | tf_op jit(solution)/shard_map/feed_both/pallas_call | solution.py:654
  435.0 27.3 %early_grads.1.early = bf16[8,8,256,256]{3,2,1,0:T(8,128)(2,1)} custom-call(bf16[2048,2048]{1,0:T(8,128)(2,1)} %bitcast.58, bf16[2048,2048]{1,0:T(8,128)(2,1)} %bitcast.57, bf16[2048,1024]{1,0:T(8,128)(2,1)} %bitcast.74, bf16[2048,1024]{1,0:T(8,128)(2,1)} %bitcast.75), custom_call_target="tpu_custom_call" | custom-call | tf_op jit(solution)/shard_map/early_grads/pallas_call | solution.py:1427
  462.3 418.7 %back_part.1 = (bf16[12,8,256,256]{3,2,1,0:T(8,128)(2,1)}, bf16[4,64,2048]{2,1,0:T(8,128)(2,1)}, bf16[4,64,2048]{2,1,0:T(8,128)(2,1)}, f32[8,4,8,2048]{3,2,1,0:T...) custom-call(bf16[8,256,2048]{2,1,0:T(8,128)(2,1)} %get-tuple-element, ...), custom_call_target="tpu_custom_call" | custom-call | tf_op jit(solution)/shard_map/back_part/pallas_call | solution.py:1332
  881.0 13.5 %mlp_spread.1 = f32[256,16384]{1,0:T(8,128)} custom-call(bf16[12,8,256,256]{3,2,1,0:T(8,128)(2,1)} %get-tuple-element.31.share_ref), custom_call_target="tpu_custom_call" | custom-call | tf_op jit(solution)/shard_map/mlp_spread/pallas_call | solution.py:1451
  894.5 6.1 attn_spread.1
  901.8 13.9 %fusion.19 = f32[32,256]{1,0:T(8,128)S(1)} fusion(f32[32,12288]{1,0:T(8,128)S(1)} %bitcast.64, f32[256,12288]{1,0:T(8,128)} %param.16), kind=kOutput, calls=%fused_computation.37 | convolution fusion | flops 1207959552 | bytes 14188544 | tf_op jit(solution)/shard_map/dot_general | solution.py:1595
  915.7 12.4 %fusion.20 = f32[256,12288]{1,0:T(8,128)} fusion(f32[32,256]{1,0:T(8,128)S(1)} %fusion.8, f32[32,12288]{1,0:T(8,128)S(1)} %bitcast.65), kind=kOutput, calls=%fused_computation.38 | convolution fusion | flops 1207959552 | bytes 14188544 | tf_op jit(solution)/shard_map/dot_general | solution.py:1592
  929.8 1.6 convert_element_type.62
  (48 shorter events, 17.1 us)
Async XLA Ops:
  7.2 85.6 %all-to-all-start.1 = ((bf16[4,64,2048]{2,1,0:T(8,128)(2,1)}), bf16[4,64,2048]{2,1,0:T(8,128)(2,1)}, u32[]{:S(2)}, u32[]{:S(2)}) async-start(bf16[4,64,2048]{2,1,0:T(8,128)(2,1)} %param.10), calls=%async_computation.1 | async-start | bytes 2097152 | tf_op jit(solution)/shard_map/all_to_all | solution.py:1500
  13.5 379.9 %all-gather.3.cloned.1.call-start = ((), (), s32[]{:S(2)}) async-start(), calls=%async_computation.4 | async-start | bytes 9437184 | tf_op jit(solution)/shard_map/all_gather | solution.py:1546
  26.5 10.1 %copy-start.3 = (f32[256,8192]{1,0:T(8,128)S(1)}, f32[256,8192]{1,0:T(8,128)}, u32[]{:S(2)}) copy-start(f32[256,8192]{1,0:T(8,128)} %param.13) | copy-start | bytes 25165828
  37.1 2.0 copy-start.2
  96.5 31.3 %all-to-all-start = ((bf16[4,64,2048]{2,1,0:T(8,128)(2,1)}), bf16[4,64,2048]{2,1,0:T(8,128)(2,1)S(1)}, u32[]{:S(2)}, u32[]{:S(2)}) async-start(bf16[4,64,2048]{2,1,0:T(8,128)(2,1)} %param.9), calls=%async_computation | async-start | bytes 2097152 | tf_op jit(solution)/shard_map/all_to_all | solution.py:1500
  127.8 221.2 %copy-start = (bf16[4,64,2048]{2,1,0:T(8,128)(2,1)}, bf16[4,64,2048]{2,1,0:T(8,128)(2,1)S(1)}, u32[]{:S(2)}) copy-start(bf16[4,64,2048]{2,1,0:T(8,128)(2,1)S(1)} %all-to-all-done) | copy-start | bytes 3145732
  127.8 67.8 %all-to-all-start.2 = ((bf16[8,256,1024]{2,1,0:T(8,128)(2,1)}), bf16[8,256,1024]{2,1,0:T(8,128)(2,1)}, u32[]{:S(2)}, u32[]{:S(2)}) async-start(bf16[8,256,1024]{2,1,0:T(8,128)(2,1)} %bitcast.61), calls=%async_computation.2 | async-start | bytes 8388608 | tf_op jit(solution)/shard_map/all_to_all | solution.py:1539
  195.6 7.9 copy-start.7
  195.6 197.7 %all-to-all-start.3 = ((bf16[8,256,1024]{2,1,0:T(8,128)(2,1)}), bf16[8,256,1024]{2,1,0:T(8,128)(2,1)}, u32[]{:S(2)}, u32[]{:S(2)}) async-start(bf16[8,256,1024]{2,1,0:T(8,128)(2,1)} %bitcast.60), calls=%async_computation.3 | async-start | bytes 8388608 | tf_op jit(solution)/shard_map/all_to_all | solution.py:1539
  351.1 1.3 copy-start.1
  894.5 6.1 copy-start.4
  915.7 14.1 %copy-start.5 = (bf16[4,64,2048]{2,1,0:T(8,128)(2,1)S(1)}, bf16[4,64,2048]{2,1,0:T(8,128)(2,1)}, u32[]{:S(2)}) copy-start(bf16[4,64,2048]{2,1,0:T(8,128)(2,1)} %get-tuple-element.30) | copy-start | bytes 3145732
  928.2 3.2 copy-start.6
Sparse Core Ops, SparseCore 0:
  96.6 80.3 all-gather.2

commit v3 on v0

--- a/solution.py
+++ b/solution.py
@@ -1,6 +1,11 @@
+import functools
+import math
+
 import jax
 import jax.numpy as jnp
 from jax import lax
+from jax.experimental import pallas as pl
+from jax.experimental.pallas import tpu as pltpu
 from jax.sharding import PartitionSpec as P
 
 HD = 128
@@ -239,9 +244,1578 @@
     )
 
 
+MESH_ID = pl.DeviceIdType.MESH
+VMEM_BYTES = 56 * 1024 * 1024
+
+
+def contract(left, right, left_dim, right_dim):
+    return lax.dot_general(
+        left, right, (((left_dim,), (right_dim,)), ((), ())), preferred_element_type=jnp.float32
+    )
+
+
+def plane_places():
+    mine = lax.axis_index("fsdp")
+    plane = lax.axis_index("blk")
+    core = lax.rem(mine, 2)
+    col = lax.rem(mine // 2, 2)
+    row = mine // 4
+
+    def at(flip):
+        flip_row, flip_col, flip_core = flip // 4, (flip // 2) % 2, flip % 2
+        new_row = 1 - row if flip_row else row
+        new_col = 1 - col if flip_col else col
+        new_core = 1 - core if flip_core else core
+        return new_row * 4 + new_col * 2 + new_core
+
+    return mine, plane, at
+
+
+def greet(places):
+    barrier = pltpu.get_barrier_semaphore()
+    for place in places:
+        pl.semaphore_signal(barrier, inc=1, device_id=place, device_id_type=MESH_ID)
+    pl.semaphore_wait(barrier, len(places))
+
+
+def remote(src, dst, send_sem, recv_sem, place):
+    return pltpu.make_async_remote_copy(
+        src_ref=src,
+        dst_ref=dst,
+        send_sem=send_sem,
+        recv_sem=recv_sem,
+        device_id=place,
+        device_id_type=MESH_ID,
+    )
+
+
+PIECES = 4
+
+
+def softmax_rows(queries, key_rows):
+    scores = contract(queries, key_rows, 1, 1) * HD ** (-0.5)
+    exponent = jnp.exp(scores - jnp.max(scores, axis=-1, keepdims=True))
+    return exponent / jnp.sum(exponent, axis=-1, keepdims=True)
+
+
+def rms_scale(features):
+    return lax.rsqrt(jnp.mean(features * features, axis=-1, keepdims=True) + EPSILON)
+
+
+CHUNKS = 12
+FIRST = 4
+UP_TICK = 4
+LATE_TICK = 8
+EARLY = 8
+HALF_ROWS = 128
+BAND = 32
+
+
+def flipped(mine, flip):
+    total = 0
+    for bit in (1, 2, 4):
+        total = total + lax.rem(mine // bit + flip // bit, 2) * bit
+    return total
+
+
+def bands(count, step):
+    @pl.loop(0, count // BAND)
+    def _(index):
+        step(pl.ds(pl.multiple_of(index * BAND, BAND), BAND))
+
+
+def plain(ref, rows):
+    return ref[rows, :].astype(jnp.float32)
+
+
+def column_products(source, right, cols, staged, result, load_sems, store_sems):
+    rows = cols.shape[-1]
+    count = result.shape[0]
+
+    def load(block):
+        slot = lax.rem(block, 2)
+        return pltpu.make_async_copy(
+            source.at[:, :, pl.ds(pl.multiple_of(block * rows, rows), rows)],
+            cols.at[slot],
+            load_sems.at[slot],
+        )
+
+    def store(block):
+        slot = lax.rem(block, 2)
+        return pltpu.make_async_copy(
+            staged.at[slot, pl.ds(0, count)], result.at[:, block], store_sems.at[slot]
+        )
+
+    load(0).start()
+
+    @pl.loop(0, 8)
+    def _(block):
+        slot = lax.rem(block, 2)
+        load(block).wait()
+
+        @pl.when(block < 7)
+        def _():
+            load(block + 1).start()
+
+        @pl.when(block >= 2)
+        def _():
+            store(block - 2).wait()
+
+        product = contract(cols[slot].reshape(8 * rows, rows), right[...], 0, 0)
+        for number in range(count):
+            staged[slot, number] = product[:, number * rows : (number + 1) * rows].astype(
+                jnp.bfloat16
+            )
+        store(block).start()
+
+    store(6).wait()
+    store(7).wait()
+
+
+GELU_SCALE = (2.0 / math.pi) ** 0.5
+
+
+def gelu_and_slope(pre):
+    squared = pre * pre
+    bend = jnp.tanh(GELU_SCALE * (pre + 0.044715 * (squared * pre)))
+    rise = 0.5 * (1.0 + bend)
+    slope = rise + 0.5 * pre * (1.0 - bend * bend) * (GELU_SCALE * (1.0 + 3.0 * 0.044715 * squared))
+    return pre * rise, slope
+
+
+class Plane:
+    def __init__(self):
+        self.mine, self.place, self.at = plane_places()
+
+    def to(self, flip):
+        return (self.at(flip), self.place)
+
+    def got(self, ref, sem):
+        remote(ref, ref, sem, sem, (self.mine, self.place)).wait_recv()
+
+    def gone(self, ref, sem):
+        remote(ref, ref, sem, sem, (self.mine, self.place)).wait_send()
+
+
+def scatter_flow(plane, own_of, fetch, peer, far, near, sems, finish):
+    core_recv, far_send, far_recv, near_send, near_recv = sems
+    rows = near.shape[1]
+    half = rows // 2
+    sent = []
+
+    def add(slot, start, count, extra=None):
+        own = own_of(slot)
+
+        def step(band):
+            at = pl.ds(pl.multiple_of(start + band.start, BAND), BAND)
+            total = plain(own, at) + plain(peer.at[slot], at)
+            if extra is not None:
+                total = total + plain(extra, band)
+            peer[slot, at, :] = total.astype(jnp.bfloat16)
+
+        bands(count, step)
+
+    def send(src, dst, flip, send_sem, recv_sem):
+        copy = remote(src, dst, send_sem, recv_sem, plane.to(flip))
+        copy.start()
+        sent.append(copy)
+
+    def send_near(slot, part):
+        at = pl.ds(part * half, half)
+        index = (slot - 1) * 2 + part
+        send(
+            peer.at[slot, at],
+            near.at[slot - 1, at],
+            2 * slot,
+            near_send.at[index],
+            near_recv.at[index],
+        )
+
+    fetch(3)
+    plane.got(peer.at[3], core_recv.at[3])
+    add(3, 0, rows)
+    send(peer.at[3, pl.ds(0, half)], far.at[0], 2, far_send.at[0], far_recv.at[0])
+    send(peer.at[3, pl.ds(half, half)], far.at[1], 4, far_send.at[1], far_recv.at[1])
+    fetch(1)
+    plane.got(peer.at[1], core_recv.at[1])
+    add(1, 0, half)
+    send_near(1, 0)
+    fetch(2)
+    plane.got(peer.at[2], core_recv.at[2])
+    add(2, half, half)
+    send_near(2, 1)
+    yield
+    plane.got(far.at[0], far_recv.at[0])
+    add(2, 0, half, far.at[0])
+    send_near(2, 0)
+    plane.got(far.at[1], far_recv.at[1])
+    add(1, half, half, far.at[1])
+    send_near(1, 1)
+    fetch(0)
+    plane.got(peer.at[0], core_recv.at[0])
+    yield
+    for slot in (1, 2):
+        for part in (0, 1):
+            at = pl.ds(part * half, half)
+            plane.got(near.at[slot - 1, at], near_recv.at[(slot - 1) * 2 + part])
+    own = own_of(0)
+
+    def step(at):
+        finish(
+            at,
+            plain(own, at)
+            + plain(peer.at[0], at)
+            + plain(near.at[0], at)
+            + plain(near.at[1], at),
+        )
+
+    bands(rows, step)
+    for copy in sent:
+        copy.wait_send()
+
+
+def back_kernel(
+    down_low,
+    up_weight,
+    hidden_all,
+    slope_all,
+    grad_mlp_all,
+    h_two_all,
+    first_grads,
+    h_all,
+    qkv_all,
+    attended_all,
+    qkv_weight,
+    out_weight,
+    features,
+    first_sum,
+    attn_out,
+    grad_out,
+    mod,
+    shares,
+    token_out,
+    token_grad,
+    mod_out,
+    more,
+    partial_out,
+    land_a,
+    land_b,
+    first_buf,
+    second_buf,
+    stage,
+    own_pair,
+    grad_all,
+    grad_first,
+    saved_grad,
+    cols_buf,
+    qkv_buf,
+    attended_buf,
+    staged_buf,
+    out_sum,
+    sum_buf,
+    in_buf,
+    half_buf,
+    half_in,
+    mod_sum,
+    mod_land,
+    core_send,
+    core_recv,
+    far_send,
+    far_recv,
+    near_send,
+    near_recv,
+    stage_sems,
+    gather_send,
+    gather_recv,
+    load_sems,
+    weight_sems,
+    z_sems,
+    x_sems,
+    zload_sems,
+    token_sems,
+    mod_sems,
+    mod_gather_sems,
+):
+    plane = Plane()
+    mine, place = plane.mine, plane.place
+    rows, width = features.shape
+    at = plane.at
+    own_grad, image_out = own_pair.at[0], own_pair.at[1]
+    is_mid = (place == 1) | (place == 2)
+    my_half = pl.ds(pl.multiple_of(jnp.where(place == 2, HALF_ROWS, 0), HALF_ROWS), HALF_ROWS)
+    other_half = pl.ds(pl.multiple_of(jnp.where(place == 2, 0, HALF_ROWS), HALF_ROWS), HALF_ROWS)
+    partner = (mine, 3 - place)
+    outer = (mine, jnp.where(place == 1, 0, 3))
+    inner = (mine, jnp.where(place == 0, 1, 2))
+    others = [lax.rem(place + step, 4) for step in (1, 2, 3)]
+    greet([plane.to(flip) for flip in range(1, 8)] + [(mine, other) for other in others])
+
+    def z_copy(kind, chunk, src, dst, target):
+        return remote(src, dst, z_sems.at[0, kind, chunk], z_sems.at[1, kind, chunk], target)
+
+    def own_chunk(chunk):
+        return first_grads.at[chunk] if chunk < FIRST else more.at[chunk - FIRST]
+
+    def start_outward(chunk):
+        z_copy(0, chunk, own_chunk(chunk), land_a.at[chunk], inner).start()
+
+    def stage_d(k):
+        region = shares.at[k, :, other_half]
+        plane.got(region, z_sems.at[1, 2, k])
+        z_copy(4, k, region, region, outer).start()
+
+    def stage_x(k):
+        region = shares.at[k, :, my_half]
+        plane.got(region, x_sems.at[1, k])
+        z_copy(2, k, region, region, partner).start()
+        z_copy(3, k, region, region, outer).start()
+
+    def stage_f(k):
+        slot = k % 2
+        load = pltpu.make_async_copy(land_b.at[k], half_in, zload_sems.at[2])
+        plane.got(land_b.at[k], z_sems.at[1, 1, k])
+        load.start()
+        if k >= 2:
+            plane.gone(half_buf.at[slot, pl.ds(0, 7)], x_sems.at[0, k - 2])
+        load.wait()
+
+        @pl.loop(0, 8)
+        def _(block):
+            half_buf[slot, block] = (
+                sum_buf[slot, block, my_half, :].astype(jnp.float32)
+                + half_in[block].astype(jnp.float32)
+            ).astype(jnp.bfloat16)
+
+        if k == CHUNKS - 1:
+            pltpu.make_async_copy(
+                half_buf.at[slot], shares.at[k, :, my_half], x_sems.at[1, k]
+            ).start()
+            return
+        pltpu.make_async_copy(
+            half_buf.at[slot, mine], shares.at[k, mine, my_half], x_sems.at[1, k]
+        ).start()
+        for flip in (6, 7, 2, 4, 3, 5, 1):
+            remote(
+                half_buf.at[slot, at(flip)],
+                shares.at[k, mine, my_half],
+                x_sems.at[0, k],
+                x_sems.at[1, k],
+                plane.to(flip),
+            ).start()
+
+    def stage_s(k):
+        slot = k % 2
+        if k >= 2:
+            plane.gone(sum_buf.at[slot, :, other_half], z_sems.at[0, 1, k - 2])
+        own_load = pltpu.make_async_copy(own_chunk(k), sum_buf.at[slot], zload_sems.at[0])
+        own_load.start()
+        in_load = pltpu.make_async_copy(land_a.at[k], in_buf, zload_sems.at[1])
+        plane.got(land_a.at[k], z_sems.at[1, 0, k])
+        in_load.start()
+        own_load.wait()
+        in_load.wait()
+
+        @pl.loop(0, 8)
+        def _(block):
+            sum_buf[slot, block] = (
+                sum_buf[slot, block].astype(jnp.float32) + in_buf[block].astype(jnp.float32)
+            ).astype(jnp.bfloat16)
+
+        z_copy(1, k, sum_buf.at[slot, :, other_half], land_b.at[k], partner).start()
+
+    def start_tick(chunk):
+        return LATE_TICK if chunk >= EARLY else (UP_TICK if chunk >= FIRST else -1)
+
+    def tick(now):
+        @pl.when(jnp.logical_not(is_mid))
+        def _():
+            for chunk in range(CHUNKS):
+                if start_tick(chunk) == now:
+                    start_outward(chunk)
+
+        @pl.when(is_mid)
+        def _():
+            if 0 <= now - 3 < CHUNKS:
+                stage_d(now - 3)
+            if 0 <= now - 2 < CHUNKS:
+                stage_x(now - 2)
+            if 0 <= now - 1 < CHUNKS:
+                stage_f(now - 1)
+            if now < CHUNKS:
+                stage_s(now)
+
+    @pl.when(jnp.logical_not(is_mid))
+    def _():
+        for chunk in range(CHUNKS):
+            if start_tick(chunk) < 0:
+                start_outward(chunk)
+
+    attended_load = pltpu.make_async_copy(attended_all, attended_buf, load_sems.at[0])
+    attended_load.start()
+    feed = up_weight.shape[-1]
+    down_part, up_part = pl.ds(0, feed), pl.ds(feed, feed)
+
+    pltpu.make_async_copy(
+        down_low.at[mine], grad_all.at[mine, :, down_part], weight_sems.at[0, 0]
+    ).start()
+    for flip in (6, 7, 2, 4, 3, 5, 1):
+        remote(
+            down_low.at[at(flip)],
+            grad_all.at[mine, :, down_part],
+            weight_sems.at[0, flip],
+            weight_sems.at[1, flip],
+            plane.to(flip),
+        ).start()
+    up_load = pltpu.make_async_copy(up_weight, grad_all.at[:, :, up_part], load_sems.at[5])
+    up_load.start()
+    mod_sum[...] = jnp.zeros_like(mod_sum)
+    row = {
+        name: number
+        for number, name in enumerate(
+            ("shift_one", "scale_one", "gate_one", "shift_two", "scale_two", "gate_two", "live")
+        )
+    }
+
+    def mod_row(name):
+        return mod[pl.ds(row[name], 1), :]
+
+    def accumulate(name, value):
+        mod_sum[pl.ds(row[name], 1), :] += jnp.sum(value, axis=0, keepdims=True)
+
+    def sems(number):
+        return (
+            core_recv.at[number],
+            far_send.at[number],
+            far_recv.at[number],
+            near_send.at[number],
+            near_recv.at[number],
+        )
+
+    def give(src, buf, number, slot):
+        remote(
+            src, buf.at[slot], core_send.at[number, slot], core_recv.at[number, slot], plane.to(1)
+        ).start()
+
+    def staged_flow(source, buf, number, finish):
+        for slot in (3, 1, 2, 0):
+            give(source.at[at((2 * slot) ^ 1)], buf, number, slot)
+        order = {3: 0, 1: 1, 2: 0, 0: 1}
+
+        def load(slot):
+            return pltpu.make_async_copy(
+                source.at[at(2 * slot)], stage.at[order[slot]], stage_sems.at[number, slot]
+            )
+
+        load(3).start()
+        load(1).start()
+
+        def fetch(slot):
+            if slot == 2:
+                load(2).start()
+            if slot == 0:
+                load(0).start()
+            load(slot).wait()
+
+        return scatter_flow(
+            plane,
+            lambda slot: stage.at[order[slot]],
+            fetch,
+            buf.at[pl.ds(0, 4)],
+            Halves(buf.at[6], rows // 2),
+            buf.at[pl.ds(4, 2)],
+            sems(number),
+            finish,
+        )
+
+    def run(flow, first_tick):
+        for step, _ in enumerate(flow):
+            tick(first_tick + step)
+
+    def finish_out(where, value):
+        base = first_sum[where, :]
+        own_pair[1, where, :] = (
+            mod_row("live") * (base + mod_row("gate_two") * value)
+        ).astype(jnp.bfloat16)
+        accumulate("gate_two", plain(grad_out, where) * value)
+
+    token_copies = []
+
+    def return_tokens(image, result, number):
+        piece = rows // 4
+        own = pltpu.make_async_copy(
+            image.at[pl.ds(pl.multiple_of(place * piece, piece), piece)],
+            result.at[place],
+            token_sems.at[0, number, 0],
+        )
+        own.start()
+        token_copies.append(own)
+        for step, other in enumerate(others):
+            copy = remote(
+                image.at[pl.ds(pl.multiple_of(other * piece, piece), piece)],
+                result.at[place],
+                token_sems.at[0, number, step + 1],
+                token_sems.at[1, number, step + 1],
+                (mine, other),
+            )
+            copy.start()
+            token_copies.append(copy)
+
+
+    def back_norm(source, value, scale_name, shift_name):
+        inverse = rms_scale(source)
+        unit = source * inverse
+        inner = value * (1.0 + mod_row(scale_name))
+        accumulate(scale_name, value * unit)
+        accumulate(shift_name, value)
+        return (inner - unit * jnp.mean(inner * unit, axis=-1, keepdims=True)) * inverse
+
+    def finish_feed(where, value):
+        total = back_norm(first_sum[where, :], value, "scale_two", "shift_two") + plain(
+            grad_out, where
+        )
+        grad_first[where, :] = total
+        accumulate("gate_one", total * plain(attn_out, where))
+        low_grad = (mod_row("gate_one") * total).astype(jnp.bfloat16)
+        own_pair[0, where, :] = low_grad
+        grad_all[mine, where, :] = low_grad
+
+    up_load.wait()
+    pltpu.make_async_copy(
+        down_low.at[mine], grad_all.at[mine, :, down_part], weight_sems.at[0, 0]
+    ).wait()
+    tick(0)
+    tick(1)
+    for flip in range(1, 8):
+        plane.got(grad_all.at[at(flip), :, down_part], weight_sems.at[1, flip])
+        plane.gone(down_low.at[0], weight_sems.at[0, flip])
+
+    def image_loads(step):
+        image = flipped(mine, step)
+        return [
+            pltpu.make_async_copy(
+                hidden_all.at[image], stage.at[0, :, pl.ds(0, feed)], load_sems.at[6]
+            ),
+            pltpu.make_async_copy(
+                slope_all.at[image], stage.at[0, :, pl.ds(feed, feed)], load_sems.at[7]
+            ),
+            pltpu.make_async_copy(grad_mlp_all.at[image], stage.at[1], load_sems.at[8]),
+        ]
+
+    def out_store(step):
+        return pltpu.make_async_copy(
+            own_pair.at[lax.rem(step, 2)],
+            partial_out.at[flipped(mine, step)],
+            load_sems.at[9 + lax.rem(step, 2)],
+        )
+
+    for load in image_loads(0):
+        load.start()
+
+    @pl.loop(0, 8)
+    def _(step):
+        for load in image_loads(step):
+            load.wait()
+        image = flipped(mine, step)
+        image_rows = pl.ds(pl.multiple_of(image * rows, rows), rows)
+
+        @pl.when(step >= 2)
+        def _():
+            out_store(step - 2).wait()
+
+        down = grad_all[:, :, 0:feed].reshape(8 * rows, feed)
+        grad_hidden = contract(stage[1], down, 1, 0)
+        saved_grad[image_rows, :] = (
+            grad_hidden * stage[0, :, feed : 2 * feed].astype(jnp.float32)
+        ).astype(jnp.bfloat16)
+        own_pair[lax.rem(step, 2)] = contract(stage[0, :, 0:feed], down, 1, 1).astype(jnp.bfloat16)
+        out_store(step).start()
+
+        @pl.when(step < 7)
+        def _():
+            for load in image_loads(step + 1):
+                load.start()
+
+        up = grad_all[:, :, feed : 2 * feed].reshape(8 * rows, feed)
+        second_buf[step] = contract(saved_grad[image_rows, :], up, 1, 1).astype(jnp.bfloat16)
+        for number in (1, 3, 5, 7):
+
+            @pl.when(step == number)
+            def _(number=number):
+                give(second_buf.at[number], first_buf, 1, number // 2)
+
+        @pl.when(step == 3)
+        def _():
+            tick(2)
+
+    out_store(6).wait()
+    out_store(7).wait()
+    tick(3)
+    column_products(
+        h_two_all,
+        saved_grad,
+        cols_buf,
+        staged_buf,
+        more.at[pl.ds(0, 4)],
+        load_sems.at[pl.ds(3, 2)],
+        load_sems.at[pl.ds(11, 2)],
+    )
+
+    def own_flow(number, finish):
+        return scatter_flow(
+            plane,
+            lambda slot: second_buf.at[2 * slot],
+            lambda slot: None,
+            first_buf.at[pl.ds(0, 4)],
+            Halves(first_buf.at[6], rows // 2),
+            first_buf.at[pl.ds(4, 2)],
+            sems(number),
+            finish,
+        )
+
+    run(own_flow(1, finish_feed), 4)
+    for slot in range(4):
+        plane.gone(second_buf.at[slot], core_send.at[1, slot])
+
+    gather = Gather(plane, own_grad, grad_all, gather_send, gather_recv)
+    gather.start()
+
+    def qkv_load(step):
+        return pltpu.make_async_copy(
+            qkv_all.at[flipped(mine, step)], qkv_buf.at[lax.rem(step, 2)], load_sems.at[1 + lax.rem(step, 2)]
+        )
+
+    qkv_load(0).start()
+    attended_load.wait()
+    out_sum[...] = jnp.zeros_like(out_sum)
+    columns = qkv_buf.shape[-1]
+    third = columns // 3
+    scale = HD ** (-0.5)
+
+    @pl.loop(0, 8)
+    def _(step):
+        for number in range(8):
+
+            @pl.when(step == number)
+            def _(number=number):
+                gather.step(number)
+                if number == 7:
+                    gather.finish()
+
+        image = flipped(mine, step)
+        slot = lax.rem(step, 2)
+        qkv_load(step).wait()
+
+        @pl.when(step < 7)
+        def _():
+            qkv_load(step + 1).start()
+
+        grad = grad_all[image]
+        grad_attended = contract(grad, out_weight[...], 1, 1).astype(jnp.bfloat16)
+        image_rows = pl.ds(pl.multiple_of(image * rows, rows), rows)
+        for head in range(third // HD):
+            begin = head * HD
+            queries = qkv_buf[slot, :, begin : begin + HD]
+            key_rows = qkv_buf[slot, :, third + begin : third + begin + HD]
+            value_rows = qkv_buf[slot, :, 2 * third + begin : 2 * third + begin + HD]
+            grad_head = grad_attended[:, begin : begin + HD]
+            attention = softmax_rows(queries, key_rows)
+            grad_weights = contract(grad_head, value_rows, 1, 1)
+            row_delta = jnp.sum(attention * grad_weights, axis=-1, keepdims=True)
+            grad_scores = (attention * (grad_weights - row_delta)).astype(jnp.bfloat16)
+            saved_grad[image_rows, begin : begin + HD] = (
+                contract(grad_scores, key_rows, 1, 0) * scale
+            ).astype(jnp.bfloat16)
+            saved_grad[image_rows, third + begin : third + begin + HD] = (
+                contract(grad_scores, queries, 0, 0) * scale
+            ).astype(jnp.bfloat16)
+            saved_grad[image_rows, 2 * third + begin : 2 * third + begin + HD] = contract(
+                attention.astype(jnp.bfloat16), grad_head, 0, 0
+            ).astype(jnp.bfloat16)
+        out_sum[...] += contract(attended_buf[image], grad, 0, 0)
+        second_buf[step] = contract(saved_grad[image_rows, 0:columns], qkv_weight[...], 1, 1).astype(
+            jnp.bfloat16
+        )
+        for number in (1, 3, 5, 7):
+
+            @pl.when(step == number)
+            def _(number=number):
+                give(second_buf.at[number], first_buf, 2, number // 2)
+
+        for number, now in ((2, 6), (5, 7)):
+
+            @pl.when(step == number)
+            def _(now=now):
+                tick(now)
+
+    for block in range(8):
+        staged_buf[0, 0] = out_sum[:, block * rows : (block + 1) * rows].astype(jnp.bfloat16)
+        pltpu.sync_copy(staged_buf.at[0, 0], more.at[7, block])
+    column_products(
+        h_all,
+        saved_grad.at[:, pl.ds(0, columns)],
+        cols_buf,
+        staged_buf,
+        more.at[pl.ds(4, 3)],
+        load_sems.at[pl.ds(3, 2)],
+        load_sems.at[pl.ds(11, 2)],
+    )
+
+    def finish_input(where, value):
+        total = back_norm(plain(features, where), value, "scale_one", "shift_one")
+        own_pair[0, where, :] = (total + grad_first[where, :]).astype(jnp.bfloat16)
+
+    run(own_flow(2, finish_input), 8)
+    return_tokens(own_grad, token_grad, 1)
+    run(staged_flow(partial_out, grad_all, 0, finish_out), 10)
+    return_tokens(image_out, token_out, 0)
+
+    mod_copies = []
+    mod_sum[7:8, :] = mod[7:8, :]
+    mod_rows = pl.ds(pl.multiple_of(place * 8, 8), 8)
+    mod_land[mod_rows, :] = mod_sum[...]
+    for step, other in enumerate(others):
+        copy = remote(
+            mod_sum, mod_land.at[mod_rows], mod_sems.at[0, step], mod_sems.at[1, step], (mine, other)
+        )
+        copy.start()
+        mod_copies.append(copy)
+    tick(12)
+    for copy in mod_copies:
+        copy.wait_recv()
+    own = pltpu.make_async_copy(mod_land, mod_out.at[mine], mod_sems.at[0, 3])
+    own.start()
+    mod_gather = Gather(plane, mod_land, mod_out, mod_gather_sems.at[0], mod_gather_sems.at[1])
+    mod_gather.start()
+    tick(13)
+    mod_gather.middle()
+    mod_gather.far()
+    for flip in (1, 3, 5, 7):
+        mod_gather.crossed(flip)
+    mod_gather.finish()
+    tick(14)
+    own.wait()
+    for copy in mod_copies:
+        copy.wait_send()
+    for copy in token_copies:
+        copy.wait()
+    for number in (0, 2):
+        for slot in range(4):
+            plane.gone(second_buf.at[slot], core_send.at[number, slot])
+
+    @pl.when(is_mid)
+    def _():
+        for k in (CHUNKS - 2, CHUNKS - 1):
+            plane.gone(sum_buf.at[k % 2, :, other_half], z_sems.at[0, 1, k])
+        plane.gone(half_buf.at[0, pl.ds(0, 7)], x_sems.at[0, CHUNKS - 2])
+        for k in range(CHUNKS):
+            plane.gone(shares.at[k, :, my_half], z_sems.at[0, 2, k])
+            plane.gone(shares.at[k, :, my_half], z_sems.at[0, 3, k])
+            plane.gone(shares.at[k, :, other_half], z_sems.at[0, 4, k])
+
+    @pl.when(jnp.logical_not(is_mid))
+    def _():
+        first = pl.ds(pl.multiple_of(jnp.where(place == 0, 0, HALF_ROWS), HALF_ROWS), HALF_ROWS)
+        second = pl.ds(pl.multiple_of(jnp.where(place == 0, HALF_ROWS, 0), HALF_ROWS), HALF_ROWS)
+        for k in range(CHUNKS):
+            plane.gone(land_a.at[k], z_sems.at[0, 0, k])
+            plane.got(shares.at[k, :, first], z_sems.at[1, 3, k])
+            plane.got(shares.at[k, :, second], z_sems.at[1, 4, k])
+
+
+def back_part(*operands):
+    h_all, qkv_weight = operands[7], operands[10]
+    _, rows, width = h_all.shape
+    columns = qkv_weight.shape[1]
+    feed = operands[1].shape[-1]
+    low, full = jnp.bfloat16, jnp.float32
+    dma = pltpu.SemaphoreType.DMA
+    anywhere, inside = pl.BlockSpec(memory_space=pl.ANY), pl.BlockSpec(memory_space=pltpu.VMEM)
+    return pl.pallas_call(
+        back_kernel,
+        out_shape=[
+            jax.ShapeDtypeStruct((CHUNKS, 8, rows, rows), low),
+            jax.ShapeDtypeStruct((4, rows // 4, width), low),
+            jax.ShapeDtypeStruct((4, rows // 4, width), low),
+            jax.ShapeDtypeStruct((8, 32, width), full),
+            jax.ShapeDtypeStruct((CHUNKS - FIRST, 8, rows, rows), low),
+            jax.ShapeDtypeStruct((8, rows, width), low),
+            jax.ShapeDtypeStruct((CHUNKS, 8, rows, rows), low),
+            jax.ShapeDtypeStruct((CHUNKS, 8, HALF_ROWS, rows), low),
+        ],
+        in_specs=[anywhere] * 10 + [inside] * 7,
+        out_specs=[anywhere] * 8,
+        scratch_shapes=[
+            pltpu.VMEM((7, rows, width), low),
+            pltpu.VMEM((8, rows, width), low),
+            pltpu.VMEM((2, rows, width), low),
+            pltpu.VMEM((2, rows, width), low),
+            pltpu.VMEM((8, rows, width), low),
+            pltpu.VMEM((rows, width), full),
+            pltpu.VMEM((8 * rows, feed), low),
+            pltpu.VMEM((2, 8, rows, rows), low),
+            pltpu.VMEM((2, rows, columns), low),
+            pltpu.VMEM((8, rows, columns // 3), low),
+            pltpu.VMEM((2, 4, rows, rows), low),
+            pltpu.VMEM((columns // 3, width), full),
+            pltpu.VMEM((2, 8, rows, rows), low),
+            pltpu.VMEM((8, rows, rows), low),
+            pltpu.VMEM((2, 8, HALF_ROWS, rows), low),
+            pltpu.VMEM((8, HALF_ROWS, rows), low),
+            pltpu.VMEM((8, width), full),
+            pltpu.VMEM((32, width), full),
+            dma((3, 4)),
+            dma((3, 4)),
+            dma((3, 2)),
+            dma((3, 2)),
+            dma((3, 4)),
+            dma((3, 4)),
+            dma((2, 4)),
+            dma((7 * PIECES,)),
+            dma((7 * PIECES,)),
+            dma((13,)),
+            dma((2, 8)),
+            dma((2, 5, CHUNKS)),
+            dma((2, CHUNKS)),
+            dma((3,)),
+            dma((2, 2, 4)),
+            dma((2, 4)),
+            dma((2, 7 * PIECES)),
+        ],
+        compiler_params=pltpu.CompilerParams(
+            collective_id=4, has_side_effects=True, vmem_limit_bytes=63 * 1024 * 1024
+        ),
+        name="back_part",
+    )(*operands)
+
+
+def mlp_spread_kernel(share_ref, out_ref):
+    size = share_ref.shape[-1]
+    for number in range(4):
+        out_ref[:, number * size : (number + 1) * size] = share_ref[number, 0].astype(jnp.float32)
+
+
+def mlp_spread(shares):
+    rows = shares.shape[2]
+    return pl.pallas_call(
+        mlp_spread_kernel,
+        grid=(2, 8),
+        out_shape=jax.ShapeDtypeStruct((rows, 64 * rows), jnp.float32),
+        in_specs=[pl.BlockSpec((4, 1, rows, rows), lambda part, block: (1 - part, block, 0, 0))],
+        out_specs=pl.BlockSpec((rows, 4 * rows), lambda part, block: (0, part * 8 + block)),
+        compiler_params=pltpu.CompilerParams(vmem_limit_bytes=VMEM_BYTES),
+        name="mlp_spread",
+    )(shares)
+
+
+def attn_spread_kernel(share_ref, out_ref):
+    size = share_ref.shape[-1]
+    for number in range(8):
+        out_ref[:, number * size : (number + 1) * size] = share_ref[0, number].astype(jnp.float32)
+
+
+def attn_spread(shares):
+    rows = shares.shape[2]
+    return pl.pallas_call(
+        attn_spread_kernel,
+        grid=(4,),
+        out_shape=jax.ShapeDtypeStruct((rows, 32 * rows), jnp.float32),
+        in_specs=[pl.BlockSpec((1, 8, rows, rows), lambda part: (EARLY + part, 0, 0, 0))],
+        out_specs=pl.BlockSpec((rows, 8 * rows), lambda part: (0, part)),
+        compiler_params=pltpu.CompilerParams(vmem_limit_bytes=VMEM_BYTES),
+        name="attn_spread",
+    )(shares)
+
+
+class Gather:
+    def __init__(self, plane, own, result, send_sems, recv_sems):
+        self.plane, self.own, self.result = plane, own, result
+        self.send_sems, self.recv_sems = send_sems, recv_sems
+        self.piece = own.shape[0] // PIECES
+
+    def put(self, src, owner, part, flip, slot):
+        remote(
+            src,
+            self.result.at[owner, pl.ds(part * self.piece, self.piece)],
+            self.send_sems.at[slot],
+            self.recv_sems.at[slot],
+            self.plane.to(flip),
+        ).start()
+
+    def arrived(self, flip, part, slot):
+        ref = self.result.at[self.plane.at(flip), pl.ds(part * self.piece, self.piece)]
+        self.plane.got(ref, self.recv_sems.at[slot])
+        return ref
+
+    def start(self):
+        mine = self.plane.mine
+        for part in range(PIECES):
+            src = self.own.at[pl.ds(part * self.piece, self.piece)]
+            self.put(src, mine, part, 2, part)
+            self.put(src, mine, part, 4, PIECES + part)
+            self.put(src, mine, part, 1, 3 * PIECES + part)
+
+    def middle(self):
+        at = self.plane.at
+        for part in range(PIECES):
+            got = self.arrived(2, part, part)
+            if part < PIECES // 2:
+                self.put(got, at(2), part, 4, 2 * PIECES + part)
+            self.put(got, at(2), part, 1, 4 * PIECES + part)
+            got = self.arrived(4, part, PIECES + part)
+            if part >= PIECES // 2:
+                self.put(got, at(4), part, 2, 2 * PIECES + part)
+            self.put(got, at(4), part, 1, 5 * PIECES + part)
+
+    def far(self):
+        for part in range(PIECES):
+            got = self.arrived(6, part, 2 * PIECES + part)
+            self.put(got, self.plane.at(6), part, 1, 6 * PIECES + part)
+
+    def crossed(self, flip):
+        for part in range(PIECES):
+            self.arrived(flip, part, (3 + flip // 2) * PIECES + part)
+
+    def step(self, number):
+        if number == 2:
+            self.middle()
+        if number == 6:
+            self.far()
+        if number % 2:
+            self.crossed(number)
+
+    def finish(self):
+        for slot in range(7 * PIECES):
+            self.plane.gone(self.own.at[pl.ds(0, self.piece)], self.send_sems.at[slot])
+
+
+class Halves:
+    def __init__(self, ref, half):
+        self.ref, self.half = ref, half
+
+    @property
+    def at(self):
+        return self
+
+    def __getitem__(self, number):
+        return self.ref.at[pl.ds(number * self.half, self.half)]
+
+
+def front_kernel(
+    bin_ids,
+    image_counts,
+    noise,
+    mod_bias,
+    block_input,
+    cotangent,
+    attn_weight,
+    mlp_weight,
+    mod_weight,
+    qkv_weight,
+    out_weight,
+    up_weight,
+    down_low,
+    h_one_all,
+    h_two_all,
+    grad_mlp_all,
+    qkv_all,
+    attended_all,
+    hidden_all,
+    slope_all,
+    first_grads,
+    features,
+    first_sum,
+    attn_out,
+    grad_out,
+    mod,
+    load_buf,
+    qkv_stage,
+    up_stage,
+    weight_buf,
+    hidden_buf,
+    cols_buf,
+    staged_buf,
+    h_all,
+    qkv_buf,
+    attended_buf,
+    part_buf,
+    scatter_buf,
+    own_h,
+    own_grad,
+    own_next,
+    bin_row,
+    bin_land,
+    mod_part,
+    mod_land,
+    load_sems,
+    token_sems,
+    bin_sems,
+    mod_sems,
+    weight_sems,
+    gather_sems,
+    core_send,
+    core_recv,
+    far_send,
+    far_recv,
+    near_send,
+    near_recv,
+    copy_sems,
+):
+    plane = Plane()
+    mine, place, at = plane.mine, plane.place, plane.at
+    rows, width = own_h.shape
+    feed = up_stage.shape[-1]
+    columns = qkv_stage.shape[-1]
+    third = columns // 3
+    piece = rows // 4
+    others = [lax.rem(place + step, 4) for step in (1, 2, 3)]
+    flips = (6, 7, 2, 4, 3, 5, 1, 0)
+    greet([plane.to(flip) for flip in range(1, 8)] + [(mine, other) for other in others])
+
+    token_copies = []
+    my_rows = pl.ds(pl.multiple_of(place * piece, piece), piece)
+    for number, (source, result) in enumerate(((block_input, features), (cotangent, grad_out))):
+        copies = [
+            pltpu.make_async_copy(
+                source.at[place], result.at[my_rows], token_sems.at[0, number, 0]
+            )
+        ]
+        for step, other in enumerate(others):
+            copies.append(
+                remote(
+                    source.at[other],
+                    result.at[my_rows],
+                    token_sems.at[0, number, step + 1],
+                    token_sems.at[1, number, step + 1],
+                    (mine, other),
+                )
+            )
+        for copy in copies:
+            copy.start()
+        token_copies.append(copies)
+
+    lanes = lax.broadcasted_iota(jnp.int32, bin_row.shape, 1)
+    bin_row[...] = jnp.where(lanes == bin_ids[place], 1.0, 0.0).astype(jnp.float32)
+    bin_land[mine] = bin_row[...]
+    bin_copies = [
+        remote(
+            bin_row, bin_land.at[mine], bin_sems.at[0, flip], bin_sems.at[1, flip], plane.to(flip)
+        )
+        for flip in range(1, 8)
+    ]
+    for copy in bin_copies:
+        copy.start()
+
+    def load_columns(source, slot, begins, size):
+        return [
+            pltpu.make_async_copy(
+                source.at[:, pl.ds(begin, size)],
+                load_buf.at[slot, :, pl.ds(number * size, size)],
+                load_sems.at[slot, number],
+            )
+            for number, begin in enumerate(begins)
+        ]
+
+    def cast_and_send(source, begins_of, size, stage, result, kind):
+        loads = [load_columns(source, step % 2, begins_of(at(flip)), size) for step, flip in enumerate(flips)]
+        total = size * len(loads[0])
+        for load in loads[0]:
+            load.start()
+        for step, flip in enumerate(flips):
+            if step + 1 < len(flips):
+                for load in loads[step + 1]:
+                    load.start()
+            for load in loads[step]:
+                load.wait()
+
+            def cast(band, step=step):
+                stage[step, band, :] = load_buf[step % 2, band, :total].astype(jnp.bfloat16)
+
+            bands(rows, cast)
+            if flip:
+                remote(
+                    stage.at[step],
+                    result.at[mine],
+                    weight_sems.at[0, kind, flip],
+                    weight_sems.at[1, kind, flip],
+                    plane.to(flip),
+                ).start()
+            else:
+                pltpu.make_async_copy(
+                    stage.at[step], result.at[mine], weight_sems.at[0, kind, 0]
+                ).start()
+
+    def weights_arrived(result, kind):
+        for flip in range(1, 8):
+            plane.got(result.at[at(flip)], weight_sems.at[1, kind, flip])
+
+    def weights_gone(stage, result, kind):
+        pltpu.make_async_copy(stage.at[7], result.at[mine], weight_sems.at[0, kind, 0]).wait()
+        for flip in range(1, 8):
+            plane.gone(stage.at[0], weight_sems.at[0, kind, flip])
+
+    cast_and_send(
+        attn_weight,
+        lambda owner: [number * width + owner * third for number in range(3)],
+        third,
+        qkv_stage,
+        qkv_weight,
+        0,
+    )
+
+    for copy in bin_copies:
+        copy.wait_recv()
+    bins = noise.shape[0]
+    activated = noise[...] / (1.0 + jnp.exp(-noise[...]))
+    chosen = jnp.dot(
+        bin_land[:, 0, :bins], activated, precision=PRECISE, preferred_element_type=jnp.float32
+    )
+
+    def load_mod(number):
+        return pltpu.make_async_copy(
+            mod_weight.at[:, pl.ds(number * width, width)],
+            load_buf.at[number % 2],
+            load_sems.at[number % 2, 0],
+        )
+
+    load_mod(0).start()
+    mod_part[...] = jnp.zeros_like(mod_part)
+    for number in range(6):
+        if number < 5:
+            load_mod(number + 1).start()
+        load_mod(number).wait()
+        mod_part[:, number, :] = jnp.dot(
+            chosen, load_buf[number % 2], precision=PRECISE, preferred_element_type=jnp.float32
+        )
+    quarter = width // 4
+    for number in range(3):
+        index = 3 * mine + number
+        where = pl.ds(pl.multiple_of(lax.rem(index, 4) * quarter, quarter), quarter)
+        for image in range(8):
+            mod_part[image, pl.ds(index // 4, 1), where] += mod_bias[
+                :, number * quarter : (number + 1) * quarter
+            ]
+    mod_copies = [
+        remote(
+            mod_part.at[at(flip)],
+            mod_land.at[mine],
+            mod_sems.at[0, flip],
+            mod_sems.at[1, flip],
+            plane.to(flip),
+        )
+        for flip in range(1, 8)
+    ]
+    for copy in mod_copies:
+        copy.start()
+    mod_land[mine] = mod_part[mine]
+    for copy in mod_copies:
+        copy.wait_recv()
+    total = mod_land[0]
+    for number in range(1, 8):
+        total = total + mod_land[number]
+    mod[...] = total
+    live = jnp.where(place < image_counts[0], 1.0, 0.0).astype(jnp.float32)
+    mod[6:7, :] = jnp.full((1, width), 1.0, jnp.float32) * live
+    mod[7:8, :] = jnp.zeros((1, width), jnp.float32)
+    mod[7:8, :128] = bin_row[0:1, :]
+
+    def mod_row(number):
+        return mod[number : number + 1, :]
+
+    def tokens_arrived(number):
+        for copy in token_copies[number]:
+            if copy is token_copies[number][0]:
+                copy.wait()
+            else:
+                copy.wait_recv()
+
+    tokens_arrived(0)
+
+    def first_norm(band):
+        source = plain(features, band)
+        normed = (source * rms_scale(source) * (1.0 + mod_row(1)) + mod_row(0)).astype(jnp.bfloat16)
+        own_h[band, :] = normed
+        h_all[mine, band, :] = normed
+
+    bands(rows, first_norm)
+    h_gather = Gather(plane, own_h, h_all, gather_sems.at[0, 0], gather_sems.at[0, 1])
+    h_gather.start()
+    cast_and_send(
+        mlp_weight, lambda owner: [owner * feed], feed, up_stage, up_weight, 1
+    )
+
+    tokens_arrived(1)
+
+    def feed_grad(band):
+        scaled = plain(grad_out, band) * mod_row(6)
+        grad_out[band, :] = scaled.astype(jnp.bfloat16)
+        own_grad[band, :] = (mod_row(5) * scaled).astype(jnp.bfloat16)
+
+    bands(rows, feed_grad)
+    grad_own = pltpu.make_async_copy(own_grad, grad_mlp_all.at[mine], copy_sems.at[0])
+    grad_own.start()
+    grad_gather = Gather(plane, own_grad, grad_mlp_all, gather_sems.at[1, 0], gather_sems.at[1, 1])
+    grad_gather.start()
+    def down_load(owner):
+        return pltpu.make_async_copy(
+            mlp_weight.at[:, pl.ds((8 + owner) * feed, feed)],
+            load_buf.at[owner % 2, :, pl.ds(0, feed)],
+            load_sems.at[owner % 2, 0],
+        )
+
+    def down_store(owner):
+        return pltpu.make_async_copy(
+            part_buf.at[owner, :, pl.ds(0, feed)], down_low.at[owner], copy_sems.at[6 + owner]
+        )
+
+    down_load(0).start()
+    for owner in range(8):
+        if owner < 7:
+            down_load(owner + 1).start()
+        down_load(owner).wait()
+
+        def cast_down(band, owner=owner):
+            part_buf[owner, band, 0:feed] = load_buf[owner % 2, band, 0:feed].astype(jnp.bfloat16)
+
+        bands(rows, cast_down)
+        down_store(owner).start()
+    for owner in range(8):
+        down_store(owner).wait()
+    load = pltpu.make_async_copy(
+        attn_weight.at[:, pl.ds(3 * width, width)], load_buf.at[0], load_sems.at[0, 0]
+    )
+    load.start()
+    load.wait()
+
+    def cast_out(band):
+        out_weight[band, :] = load_buf[0, band, :].astype(jnp.bfloat16)
+
+    bands(rows, cast_out)
+
+    weights_arrived(qkv_weight, 0)
+    weights_gone(qkv_stage, qkv_weight, 0)
+    load = pltpu.make_async_copy(qkv_weight, weight_buf, copy_sems.at[1])
+    load.start()
+    load.wait()
+
+    @pl.loop(0, 8)
+    def _(step):
+        for number in range(8):
+
+            @pl.when(step == number)
+            def _(number=number):
+                h_gather.step(number)
+
+        image = flipped(mine, step)
+        pltpu.make_async_copy(h_all.at[image], h_one_all.at[image], copy_sems.at[2]).start()
+        projected = contract(
+            h_all[image], weight_buf[...].reshape(8 * rows, columns), 1, 0
+        ).astype(jnp.bfloat16)
+        qkv_buf[image] = projected
+        for head in range(third // HD):
+            begin = head * HD
+            queries = projected[:, begin : begin + HD]
+            key_rows = projected[:, third + begin : third + begin + HD]
+            value_rows = projected[:, 2 * third + begin : 2 * third + begin + HD]
+            attention = softmax_rows(queries, key_rows).astype(jnp.bfloat16)
+            attended_buf[image, :, begin : begin + HD] = contract(
+                attention, value_rows, 1, 0
+            ).astype(jnp.bfloat16)
+        part_buf[step] = contract(attended_buf[image], out_weight[...], 1, 0).astype(jnp.bfloat16)
+        pltpu.make_async_copy(h_all.at[image], h_one_all.at[image], copy_sems.at[2]).wait()
+
+        @pl.when(step == 7)
+        def _():
+            h_gather.finish()
+
+        for number in (1, 3, 5, 7):
+
+            @pl.when(step == number)
+            def _(number=number):
+                slot = number // 2
+                remote(
+                    part_buf.at[number],
+                    scatter_buf.at[slot],
+                    core_send.at[slot],
+                    core_recv.at[slot],
+                    plane.to(1),
+                ).start()
+
+    keeps = [
+        pltpu.make_async_copy(qkv_buf, qkv_all, copy_sems.at[3]),
+        pltpu.make_async_copy(attended_buf, attended_all, copy_sems.at[4]),
+    ]
+    for copy in keeps:
+        copy.start()
+
+    def second_norm(band, value):
+        attn_out[band, :] = value.astype(jnp.bfloat16)
+        source = plain(features, band) + mod_row(2) * value
+        first_sum[band, :] = source
+        normed = (source * rms_scale(source) * (1.0 + mod_row(4)) + mod_row(3)).astype(jnp.bfloat16)
+        own_next[band, :] = normed
+        h_all[mine, band, :] = normed
+
+    flow = scatter_flow(
+        plane,
+        lambda slot: part_buf.at[2 * slot],
+        lambda slot: None,
+        scatter_buf.at[pl.ds(0, 4)],
+        Halves(scatter_buf.at[6], rows // 2),
+        scatter_buf.at[pl.ds(4, 2)],
+        (core_recv, far_send, far_recv, near_send, near_recv),
+        second_norm,
+    )
+    for number, _ in enumerate(flow):
+        if number == 1:
+            grad_gather.middle()
+    for slot in range(4):
+        plane.gone(part_buf.at[slot], core_send.at[slot])
+    next_gather = Gather(plane, own_next, h_all, gather_sems.at[2, 0], gather_sems.at[2, 1])
+    next_gather.start()
+    grad_gather.far()
+    weights_arrived(up_weight, 1)
+    weights_gone(up_stage, up_weight, 1)
+    load = pltpu.make_async_copy(up_weight, up_stage, copy_sems.at[1])
+    load.start()
+    load.wait()
+
+    @pl.loop(0, 8)
+    def _(step):
+        for number in range(8):
+
+            @pl.when(step == number)
+            def _(number=number):
+                next_gather.step(number)
+
+        image = flipped(mine, step)
+        pre = contract(h_all[image], up_stage[...].reshape(8 * rows, feed), 1, 0)
+        hidden, slope = gelu_and_slope(pre)
+        hidden_buf[pl.ds(pl.multiple_of(image * rows, rows), rows), :] = hidden.astype(jnp.bfloat16)
+        part_buf[image, :, 0:feed] = slope.astype(jnp.bfloat16)
+
+    keeps.append(pltpu.make_async_copy(h_all, h_two_all, copy_sems.at[2]))
+    keeps.append(pltpu.make_async_copy(hidden_buf, hidden_all, copy_sems.at[5]))
+    keeps.append(
+        pltpu.make_async_copy(part_buf.at[:, :, pl.ds(0, feed)], slope_all, copy_sems.at[1])
+    )
+    for copy in keeps[-3:]:
+        copy.start()
+    for flip in (1, 3, 5, 7):
+        grad_gather.crossed(flip)
+    grad_own.wait()
+    column_products(
+        grad_mlp_all,
+        hidden_buf,
+        cols_buf,
+        staged_buf,
+        first_grads,
+        copy_sems.at[pl.ds(6, 2)],
+        copy_sems.at[pl.ds(8, 2)],
+    )
+    for gather in (grad_gather, next_gather):
+        gather.finish()
+    for copy in keeps:
+        copy.wait()
+    for copies in token_copies:
+        for copy in copies[1:]:
+            copy.wait_send()
+    for copy in bin_copies + mod_copies:
+        copy.wait_send()
+
+
+def front_part(
+    bin_ids,
+    image_counts,
+    noise,
+    mod_bias,
+    block_input,
+    cotangent,
+    attn_weight,
+    mlp_weight,
+    mod_weight,
+):
+    slots, local_tok, width = block_input.shape
+    rows = slots * local_tok
+    columns, feed = 3 * width // 8, mlp_weight.shape[1] // 16
+    low, full = jnp.bfloat16, jnp.float32
+    dma = pltpu.SemaphoreType.DMA
+    anywhere, inside = pl.BlockSpec(memory_space=pl.ANY), pl.BlockSpec(memory_space=pltpu.VMEM)
+    scalars = pl.BlockSpec(memory_space=pltpu.SMEM)
+    return pl.pallas_call(
+        front_kernel,
+        out_shape=[
+            jax.ShapeDtypeStruct((8, rows, columns), low),
+            jax.ShapeDtypeStruct((rows, width), low),
+            jax.ShapeDtypeStruct((8, rows, feed), low),
+            jax.ShapeDtypeStruct((8, rows, feed), low),
+            jax.ShapeDtypeStruct((8, rows, width), low),
+            jax.ShapeDtypeStruct((8, rows, width), low),
+            jax.ShapeDtypeStruct((8, rows, width), low),
+            jax.ShapeDtypeStruct((8, rows, columns), low),
+            jax.ShapeDtypeStruct((8, rows, columns // 3), low),
+            jax.ShapeDtypeStruct((8 * rows, feed), low),
+            jax.ShapeDtypeStruct((8, rows, feed), low),
+            jax.ShapeDtypeStruct((FIRST, 8, rows, rows), low),
+            jax.ShapeDtypeStruct((rows, width), low),
+            jax.ShapeDtypeStruct((rows, width), full),
+            jax.ShapeDtypeStruct((rows, width), low),
+            jax.ShapeDtypeStruct((rows, width), low),
+            jax.ShapeDtypeStruct((8, width), full),
+        ],
+        in_specs=[scalars] * 2 + [inside] * 2 + [anywhere] * 5,
+        out_specs=[anywhere, inside] + [anywhere] * 10 + [inside] * 5,
+        scratch_shapes=[
+            pltpu.VMEM((2, rows, width), full),
+            pltpu.VMEM((8, rows, columns), low),
+            pltpu.VMEM((8, rows, feed), low),
+            pltpu.VMEM((8, rows, columns), low),
+            pltpu.VMEM((8 * rows, feed), low),
+            pltpu.VMEM((2, 8, rows, rows), low),
+            pltpu.VMEM((2, 4, rows, rows), low),
+            pltpu.VMEM((8, rows, width), low),
+            pltpu.VMEM((8, rows, columns), low),
+            pltpu.VMEM((8, rows, columns // 3), low),
+            pltpu.VMEM((8, rows, width), low),
+            pltpu.VMEM((7, rows, width), low),
+            pltpu.VMEM((rows, width), low),
+            pltpu.VMEM((rows, width), low),
+            pltpu.VMEM((rows, width), low),
+            pltpu.VMEM((8, 128), full),
+            pltpu.VMEM((8, 8, 128), full),
+            pltpu.VMEM((8, 8, width), full),
+            pltpu.VMEM((8, 8, width), full),
+            dma((2, 3)),
+            dma((2, 2, 4)),
+            dma((2, 8)),
+            dma((2, 8)),
+            dma((2, 2, 8)),
+            dma((3, 2, 7 * PIECES)),
+            dma((4,)),
+            dma((4,)),
+            dma((2,)),
+            dma((2,)),
+            dma((4,)),
+            dma((4,)),
+            dma((14,)),
+        ],
+        compiler_params=pltpu.CompilerParams(
+            collective_id=5, has_side_effects=True, vmem_limit_bytes=63 * 1024 * 1024
+        ),
+        name="front_part",
+    )(
+        bin_ids,
+        image_counts,
+        noise,
+        mod_bias,
+        block_input,
+        cotangent,
+        attn_weight,
+        mlp_weight,
+        mod_weight,
+    )
+
+
+def plane_body(
+    block_input,
+    cotangent,
+    bin_ids,
+    image_counts,
+    attn_weight,
+    mlp_weight,
+    noise_table,
+    mod_weight,
+    mod_bias,
+):
+    model_width = block_input.shape[2]
+    rows = attn_weight.shape[0]
+    bins = noise_table.shape[0]
+    bias_piece = mod_bias.shape[0]
+    mine = lax.axis_index("fsdp")
+    (
+        qkv_weight,
+        out_weight,
+        up_weight,
+        down_low,
+        h_one_all,
+        h_two_all,
+        grad_mlp_all,
+        qkv_all,
+        attended_all,
+        hidden_all,
+        slope_all,
+        first_grads,
+        features,
+        first_sum,
+        attn_out,
+        grad_out,
+        mod_rows,
+    ) = front_part(
+        bin_ids,
+        image_counts,
+        noise_table,
+        mod_bias.reshape(1, bias_piece),
+        block_input,
+        cotangent,
+        attn_weight,
+        mlp_weight,
+        mod_weight,
+    )
+
+    def flat(array):
+        return array.reshape(-1, array.shape[-1])
+
+    shares, token_out, token_grad, mod_out, _, _, _, _ = back_part(
+        down_low,
+        up_weight,
+        hidden_all.reshape(8, rows, -1),
+        slope_all,
+        grad_mlp_all,
+        h_two_all,
+        first_grads,
+        h_one_all,
+        qkv_all,
+        attended_all,
+        flat(qkv_weight),
+        out_weight,
+        features,
+        first_sum,
+        attn_out,
+        grad_out,
+        mod_rows,
+    )
+    mod_out = mod_out.reshape(8, 4, 8, model_width)
+    block_out, input_grad = token_out, token_grad.astype(jnp.float32)
+    attn_weight_grad, mlp_weight_grad = attn_spread(shares), mlp_spread(shares)
+    grad_images = mod_out[:, :, :6].reshape(-1, 6 * model_width)
+    onehot_all = mod_out[:, :, 7, :bins].reshape(-1, bins)
+    activated = jax.nn.silu(noise_table)
+    chosen_all = jnp.dot(onehot_all, activated, precision=PRECISE)
+    mod_weight_grad = lax.dot_general(
+        chosen_all, grad_images, (((0,), (0,)), ((), ())), precision=PRECISE
+    )
+    image_term = lax.dot_general(
+        grad_images, mod_weight, (((1,), (1,)), ((), ())), precision=PRECISE
+    )
+    table_term = lax.dot_general(onehot_all, image_term, (((0,), (0,)), ((), ())), precision=PRECISE)
+    noise_grad = jax.vjp(jax.nn.silu, noise_table)[1](table_term)[0]
+    mod_bias_grad = lax.dynamic_slice_in_dim(
+        jnp.sum(grad_images, axis=0), mine * bias_piece, bias_piece
+    )
+    return (
+        block_out,
+        input_grad,
+        attn_weight_grad,
+        mlp_weight_grad,
+        noise_grad,
+        mod_weight_grad,
+        mod_bias_grad,
+    )
+
+
 def solution(mesh):
+    fits = mesh.shape["fsdp"] == 8 and mesh.shape["blk"] == 4
     return jax.shard_map(
-        body,
+        plane_body if fits else body,
         mesh=mesh,
         in_specs=(
             P("fsdp", "blk", None),

time: 2230 us -> 780 us (0.35)
  waiting for transfers between devices: 1790 us -> 0 us
  Pallas kernels: 0 us -> 724 us
  matrix products: 246 us -> 33.5 us
  other arithmetic: 125 us -> 3.48 us
  local copies, waits for them, and re-layouts: 45.8 us -> 4.82 us
    pallas_call x0 -> x4, Pallas kernels: none -> 724 us  [the longest x1 439 us: back_part(): pl.pallas_call(back_kernel, out_shape=[jax.ShapeDtypeStruct((CHUNKS, 8, r...]
    reduce_scatter x4 -> x0, waiting for transfers between devices: 609 us -> none  [the longest x1 387 us: body(): lax.psum_scatter(jnp.concatenate([rows_product(h_part, grad_pre), rows_pr...]
    psum x3 -> x0, waiting for transfers between devices: 603 us -> none  [the longest x1 398 us: body(): lax.psum(attn_part, 'blk').astype(jnp.float32)]
    all_gather x4 -> x0, waiting for transfers between devices: 575 us -> none  [the longest x1 274 us: body(): lax.all_gather(mlp_weight.astype(jnp.bfloat16), 'fsdp', axis=0, tiled=True)]
    dot_general x23 -> x4, matrix products: 246 us -> 33.5 us  [the longest x1 21.4 us: plane_body(): lax.dot_general(chosen_all, grad_images, (((0,), (0,)), ((), ())), precis...]
    concatenate x2 -> x0, other arithmetic: 69.6 us -> none  [the longest x1 46.9 us: body(): jnp.concatenate([rows_product(h_part, grad_pre), rows_product(grad_mlp, h...]
    convert_element_type x9 -> x1, other arithmetic: 37.2 us -> 1.56 us  [plane_body(): block_out, input_grad = (token_out, token_grad.astype(jnp.float32))]
  transfers between devices with their start and end apart: 11 -> 0, of which waited for: 11 -> 0; matrix products, arithmetic and copies ran while one was open for 10% -> 0% of each run, Pallas kernels for 0% -> 0%
where the time goes in v3:
time: 780 us; the launch traced here: 768 us
  Pallas kernels  724 us (93%)
  matrix products  33.5 us (4%)
    pallas_call x1, Pallas kernels, back_part(): pl.pallas_call(back_kernel, out_shape=[jax.ShapeDtypeStruct((CHUNKS, 8, r...  439 us
    pallas_call x1, Pallas kernels, front_part(): pl.pallas_call(front_kernel, out_shape=[jax.ShapeDtypeStruct((8, rows, co...  265 us
    dot_general x1, matrix products, plane_body(): lax.dot_general(chosen_all, grad_images, (((0,), (0,)), ((), ())), precis...  21.4 us

profile of v3, /device:TPU:0, one launch (start us, length us, event | category | flops | bytes accessed | tf_op | source)
XLA Modules:
  0.0 767.7 jit_solution(12252633868523954675)
XLA Ops:
  0.6 1.3 reshape.30.mod_bias
  2.6 265.4 %front_part.1 = (bf16[8,256,768]{2,1,0:T(8,128)(2,1)}, bf16[256,2048]{1,0:T(8,128)(2,1)}, bf16[8,256,1024]{2,1,0:T(8,128)(2,1)}, bf16[8,256,1024]{2,1,0:T(8,128)...) custom-call(s32[4]{0:T(128)} %bin_ids.1, ...), custom_call_target="tpu_custom_call" | custom-call | tf_op jit(solution)/shard_map/front_part/pallas_call | solution.py:1644
  268.0 439.4 %back_part.1 = (bf16[12,8,256,256]{3,2,1,0:T(8,128)(2,1)}, bf16[4,64,2048]{2,1,0:T(8,128)(2,1)}, bf16[4,64,2048]{2,1,0:T(8,128)(2,1)}, f32[8,32,2048]{2,1,0:T(8,...) custom-call(bf16[8,256,1024]{2,1,0:T(8,128)(2,1)} %get-tuple-element, ...), custom_call_target="tpu_custom_call" | custom-call | tf_op jit(solution)/shard_map/back_part/pallas_call | solution.py:1033
  707.4 0.0 copy-start.3
  707.4 1.9 slice_reduce_fusion
  709.3 0.9 copy.16
  710.3 0.9 slice.8
  711.2 0.0 copy-done.3
  711.2 0.2 fusion.2
  711.4 0.0 copy-start
  711.4 21.4 %fusion.7 = f32[256,12288]{1,0:T(8,128)} fusion(f32[32,256]{1,0:T(8,128)S(1)} %fusion.2, f32[32,12288]{1,0:T(8,128)S(1)} %bitcast.14), kind=kOutput, calls=%fused_computation.10 | convolution fusion | flops 1207959552 | bytes 14188544 | tf_op jit(solution)/shard_map/dot_general | solution.py:1793
  732.8 0.0 copy-done
  732.8 11.0 %fusion.6 = f32[32,256]{1,0:T(8,128)S(1)} fusion(f32[32,12288]{1,0:T(8,128)S(1)} %bitcast.15, f32[256,12288]{1,0:T(8,128)S(1)} %copy-done), kind=kOutput, calls=%fused_computation.9 | convolution fusion | flops 1207959552 | bytes 14188544 | tf_op jit(solution)/shard_map/dot_general | solution.py:1796
  743.8 0.9 fusion.1
  744.7 13.5 %mlp_spread.1 = f32[256,16384]{1,0:T(8,128)} custom-call(bf16[12,8,256,256]{3,2,1,0:T(8,128)(2,1)} %get-tuple-element.47.share_ref), custom_call_target="tpu_custom_call" | custom-call | tf_op jit(solution)/shard_map/mlp_spread/pallas_call | solution.py:1099
  758.2 0.0 copy-start.1
  758.2 0.0 copy-start.2
  758.2 6.1 attn_spread.1
  764.3 0.7 dynamic_slice.3
  765.0 0.0 copy-done.1
  765.0 1.6 convert_element_type.3
  766.5 0.0 copy-done.2
  766.5 1.0 copy.19
  (1 shorter events, 0.0 us)
Async XLA Ops:
  707.4 3.8 copy-start.3
  711.4 21.4 %copy-start = (f32[256,12288]{1,0:T(8,128)S(1)}, f32[256,12288]{1,0:T(8,128)}, u32[]{:S(2)}) copy-start(f32[256,12288]{1,0:T(8,128)} %mod_weight.1) | copy-start | bytes 37748740
  758.2 6.8 copy-start.1
  758.2 8.4 %copy-start.2 = (bf16[4,64,2048]{2,1,0:T(8,128)(2,1)S(1)}, bf16[4,64,2048]{2,1,0:T(8,128)(2,1)}, u32[]{:S(2)}) copy-start(bf16[4,64,2048]{2,1,0:T(8,128)(2,1)} %get-tuple-element.58) | copy-start | bytes 3145732

commit v4 on v3

--- a/solution.py
+++ b/solution.py
@@ -304,8 +304,6 @@
 
 CHUNKS = 12
 FIRST = 4
-UP_TICK = 4
-LATE_TICK = 8
 EARLY = 8
 HALF_ROWS = 128
 BAND = 32
@@ -328,7 +326,7 @@
     return ref[rows, :].astype(jnp.float32)
 
 
-def column_products(source, right, cols, staged, result, load_sems, store_sems):
+def column_products(source, right, cols, staged, result, load_sems, store_sems, pieces=None, hook=None):
     rows = cols.shape[-1]
     count = result.shape[0]
 
@@ -361,11 +359,16 @@
         def _():
             store(block - 2).wait()
 
+        if hook:
+            hook(block)
         product = contract(cols[slot].reshape(8 * rows, rows), right[...], 0, 0)
         for number in range(count):
-            staged[slot, number] = product[:, number * rows : (number + 1) * rows].astype(
-                jnp.bfloat16
-            )
+            begins = pieces[number] if pieces else (number * rows,)
+            size = rows // len(begins)
+            for index, begin in enumerate(begins):
+                staged[slot, number, :, index * size : (index + 1) * size] = product[
+                    :, begin : begin + size
+                ].astype(jnp.bfloat16)
         store(block).start()
 
     store(6).wait()
@@ -454,10 +457,11 @@
     fetch(0)
     plane.got(peer.at[0], core_recv.at[0])
     yield
-    for slot in (1, 2):
-        for part in (0, 1):
-            at = pl.ds(part * half, half)
-            plane.got(near.at[slot - 1, at], near_recv.at[(slot - 1) * 2 + part])
+    for slot, part in ((1, 0), (2, 1), (2, 0), (1, 1)):
+        at = pl.ds(part * half, half)
+        plane.got(near.at[slot - 1, at], near_recv.at[(slot - 1) * 2 + part])
+        if (slot, part) == (2, 1):
+            yield
     own = own_of(0)
 
     def step(at):
@@ -504,7 +508,9 @@
     second_buf,
     stage,
     own_pair,
+    image_buf,
     grad_all,
+    down_buf,
     grad_first,
     saved_grad,
     cols_buf,
@@ -581,10 +587,7 @@
 
         @pl.loop(0, 8)
         def _(block):
-            half_buf[slot, block] = (
-                sum_buf[slot, block, my_half, :].astype(jnp.float32)
-                + half_in[block].astype(jnp.float32)
-            ).astype(jnp.bfloat16)
+            half_buf[slot, block] = sum_buf[slot, block, my_half, :] + half_in[block]
 
         if k == CHUNKS - 1:
             pltpu.make_async_copy(
@@ -617,56 +620,50 @@
 
         @pl.loop(0, 8)
         def _(block):
-            sum_buf[slot, block] = (
-                sum_buf[slot, block].astype(jnp.float32) + in_buf[block].astype(jnp.float32)
-            ).astype(jnp.bfloat16)
+            sum_buf[slot, block] = sum_buf[slot, block] + in_buf[block]
 
         z_copy(1, k, sum_buf.at[slot, :, other_half], land_b.at[k], partner).start()
 
-    def start_tick(chunk):
-        return LATE_TICK if chunk >= EARLY else (UP_TICK if chunk >= FIRST else -1)
-
-    def tick(now):
+    def send_outward(first, last):
         @pl.when(jnp.logical_not(is_mid))
         def _():
-            for chunk in range(CHUNKS):
-                if start_tick(chunk) == now:
-                    start_outward(chunk)
+            for chunk in range(first, last):
+                start_outward(chunk)
+
+    def tick(now):
+        k, odd = now // 2, now % 2
+
+        def stage(work, chunk):
+            if 0 <= chunk < CHUNKS:
+                work(chunk)
 
         @pl.when(is_mid)
         def _():
-            if 0 <= now - 3 < CHUNKS:
-                stage_d(now - 3)
-            if 0 <= now - 2 < CHUNKS:
-                stage_x(now - 2)
-            if 0 <= now - 1 < CHUNKS:
-                stage_f(now - 1)
-            if now < CHUNKS:
-                stage_s(now)
-
-    @pl.when(jnp.logical_not(is_mid))
-    def _():
-        for chunk in range(CHUNKS):
-            if start_tick(chunk) < 0:
-                start_outward(chunk)
+            if odd:
+                stage(stage_f, k - 1)
+                stage(stage_d, k - 3)
+            else:
+                stage(stage_s, k)
+                stage(stage_x, k - 2)
+
+    send_outward(0, FIRST)
 
     attended_load = pltpu.make_async_copy(attended_all, attended_buf, load_sems.at[0])
     attended_load.start()
     feed = up_weight.shape[-1]
-    down_part, up_part = pl.ds(0, feed), pl.ds(feed, feed)
 
     pltpu.make_async_copy(
-        down_low.at[mine], grad_all.at[mine, :, down_part], weight_sems.at[0, 0]
+        down_low.at[mine], down_buf.at[mine], weight_sems.at[0, 0]
     ).start()
     for flip in (6, 7, 2, 4, 3, 5, 1):
         remote(
             down_low.at[at(flip)],
-            grad_all.at[mine, :, down_part],
+            down_buf.at[mine],
             weight_sems.at[0, flip],
             weight_sems.at[1, flip],
             plane.to(flip),
         ).start()
-    up_load = pltpu.make_async_copy(up_weight, grad_all.at[:, :, up_part], load_sems.at[5])
+    up_load = pltpu.make_async_copy(up_weight, grad_all.at[:, :, pl.ds(0, feed)], load_sems.at[5])
     up_load.start()
     mod_sum[...] = jnp.zeros_like(mod_sum)
     row = {
@@ -781,61 +778,47 @@
 
     up_load.wait()
     pltpu.make_async_copy(
-        down_low.at[mine], grad_all.at[mine, :, down_part], weight_sems.at[0, 0]
+        down_low.at[mine], down_buf.at[mine], weight_sems.at[0, 0]
     ).wait()
-    tick(0)
-    tick(1)
+    for now in range(5):
+        tick(now)
     for flip in range(1, 8):
-        plane.got(grad_all.at[at(flip), :, down_part], weight_sems.at[1, flip])
+        plane.got(down_buf.at[at(flip)], weight_sems.at[1, flip])
         plane.gone(down_low.at[0], weight_sems.at[0, flip])
 
     def image_loads(step):
-        image = flipped(mine, step)
+        image, slot = flipped(mine, step), lax.rem(step, 2)
         return [
             pltpu.make_async_copy(
-                hidden_all.at[image], stage.at[0, :, pl.ds(0, feed)], load_sems.at[6]
+                slope_all.at[image], image_buf.at[slot, :, pl.ds(0, feed)], load_sems.at[6 + slot]
             ),
-            pltpu.make_async_copy(
-                slope_all.at[image], stage.at[0, :, pl.ds(feed, feed)], load_sems.at[7]
-            ),
-            pltpu.make_async_copy(grad_mlp_all.at[image], stage.at[1], load_sems.at[8]),
+            pltpu.make_async_copy(grad_mlp_all.at[image], stage.at[slot], load_sems.at[8 + slot]),
         ]
-
-    def out_store(step):
-        return pltpu.make_async_copy(
-            own_pair.at[lax.rem(step, 2)],
-            partial_out.at[flipped(mine, step)],
-            load_sems.at[9 + lax.rem(step, 2)],
-        )
 
     for load in image_loads(0):
         load.start()
 
     @pl.loop(0, 8)
     def _(step):
+        @pl.when(step == 4)
+        def _():
+            tick(5)
+
+        slot = lax.rem(step, 2)
         for load in image_loads(step):
             load.wait()
-        image = flipped(mine, step)
-        image_rows = pl.ds(pl.multiple_of(image * rows, rows), rows)
-
-        @pl.when(step >= 2)
-        def _():
-            out_store(step - 2).wait()
-
-        down = grad_all[:, :, 0:feed].reshape(8 * rows, feed)
-        grad_hidden = contract(stage[1], down, 1, 0)
-        saved_grad[image_rows, :] = (
-            grad_hidden * stage[0, :, feed : 2 * feed].astype(jnp.float32)
-        ).astype(jnp.bfloat16)
-        own_pair[lax.rem(step, 2)] = contract(stage[0, :, 0:feed], down, 1, 1).astype(jnp.bfloat16)
-        out_store(step).start()
 
         @pl.when(step < 7)
         def _():
             for load in image_loads(step + 1):
                 load.start()
 
-        up = grad_all[:, :, feed : 2 * feed].reshape(8 * rows, feed)
+        image_rows = pl.ds(pl.multiple_of(flipped(mine, step) * rows, rows), rows)
+        grad_hidden = contract(stage[slot], down_buf[...].reshape(8 * rows, feed), 1, 0)
+        saved_grad[image_rows, :] = (
+            grad_hidden * image_buf[slot, :, 0:feed].astype(jnp.float32)
+        ).astype(jnp.bfloat16)
+        up = grad_all[:, :, 0:feed].reshape(8 * rows, feed)
         second_buf[step] = contract(saved_grad[image_rows, :], up, 1, 1).astype(jnp.bfloat16)
         for number in (1, 3, 5, 7):
 
@@ -843,22 +826,61 @@
             def _(number=number):
                 give(second_buf.at[number], first_buf, 1, number // 2)
 
-        @pl.when(step == 3)
+
+    def hidden_load(step):
+        slot = lax.rem(step, 2)
+        return pltpu.make_async_copy(
+            hidden_all.at[step], image_buf.at[slot, :, pl.ds(0, feed)], load_sems.at[6 + slot]
+        )
+
+    def out_store(step):
+        slot = lax.rem(step, 2)
+        return pltpu.make_async_copy(own_pair.at[slot], partial_out.at[step], load_sems.at[8 + slot])
+
+    def out_products():
+        hidden_load(0).start()
+
+        @pl.loop(0, 8)
+        def _(step):
+            slot = lax.rem(step, 2)
+            hidden_load(step).wait()
+
+            @pl.when(step < 7)
+            def _():
+                hidden_load(step + 1).start()
+
+            @pl.when(step >= 2)
+            def _():
+                out_store(step - 2).wait()
+
+            @pl.when(step == 5)
+            def _():
+                tick(9)
+
+            own_pair[slot] = contract(
+                image_buf[slot, :, 0:feed], down_buf[...].reshape(8 * rows, feed), 1, 1
+            ).astype(jnp.bfloat16)
+            out_store(step).start()
+
+        out_store(6).wait()
+        out_store(7).wait()
+
+    def up_hook(block):
+        @pl.when(block == 6)
         def _():
-            tick(2)
-
-    out_store(6).wait()
-    out_store(7).wait()
-    tick(3)
-    column_products(
-        h_two_all,
-        saved_grad,
-        cols_buf,
-        staged_buf,
-        more.at[pl.ds(0, 4)],
-        load_sems.at[pl.ds(3, 2)],
-        load_sems.at[pl.ds(11, 2)],
-    )
+            tick(7)
+
+    def up_products():
+        column_products(
+            h_two_all,
+            saved_grad,
+            cols_buf,
+            staged_buf,
+            more.at[pl.ds(0, 4)],
+            load_sems.at[pl.ds(3, 2)],
+            load_sems.at[pl.ds(11, 2)],
+            hook=up_hook,
+        )
 
     def own_flow(number, finish):
         return scatter_flow(
@@ -872,7 +894,13 @@
             finish,
         )
 
-    run(own_flow(1, finish_feed), 4)
+    tick(6)
+    up_products()
+    send_outward(FIRST, EARLY)
+    for step, _ in enumerate(own_flow(1, finish_feed)):
+        tick((8, 10, 11)[step])
+        if step == 0:
+            out_products()
     for slot in range(4):
         plane.gone(second_buf.at[slot], core_send.at[1, slot])
 
@@ -897,6 +925,10 @@
 
             @pl.when(step == number)
             def _(number=number):
+                if number in (1, 2, 4):
+                    tick({1: 12, 2: 13, 4: 15}[number])
+                if number == 2:
+                    tick(14)
                 gather.step(number)
                 if number == 7:
                     gather.finish()
@@ -913,22 +945,22 @@
         grad_attended = contract(grad, out_weight[...], 1, 1).astype(jnp.bfloat16)
         image_rows = pl.ds(pl.multiple_of(image * rows, rows), rows)
         for head in range(third // HD):
-            begin = head * HD
-            queries = qkv_buf[slot, :, begin : begin + HD]
-            key_rows = qkv_buf[slot, :, third + begin : third + begin + HD]
-            value_rows = qkv_buf[slot, :, 2 * third + begin : 2 * third + begin + HD]
+            begin, first = head * HD, 3 * head * HD
+            queries = qkv_buf[slot, :, first : first + HD]
+            key_rows = qkv_buf[slot, :, first + HD : first + 2 * HD]
+            value_rows = qkv_buf[slot, :, first + 2 * HD : first + 3 * HD]
             grad_head = grad_attended[:, begin : begin + HD]
             attention = softmax_rows(queries, key_rows)
             grad_weights = contract(grad_head, value_rows, 1, 1)
             row_delta = jnp.sum(attention * grad_weights, axis=-1, keepdims=True)
             grad_scores = (attention * (grad_weights - row_delta)).astype(jnp.bfloat16)
-            saved_grad[image_rows, begin : begin + HD] = (
+            saved_grad[image_rows, first : first + HD] = (
                 contract(grad_scores, key_rows, 1, 0) * scale
             ).astype(jnp.bfloat16)
-            saved_grad[image_rows, third + begin : third + begin + HD] = (
+            saved_grad[image_rows, first + HD : first + 2 * HD] = (
                 contract(grad_scores, queries, 0, 0) * scale
             ).astype(jnp.bfloat16)
-            saved_grad[image_rows, 2 * third + begin : 2 * third + begin + HD] = contract(
+            saved_grad[image_rows, first + 2 * HD : first + 3 * HD] = contract(
                 attention.astype(jnp.bfloat16), grad_head, 0, 0
             ).astype(jnp.bfloat16)
         out_sum[...] += contract(attended_buf[image], grad, 0, 0)
@@ -941,15 +973,11 @@
             def _(number=number):
                 give(second_buf.at[number], first_buf, 2, number // 2)
 
-        for number, now in ((2, 6), (5, 7)):
-
-            @pl.when(step == number)
-            def _(now=now):
-                tick(now)
 
     for block in range(8):
-        staged_buf[0, 0] = out_sum[:, block * rows : (block + 1) * rows].astype(jnp.bfloat16)
-        pltpu.sync_copy(staged_buf.at[0, 0], more.at[7, block])
+        in_buf[block] = out_sum[:, block * rows : (block + 1) * rows].astype(jnp.bfloat16)
+    out_copy = pltpu.make_async_copy(in_buf, more.at[7], load_sems.at[0])
+    out_copy.start()
     column_products(
         h_all,
         saved_grad.at[:, pl.ds(0, columns)],
@@ -958,15 +986,20 @@
         more.at[pl.ds(4, 3)],
         load_sems.at[pl.ds(3, 2)],
         load_sems.at[pl.ds(11, 2)],
+        [[(3 * head + number) * HD for head in range(third // HD)] for number in range(3)],
     )
 
     def finish_input(where, value):
         total = back_norm(plain(features, where), value, "scale_one", "shift_one")
         own_pair[0, where, :] = (total + grad_first[where, :]).astype(jnp.bfloat16)
 
-    run(own_flow(2, finish_input), 8)
+    out_copy.wait()
+    send_outward(EARLY, CHUNKS)
+    tick(16)
+    run(own_flow(2, finish_input), 17)
     return_tokens(own_grad, token_grad, 1)
-    run(staged_flow(partial_out, grad_all, 0, finish_out), 10)
+    for step, _ in enumerate(staged_flow(partial_out, grad_all, 0, finish_out)):
+        tick(20 + step)
     return_tokens(image_out, token_out, 0)
 
     mod_copies = []
@@ -979,20 +1012,23 @@
         )
         copy.start()
         mod_copies.append(copy)
-    tick(12)
+    tick(23)
+    tick(24)
     for copy in mod_copies:
         copy.wait_recv()
     own = pltpu.make_async_copy(mod_land, mod_out.at[mine], mod_sems.at[0, 3])
     own.start()
     mod_gather = Gather(plane, mod_land, mod_out, mod_gather_sems.at[0], mod_gather_sems.at[1])
     mod_gather.start()
-    tick(13)
+    tick(25)
+    tick(26)
     mod_gather.middle()
     mod_gather.far()
     for flip in (1, 3, 5, 7):
         mod_gather.crossed(flip)
     mod_gather.finish()
-    tick(14)
+    for now in range(27, 2 * CHUNKS + 6):
+        tick(now)
     own.wait()
     for copy in mod_copies:
         copy.wait_send()
@@ -1049,7 +1085,9 @@
             pltpu.VMEM((8, rows, width), low),
             pltpu.VMEM((2, rows, width), low),
             pltpu.VMEM((2, rows, width), low),
+            pltpu.VMEM((2, rows, feed), low),
             pltpu.VMEM((8, rows, width), low),
+            pltpu.VMEM((8, rows, feed), low),
             pltpu.VMEM((rows, width), full),
             pltpu.VMEM((8 * rows, feed), low),
             pltpu.VMEM((2, 8, rows, rows), low),
@@ -1251,6 +1289,7 @@
     bin_sems,
     mod_sems,
     weight_sems,
+    beside_sems,
     gather_sems,
     core_send,
     core_recv,
@@ -1305,10 +1344,16 @@
     for copy in bin_copies:
         copy.start()
 
+    parity = lax.rem(place, 2)
+    beside = (mine, place + 1 - 2 * parity)
+
+    def half_of(size):
+        return pl.ds(pl.multiple_of(parity * size, size), size)
+
     def load_columns(source, slot, begins, size):
         return [
             pltpu.make_async_copy(
-                source.at[:, pl.ds(begin, size)],
+                source.at[:, pl.ds(pl.multiple_of(begin, HD), size)],
                 load_buf.at[slot, :, pl.ds(number * size, size)],
                 load_sems.at[slot, number],
             )
@@ -1316,8 +1361,12 @@
         ]
 
     def cast_and_send(source, begins_of, size, stage, result, kind):
-        loads = [load_columns(source, step % 2, begins_of(at(flip)), size) for step, flip in enumerate(flips)]
+        loads = [
+            load_columns(source, step % 2, begins_of(at(flip)), size)
+            for step, flip in enumerate(flips)
+        ]
         total = size * len(loads[0])
+        half = half_of(total)
         for load in loads[0]:
             load.start()
         for step, flip in enumerate(flips):
@@ -1328,38 +1377,64 @@
                 load.wait()
 
             def cast(band, step=step):
-                stage[step, band, :] = load_buf[step % 2, band, :total].astype(jnp.bfloat16)
+                stage[step, band, 0:total] = load_buf[step % 2, band, 0:total].astype(jnp.bfloat16)
 
             bands(rows, cast)
+            src = stage.at[step, :, pl.ds(0, total)]
             if flip:
                 remote(
-                    stage.at[step],
-                    result.at[mine],
+                    src,
+                    result.at[mine, :, half],
                     weight_sems.at[0, kind, flip],
                     weight_sems.at[1, kind, flip],
                     plane.to(flip),
                 ).start()
             else:
                 pltpu.make_async_copy(
-                    stage.at[step], result.at[mine], weight_sems.at[0, kind, 0]
+                    src, result.at[mine, :, half], weight_sems.at[0, kind, 0]
                 ).start()
 
-    def weights_arrived(result, kind):
-        for flip in range(1, 8):
-            plane.got(result.at[at(flip)], weight_sems.at[1, kind, flip])
-
-    def weights_gone(stage, result, kind):
-        pltpu.make_async_copy(stage.at[7], result.at[mine], weight_sems.at[0, kind, 0]).wait()
-        for flip in range(1, 8):
-            plane.gone(stage.at[0], weight_sems.at[0, kind, flip])
+    def pass_on(stage, result, kind, total):
+        half = half_of(total)
+        pltpu.make_async_copy(
+            stage.at[7, :, pl.ds(0, total)], result.at[mine, :, half], weight_sems.at[0, kind, 0]
+        ).wait()
+        for flip in (1, 2, 3, 4, 5, 6, 7, 0):
+            piece = result.at[at(flip), :, half]
+            if flip:
+                plane.got(piece, weight_sems.at[1, kind, flip])
+            remote(
+                piece,
+                piece,
+                beside_sems.at[0, kind, flip],
+                beside_sems.at[1, kind, flip],
+                beside,
+            ).start()
+
+    def weights_ready(stage, result, kind, total):
+        for flip in range(8):
+            piece = result.at[at(flip), :, half_of(total)]
+            plane.got(piece, beside_sems.at[1, kind, flip])
+            plane.gone(piece, beside_sems.at[0, kind, flip])
+            if flip:
+                plane.gone(stage.at[0, :, pl.ds(0, total)], weight_sems.at[0, kind, flip])
 
     cast_and_send(
         attn_weight,
-        lambda owner: [number * width + owner * third for number in range(3)],
-        third,
+        lambda owner: [number * width + owner * third + parity * HD for number in range(3)],
+        HD,
         qkv_stage,
         qkv_weight,
         0,
+    )
+
+    cast_and_send(
+        mlp_weight,
+        lambda owner: [owner * feed + parity * (feed // 2)],
+        feed // 2,
+        up_stage,
+        up_weight,
+        1,
     )
 
     for copy in bin_copies:
@@ -1406,6 +1481,7 @@
     ]
     for copy in mod_copies:
         copy.start()
+    pass_on(qkv_stage, qkv_weight, 0, 3 * HD)
     mod_land[mine] = mod_part[mine]
     for copy in mod_copies:
         copy.wait_recv()
@@ -1439,9 +1515,6 @@
     bands(rows, first_norm)
     h_gather = Gather(plane, own_h, h_all, gather_sems.at[0, 0], gather_sems.at[0, 1])
     h_gather.start()
-    cast_and_send(
-        mlp_weight, lambda owner: [owner * feed], feed, up_stage, up_weight, 1
-    )
 
     tokens_arrived(1)
 
@@ -1491,8 +1564,7 @@
 
     bands(rows, cast_out)
 
-    weights_arrived(qkv_weight, 0)
-    weights_gone(qkv_stage, qkv_weight, 0)
+    weights_ready(qkv_stage, qkv_weight, 0, 3 * HD)
     load = pltpu.make_async_copy(qkv_weight, weight_buf, copy_sems.at[1])
     load.start()
     load.wait()
@@ -1512,10 +1584,10 @@
         ).astype(jnp.bfloat16)
         qkv_buf[image] = projected
         for head in range(third // HD):
-            begin = head * HD
-            queries = projected[:, begin : begin + HD]
-            key_rows = projected[:, third + begin : third + begin + HD]
-            value_rows = projected[:, 2 * third + begin : 2 * third + begin + HD]
+            begin, first = head * HD, 3 * head * HD
+            queries = projected[:, first : first + HD]
+            key_rows = projected[:, first + HD : first + 2 * HD]
+            value_rows = projected[:, first + 2 * HD : first + 3 * HD]
             attention = softmax_rows(queries, key_rows).astype(jnp.bfloat16)
             attended_buf[image, :, begin : begin + HD] = contract(
                 attention, value_rows, 1, 0
@@ -1540,6 +1612,7 @@
                     plane.to(1),
                 ).start()
 
+    pass_on(up_stage, up_weight, 1, feed // 2)
     keeps = [
         pltpu.make_async_copy(qkv_buf, qkv_all, copy_sems.at[3]),
         pltpu.make_async_copy(attended_buf, attended_all, copy_sems.at[4]),
@@ -1573,8 +1646,7 @@
     next_gather = Gather(plane, own_next, h_all, gather_sems.at[2, 0], gather_sems.at[2, 1])
     next_gather.start()
     grad_gather.far()
-    weights_arrived(up_weight, 1)
-    weights_gone(up_stage, up_weight, 1)
+    weights_ready(up_stage, up_weight, 1, feed // 2)
     load = pltpu.make_async_copy(up_weight, up_stage, copy_sems.at[1])
     load.start()
     load.wait()
@@ -1689,6 +1761,7 @@
             dma((2, 8)),
             dma((2, 8)),
             dma((2, 2, 8)),
+            dma((2, 2, 8)),
             dma((3, 2, 7 * PIECES)),
             dma((4,)),
             dma((4,)),
@@ -1713,6 +1786,77 @@
         mlp_weight,
         mod_weight,
     )
+
+
+def mod_grads_kernel(
+    rows_ref, onehot_ref, noise_ref, weight_ref, weight_grad_ref, noise_grad_ref, bias_ref, chosen, total
+):
+    part = pl.program_id(0)
+    noise = noise_ref[...]
+    onehot = onehot_ref[...]
+    rise = 1.0 / (1.0 + jnp.exp(-noise))
+
+    def exact(left, right, left_dim, right_dim):
+        return lax.dot_general(
+            left,
+            right,
+            (((left_dim,), (right_dim,)), ((), ())),
+            precision=PRECISE,
+            preferred_element_type=jnp.float32,
+        )
+
+    @pl.when(part == 0)
+    def _():
+        chosen[...] = exact(onehot, noise * rise, 1, 0)
+        total[...] = jnp.zeros_like(total)
+
+    grads = rows_ref[0]
+    bias_ref[...] = jnp.broadcast_to(jnp.sum(grads, axis=0, keepdims=True), bias_ref.shape)
+    low = grads.astype(jnp.bfloat16)
+    weight_grad_ref[...] = contract(chosen[...].astype(jnp.bfloat16), low, 0, 0)
+    total[...] += contract(weight_ref[...].astype(jnp.bfloat16), low, 1, 1)
+
+    @pl.when(part == pl.num_programs(0) - 1)
+    def _():
+        table = lax.dot_general(
+            onehot,
+            total[...],
+            (((0,), (1,)), ((), ())),
+            precision=PRECISE,
+            preferred_element_type=jnp.float32,
+        )
+        noise_grad_ref[...] = table * (rise + noise * rise * (1.0 - rise))
+
+
+def mod_grads(image_rows, onehot, noise, weight):
+    images, _, width = image_rows.shape
+    depth = weight.shape[0]
+    return pl.pallas_call(
+        mod_grads_kernel,
+        grid=(12,),
+        out_shape=[
+            jax.ShapeDtypeStruct(weight.shape, jnp.float32),
+            jax.ShapeDtypeStruct(noise.shape, jnp.float32),
+            jax.ShapeDtypeStruct((8, 6 * width), jnp.float32),
+        ],
+        in_specs=[
+            pl.BlockSpec((1, images, width // 2), lambda part: (part // 2, 0, part % 2)),
+            pl.BlockSpec(onehot.shape, lambda part: (0, 0)),
+            pl.BlockSpec(noise.shape, lambda part: (0, 0)),
+            pl.BlockSpec((depth, width // 2), lambda part: (0, part)),
+        ],
+        out_specs=[
+            pl.BlockSpec((depth, width // 2), lambda part: (0, part)),
+            pl.BlockSpec(noise.shape, lambda part: (0, 0)),
+            pl.BlockSpec((8, width // 2), lambda part: (0, part)),
+        ],
+        scratch_shapes=[
+            pltpu.VMEM((images, depth), jnp.float32),
+            pltpu.VMEM((depth, images), jnp.float32),
+        ],
+        compiler_params=pltpu.CompilerParams(vmem_limit_bytes=VMEM_BYTES),
+        name="mod_grads",
+    )(image_rows.transpose(1, 0, 2), onehot, noise, weight)
 
 
 def plane_body(
@@ -1786,21 +1930,11 @@
     mod_out = mod_out.reshape(8, 4, 8, model_width)
     block_out, input_grad = token_out, token_grad.astype(jnp.float32)
     attn_weight_grad, mlp_weight_grad = attn_spread(shares), mlp_spread(shares)
-    grad_images = mod_out[:, :, :6].reshape(-1, 6 * model_width)
     onehot_all = mod_out[:, :, 7, :bins].reshape(-1, bins)
-    activated = jax.nn.silu(noise_table)
-    chosen_all = jnp.dot(onehot_all, activated, precision=PRECISE)
-    mod_weight_grad = lax.dot_general(
-        chosen_all, grad_images, (((0,), (0,)), ((), ())), precision=PRECISE
-    )
-    image_term = lax.dot_general(
-        grad_images, mod_weight, (((1,), (1,)), ((), ())), precision=PRECISE
-    )
-    table_term = lax.dot_general(onehot_all, image_term, (((0,), (0,)), ((), ())), precision=PRECISE)
-    noise_grad = jax.vjp(jax.nn.silu, noise_table)[1](table_term)[0]
-    mod_bias_grad = lax.dynamic_slice_in_dim(
-        jnp.sum(grad_images, axis=0), mine * bias_piece, bias_piece
-    )
+    mod_weight_grad, noise_grad, bias_sums = mod_grads(
+        mod_out.reshape(-1, 8, model_width), onehot_all, noise_table, mod_weight
+    )
+    mod_bias_grad = lax.dynamic_slice_in_dim(bias_sums[0], mine * bias_piece, bias_piece)
     return (
         block_out,
         input_grad,

time: 780 us -> 703 us (0.901); the launches traced: 768 us -> 699 us
  Pallas kernels: 724 us -> 687 us
  matrix products: 33.5 us -> 0 us
    pallas_call x1, Pallas kernels: 265 us -> 226 us  [front_part(): pl.pallas_call(front_kernel, out_shape=[jax.ShapeDtypeStruct((8, rows, co...]
    dot_general x4 -> x0, matrix products: 33.5 us -> none  [the longest x1 21.4 us: plane_body(): lax.dot_general(chosen_all, grad_images, (((0,), (0,)), ((), ())), precis...]
    pallas_call x0 -> x1, Pallas kernels: none -> 16.6 us  [mod_grads(): pl.pallas_call(mod_grads_kernel, grid=(12,), out_shape=[jax.ShapeDtypeStr...]
    pallas_call x1, Pallas kernels: 439 us -> 424 us  [back_part(): pl.pallas_call(back_kernel, out_shape=[jax.ShapeDtypeStruct((CHUNKS, 8, r...]
where the time goes in v4:
time: 703 us; the launch traced here: 699 us
  Pallas kernels  687 us (98%)
  local copies, waits for them, and re-layouts  9.57 us (1%)
    pallas_call x1, Pallas kernels, back_part(): pl.pallas_call(back_kernel, out_shape=[jax.ShapeDtypeStruct((CHUNKS, 8, r...  424 us
    pallas_call x1, Pallas kernels, front_part(): pl.pallas_call(front_kernel, out_shape=[jax.ShapeDtypeStruct((8, rows, co...  226 us
    pallas_call x1, Pallas kernels, mod_grads(): pl.pallas_call(mod_grads_kernel, grid=(12,), out_shape=[jax.ShapeDtypeStr...  16.6 us

profile of v4, /device:TPU:0, one launch (start us, length us, event | category | flops | bytes accessed | tf_op | source)
XLA Modules:
  0.0 699.1 jit_solution(4401999381109473018)
XLA Ops:
  0.6 1.3 reshape.27.mod_bias
  2.6 226.2 %front_part.1 = (bf16[8,256,768]{2,1,0:T(8,128)(2,1)}, bf16[256,2048]{1,0:T(8,128)(2,1)}, bf16[8,256,1024]{2,1,0:T(8,128)(2,1)}, bf16[8,256,1024]{2,1,0:T(8,128)...) custom-call(s32[4]{0:T(128)} %bin_ids.1, ...), custom_call_target="tpu_custom_call" | custom-call | tf_op jit(solution)/shard_map/front_part/pallas_call | solution.py:1716
  228.8 424.3 %back_part.1 = (bf16[12,8,256,256]{3,2,1,0:T(8,128)(2,1)}, bf16[4,64,2048]{2,1,0:T(8,128)(2,1)}, bf16[4,64,2048]{2,1,0:T(8,128)(2,1)}, f32[8,32,2048]{2,1,0:T(8,...) custom-call(bf16[8,256,1024]{2,1,0:T(8,128)(2,1)} %get-tuple-element, ...), custom_call_target="tpu_custom_call" | custom-call | tf_op jit(solution)/shard_map/back_part/pallas_call | solution.py:1069
  653.1 4.1 copy.21
  657.2 1.5 slice.8
  658.7 16.6 %mod_grads.1 = (f32[256,12288]{1,0:T(8,128)}, f32[64,256]{1,0:T(8,128)}, f32[8,12288]{1,0:T(8,128)}) custom-call(f32[8,32,2048]{2,1,0:T(8,128)} %bitcast.10, f32[32,64]{1,0:T(8,128)} %bitcast.15, f32[64,256]{1,0:T(8,128)} %noise_ref.1, f32[256,12288]{1,0:T(8,128)} %weight_ref.1), custom_call_target="tpu_custom_call" | custom-call | tf_op jit(solution)/shard_map/mod_grads/pallas_call | solution.py:1834
  675.4 1.0 slice.7
  676.4 0.6 dynamic-slice_reduce_fusion
  677.0 13.5 %mlp_spread.1 = f32[256,16384]{1,0:T(8,128)} custom-call(bf16[12,8,256,256]{3,2,1,0:T(8,128)(2,1)} %get-tuple-element.50.share_ref), custom_call_target="tpu_custom_call" | custom-call | tf_op jit(solution)/shard_map/mlp_spread/pallas_call | solution.py:1137
  690.5 0.0 copy-start
  690.5 0.0 copy-start.1
  690.5 6.1 attn_spread.1
  696.6 0.0 copy-done
  696.6 1.6 convert_element_type.3
  698.2 0.0 copy-done.1
  698.2 1.0 copy.24
Async XLA Ops:
  690.5 6.1 copy-start
  690.5 7.7 %copy-start.1 = (bf16[4,64,2048]{2,1,0:T(8,128)(2,1)S(1)}, bf16[4,64,2048]{2,1,0:T(8,128)(2,1)}, u32[]{:S(2)}) copy-start(bf16[4,64,2048]{2,1,0:T(8,128)(2,1)} %get-tuple-element.62) | copy-start | bytes 3145732

commit v5 on v4

--- a/solution.py
+++ b/solution.py
@@ -632,19 +632,25 @@
 
     def tick(now):
         k, odd = now // 2, now % 2
-
-        def stage(work, chunk):
-            if 0 <= chunk < CHUNKS:
-                work(chunk)
+        work = [(stage_f, k - 1), (stage_d, k - 3)] if odd else [(stage_s, k), (stage_x, k - 2)]
+        work = {
+            16: [(stage_s, EARLY)],
+            17: [(stage_x, EARLY - 1)],
+            18: [(stage_s, EARLY + 1)],
+        }.get(now, work)
 
         @pl.when(is_mid)
         def _():
-            if odd:
-                stage(stage_f, k - 1)
-                stage(stage_d, k - 3)
-            else:
-                stage(stage_s, k)
-                stage(stage_x, k - 2)
+            for stage, chunk in work:
+                if 0 <= chunk < CHUNKS:
+                    stage(chunk)
+
+    def ahead():
+        @pl.when(is_mid)
+        def _():
+            stage_x(EARLY - 2)
+            stage_f(EARLY - 1)
+            stage_d(EARLY - 3)
 
     send_outward(0, FIRST)
 
@@ -853,10 +859,6 @@
             def _():
                 out_store(step - 2).wait()
 
-            @pl.when(step == 5)
-            def _():
-                tick(9)
-
             own_pair[slot] = contract(
                 image_buf[slot, :, 0:feed], down_buf[...].reshape(8 * rows, feed), 1, 1
             ).astype(jnp.bfloat16)
@@ -900,7 +902,7 @@
     for step, _ in enumerate(own_flow(1, finish_feed)):
         tick((8, 10, 11)[step])
         if step == 0:
-            out_products()
+            tick(9)
     for slot in range(4):
         plane.gone(second_buf.at[slot], core_send.at[1, slot])
 
@@ -973,6 +975,7 @@
             def _(number=number):
                 give(second_buf.at[number], first_buf, 2, number // 2)
 
+    ahead()
 
     for block in range(8):
         in_buf[block] = out_sum[:, block * rows : (block + 1) * rows].astype(jnp.bfloat16)
@@ -996,10 +999,16 @@
     out_copy.wait()
     send_outward(EARLY, CHUNKS)
     tick(16)
-    run(own_flow(2, finish_input), 17)
+    tick(17)
+    for step, _ in enumerate(own_flow(2, finish_input)):
+        for now in ((18, 19), (20,), (21,))[step]:
+            tick(now)
+        if step == 0:
+            out_products()
     return_tokens(own_grad, token_grad, 1)
     for step, _ in enumerate(staged_flow(partial_out, grad_all, 0, finish_out)):
-        tick(20 + step)
+        for now in ((22, 23), (24,), (25,))[step]:
+            tick(now)
     return_tokens(image_out, token_out, 0)
 
     mod_copies = []
@@ -1012,22 +1021,20 @@
         )
         copy.start()
         mod_copies.append(copy)
-    tick(23)
-    tick(24)
+    tick(26)
     for copy in mod_copies:
         copy.wait_recv()
     own = pltpu.make_async_copy(mod_land, mod_out.at[mine], mod_sems.at[0, 3])
     own.start()
     mod_gather = Gather(plane, mod_land, mod_out, mod_gather_sems.at[0], mod_gather_sems.at[1])
     mod_gather.start()
-    tick(25)
-    tick(26)
+    tick(27)
     mod_gather.middle()
     mod_gather.far()
     for flip in (1, 3, 5, 7):
         mod_gather.crossed(flip)
     mod_gather.finish()
-    for now in range(27, 2 * CHUNKS + 6):
+    for now in range(28, 2 * CHUNKS + 6):
         tick(now)
     own.wait()
     for copy in mod_copies:
@@ -1124,44 +1131,6 @@
         ),
         name="back_part",
     )(*operands)
-
-
-def mlp_spread_kernel(share_ref, out_ref):
-    size = share_ref.shape[-1]
-    for number in range(4):
-        out_ref[:, number * size : (number + 1) * size] = share_ref[number, 0].astype(jnp.float32)
-
-
-def mlp_spread(shares):
-    rows = shares.shape[2]
-    return pl.pallas_call(
-        mlp_spread_kernel,
-        grid=(2, 8),
-        out_shape=jax.ShapeDtypeStruct((rows, 64 * rows), jnp.float32),
-        in_specs=[pl.BlockSpec((4, 1, rows, rows), lambda part, block: (1 - part, block, 0, 0))],
-        out_specs=pl.BlockSpec((rows, 4 * rows), lambda part, block: (0, part * 8 + block)),
-        compiler_params=pltpu.CompilerParams(vmem_limit_bytes=VMEM_BYTES),
-        name="mlp_spread",
-    )(shares)
-
-
-def attn_spread_kernel(share_ref, out_ref):
-    size = share_ref.shape[-1]
-    for number in range(8):
-        out_ref[:, number * size : (number + 1) * size] = share_ref[0, number].astype(jnp.float32)
-
-
-def attn_spread(shares):
-    rows = shares.shape[2]
-    return pl.pallas_call(
-        attn_spread_kernel,
-        grid=(4,),
-        out_shape=jax.ShapeDtypeStruct((rows, 32 * rows), jnp.float32),
-        in_specs=[pl.BlockSpec((1, 8, rows, rows), lambda part: (EARLY + part, 0, 0, 0))],
-        out_specs=pl.BlockSpec((rows, 8 * rows), lambda part: (0, part)),
-        compiler_params=pltpu.CompilerParams(vmem_limit_bytes=VMEM_BYTES),
-        name="attn_spread",
-    )(shares)
 
 
 class Gather:
@@ -1788,35 +1757,55 @@
     )
 
 
-def mod_grads_kernel(
-    rows_ref, onehot_ref, noise_ref, weight_ref, weight_grad_ref, noise_grad_ref, bias_ref, chosen, total
+def tail_kernel(
+    mlp_ref,
+    attn_ref,
+    rows_ref,
+    onehot_ref,
+    noise_ref,
+    weight_ref,
+    out_ref,
+    grad_ref,
+    mlp_grad_ref,
+    attn_grad_ref,
+    weight_grad_ref,
+    noise_grad_ref,
+    bias_ref,
+    block_out_ref,
+    input_grad_ref,
+    chosen,
+    total,
 ):
-    part = pl.program_id(0)
+    step = pl.program_id(0)
+    size = mlp_ref.shape[-1]
+    for number in range(4):
+        mlp_grad_ref[:, number * size : (number + 1) * size] = mlp_ref[number, 0].astype(
+            jnp.float32
+        )
+    for number in range(2):
+        attn_grad_ref[:, number * size : (number + 1) * size] = attn_ref[0, number].astype(
+            jnp.float32
+        )
+    block_out_ref[...] = out_ref[...]
+    input_grad_ref[...] = grad_ref[...].astype(jnp.float32)
     noise = noise_ref[...]
     onehot = onehot_ref[...]
     rise = 1.0 / (1.0 + jnp.exp(-noise))
 
-    def exact(left, right, left_dim, right_dim):
-        return lax.dot_general(
-            left,
-            right,
-            (((left_dim,), (right_dim,)), ((), ())),
-            precision=PRECISE,
-            preferred_element_type=jnp.float32,
-        )
-
-    @pl.when(part == 0)
+    @pl.when(step == 0)
     def _():
-        chosen[...] = exact(onehot, noise * rise, 1, 0)
+        chosen[...] = jnp.dot(
+            onehot, noise * rise, precision=PRECISE, preferred_element_type=jnp.float32
+        )
         total[...] = jnp.zeros_like(total)
 
-    grads = rows_ref[0]
+    grads = rows_ref[...]
     bias_ref[...] = jnp.broadcast_to(jnp.sum(grads, axis=0, keepdims=True), bias_ref.shape)
     low = grads.astype(jnp.bfloat16)
     weight_grad_ref[...] = contract(chosen[...].astype(jnp.bfloat16), low, 0, 0)
     total[...] += contract(weight_ref[...].astype(jnp.bfloat16), low, 1, 1)
 
-    @pl.when(part == pl.num_programs(0) - 1)
+    @pl.when(step == pl.num_programs(0) - 1)
     def _():
         table = lax.dot_general(
             onehot,
@@ -1828,35 +1817,52 @@
         noise_grad_ref[...] = table * (rise + noise * rise * (1.0 - rise))
 
 
-def mod_grads(image_rows, onehot, noise, weight):
-    images, _, width = image_rows.shape
-    depth = weight.shape[0]
+def tail_part(shares, image_rows, onehot, noise, weight, token_out, token_grad):
+    steps = 16
+    rows = shares.shape[2]
+    images = image_rows.shape[0]
+    depth, columns = weight.shape
+    part = columns // steps
+    slots, local_tok, width = token_out.shape
+    token_spec = pl.BlockSpec((1, local_tok, width // 4), lambda step: (step // 4, 0, step % 4))
     return pl.pallas_call(
-        mod_grads_kernel,
-        grid=(12,),
+        tail_kernel,
+        grid=(steps,),
         out_shape=[
+            jax.ShapeDtypeStruct((rows, 64 * rows), jnp.float32),
+            jax.ShapeDtypeStruct((rows, 32 * rows), jnp.float32),
             jax.ShapeDtypeStruct(weight.shape, jnp.float32),
             jax.ShapeDtypeStruct(noise.shape, jnp.float32),
-            jax.ShapeDtypeStruct((8, 6 * width), jnp.float32),
+            jax.ShapeDtypeStruct((8, columns), jnp.float32),
+            jax.ShapeDtypeStruct(token_out.shape, jnp.bfloat16),
+            jax.ShapeDtypeStruct(token_grad.shape, jnp.float32),
         ],
         in_specs=[
-            pl.BlockSpec((1, images, width // 2), lambda part: (part // 2, 0, part % 2)),
-            pl.BlockSpec(onehot.shape, lambda part: (0, 0)),
-            pl.BlockSpec(noise.shape, lambda part: (0, 0)),
-            pl.BlockSpec((depth, width // 2), lambda part: (0, part)),
+            pl.BlockSpec((4, 1, rows, rows), lambda step: (1 - step // 8, step % 8, 0, 0)),
+            pl.BlockSpec((1, 2, rows, rows), lambda step: (EARLY + step // 4, step % 4, 0, 0)),
+            pl.BlockSpec((images, part), lambda step: (0, step)),
+            pl.BlockSpec(onehot.shape, lambda step: (0, 0)),
+            pl.BlockSpec(noise.shape, lambda step: (0, 0)),
+            pl.BlockSpec((depth, part), lambda step: (0, step)),
+            token_spec,
+            token_spec,
         ],
         out_specs=[
-            pl.BlockSpec((depth, width // 2), lambda part: (0, part)),
-            pl.BlockSpec(noise.shape, lambda part: (0, 0)),
-            pl.BlockSpec((8, width // 2), lambda part: (0, part)),
+            pl.BlockSpec((rows, 4 * rows), lambda step: (0, step)),
+            pl.BlockSpec((rows, 2 * rows), lambda step: (0, step)),
+            pl.BlockSpec((depth, part), lambda step: (0, step)),
+            pl.BlockSpec(noise.shape, lambda step: (0, 0)),
+            pl.BlockSpec((8, part), lambda step: (0, step)),
+            token_spec,
+            token_spec,
         ],
         scratch_shapes=[
             pltpu.VMEM((images, depth), jnp.float32),
             pltpu.VMEM((depth, images), jnp.float32),
         ],
         compiler_params=pltpu.CompilerParams(vmem_limit_bytes=VMEM_BYTES),
-        name="mod_grads",
-    )(image_rows.transpose(1, 0, 2), onehot, noise, weight)
+        name="tail_part",
+    )(shares, shares, image_rows, onehot, noise, weight, token_out, token_grad)
 
 
 def plane_body(
@@ -1928,11 +1934,23 @@
         mod_rows,
     )
     mod_out = mod_out.reshape(8, 4, 8, model_width)
-    block_out, input_grad = token_out, token_grad.astype(jnp.float32)
-    attn_weight_grad, mlp_weight_grad = attn_spread(shares), mlp_spread(shares)
     onehot_all = mod_out[:, :, 7, :bins].reshape(-1, bins)
-    mod_weight_grad, noise_grad, bias_sums = mod_grads(
-        mod_out.reshape(-1, 8, model_width), onehot_all, noise_table, mod_weight
+    (
+        mlp_weight_grad,
+        attn_weight_grad,
+        mod_weight_grad,
+        noise_grad,
+        bias_sums,
+        block_out,
+        input_grad,
+    ) = tail_part(
+        shares,
+        mod_out[:, :, :6].reshape(-1, 6 * model_width),
+        onehot_all,
+        noise_table,
+        mod_weight,
+        token_out,
+        token_grad,
     )
     mod_bias_grad = lax.dynamic_slice_in_dim(bias_sums[0], mine * bias_piece, bias_piece)
     return (

time: 703 us -> 677 us (0.963)
  Pallas kernels: 687 us -> 664 us
    pallas_call x1, Pallas kernels: 424 us -> 409 us  [back_part(): pl.pallas_call(back_kernel, out_shape=[jax.ShapeDtypeStruct((CHUNKS, 8, r...]
    pallas_call x3 -> x1, Pallas kernels: 36.2 us -> 28.8 us  [tail_part(): pl.pallas_call(tail_kernel, grid=(steps,), out_shape=[jax.ShapeDtypeStruc...]
where the time goes in v5:
time: 677 us; the launch traced here: 673 us
  Pallas kernels  664 us (98%)
  local copies, waits for them, and re-layouts  8.16 us (1%)
    pallas_call x1, Pallas kernels, back_part(): pl.pallas_call(back_kernel, out_shape=[jax.ShapeDtypeStruct((CHUNKS, 8, r...  409 us
    pallas_call x1, Pallas kernels, front_part(): pl.pallas_call(front_kernel, out_shape=[jax.ShapeDtypeStruct((8, rows, co...  226 us
    pallas_call x1, Pallas kernels, tail_part(): pl.pallas_call(tail_kernel, grid=(steps,), out_shape=[jax.ShapeDtypeStruc...  28.8 us

profile of v5, /device:TPU:0, one launch (start us, length us, event | category | flops | bytes accessed | tf_op | source)
XLA Modules:
  0.0 673.1 jit_solution(3406475391481142623)
XLA Ops:
  0.6 1.3 reshape.30.mod_bias
  2.6 226.2 %front_part.1 = (bf16[8,256,768]{2,1,0:T(8,128)(2,1)}, bf16[256,2048]{1,0:T(8,128)(2,1)}, bf16[8,256,1024]{2,1,0:T(8,128)(2,1)}, bf16[8,256,1024]{2,1,0:T(8,128)...) custom-call(s32[4]{0:T(128)} %bin_ids.1, ...), custom_call_target="tpu_custom_call" | custom-call | tf_op jit(solution)/shard_map/front_part/pallas_call | solution.py:1685
  228.8 408.6 %back_part.1 = (bf16[12,8,256,256]{3,2,1,0:T(8,128)(2,1)}, bf16[4,64,2048]{2,1,0:T(8,128)(2,1)}, bf16[4,64,2048]{2,1,0:T(8,128)(2,1)}, f32[8,32,2048]{2,1,0:T(8,...) custom-call(bf16[8,256,1024]{2,1,0:T(8,128)(2,1)} %get-tuple-element, ...), custom_call_target="tpu_custom_call" | custom-call | tf_op jit(solution)/shard_map/back_part/pallas_call | solution.py:1076
  637.4 3.7 copy.17
  641.1 1.5 slice.13
  642.6 28.8 %tail_part.1 = (f32[256,16384]{1,0:T(8,128)}, f32[256,8192]{1,0:T(8,128)}, f32[256,12288]{1,0:T(8,128)}, f32[64,256]{1,0:T(8,128)}, f32[8,12288]{1,0:T(8,128)}, ...) custom-call(bf16[12,8,256,256]{3,2,1,0:T(8,128)(2,1)} %get-tuple-element.52.mlp_ref.attn_ref, ...), custom_call_target="tpu_custom_call" | custom-call | tf_op jit(solution)/shard_map/tail_part/pallas_call | solution.py:1828
  671.4 1.0 slice.11
  672.5 0.6 dynamic-slice_reduce_fusion

commit v6 on v5

--- a/solution.py
+++ b/solution.py
@@ -489,12 +489,12 @@
     h_all,
     qkv_all,
     attended_all,
-    qkv_weight,
-    out_weight,
-    features,
-    first_sum,
-    attn_out,
-    grad_out,
+    qkv_weight_in,
+    out_weight_in,
+    features_in,
+    first_sum_in,
+    attn_out_in,
+    grad_out_in,
     mod,
     shares,
     token_out,
@@ -524,6 +524,12 @@
     half_in,
     mod_sum,
     mod_land,
+    qkv_weight,
+    out_weight,
+    features,
+    first_sum,
+    attn_out,
+    grad_out,
     core_send,
     core_recv,
     far_send,
@@ -656,6 +662,19 @@
 
     attended_load = pltpu.make_async_copy(attended_all, attended_buf, load_sems.at[0])
     attended_load.start()
+    fetches = [
+        pltpu.make_async_copy(source, result, load_sems.at[13 + number])
+        for number, (source, result) in enumerate(
+            (
+                (first_sum_in, first_sum),
+                (grad_out_in, grad_out),
+                (attn_out_in, attn_out),
+                (out_weight_in, out_weight),
+                (qkv_weight_in, qkv_weight),
+                (features_in, features),
+            )
+        )
+    ]
     feed = up_weight.shape[-1]
 
     pltpu.make_async_copy(
@@ -671,6 +690,8 @@
         ).start()
     up_load = pltpu.make_async_copy(up_weight, grad_all.at[:, :, pl.ds(0, feed)], load_sems.at[5])
     up_load.start()
+    for fetch in fetches:
+        fetch.start()
     mod_sum[...] = jnp.zeros_like(mod_sum)
     row = {
         name: number
@@ -899,6 +920,8 @@
     tick(6)
     up_products()
     send_outward(FIRST, EARLY)
+    for fetch in fetches:
+        fetch.wait()
     for step, _ in enumerate(own_flow(1, finish_feed)):
         tick((8, 10, 11)[step])
         if step == 0:
@@ -1085,7 +1108,7 @@
             jax.ShapeDtypeStruct((CHUNKS, 8, rows, rows), low),
             jax.ShapeDtypeStruct((CHUNKS, 8, HALF_ROWS, rows), low),
         ],
-        in_specs=[anywhere] * 10 + [inside] * 7,
+        in_specs=[anywhere] * 16 + [inside],
         out_specs=[anywhere] * 8,
         scratch_shapes=[
             pltpu.VMEM((7, rows, width), low),
@@ -1108,6 +1131,12 @@
             pltpu.VMEM((8, HALF_ROWS, rows), low),
             pltpu.VMEM((8, width), full),
             pltpu.VMEM((32, width), full),
+            pltpu.VMEM((8 * rows, columns), low),
+            pltpu.VMEM((rows, width), low),
+            pltpu.VMEM((rows, width), low),
+            pltpu.VMEM((rows, width), full),
+            pltpu.VMEM((rows, width), low),
+            pltpu.VMEM((rows, width), low),
             dma((3, 4)),
             dma((3, 4)),
             dma((3, 2)),
@@ -1117,7 +1146,7 @@
             dma((2, 4)),
             dma((7 * PIECES,)),
             dma((7 * PIECES,)),
-            dma((13,)),
+            dma((19,)),
             dma((2, 8)),
             dma((2, 5, CHUNKS)),
             dma((2, CHUNKS)),
@@ -1218,7 +1247,7 @@
     mlp_weight,
     mod_weight,
     qkv_weight,
-    out_weight,
+    out_weight_out,
     up_weight,
     down_low,
     h_one_all,
@@ -1229,11 +1258,11 @@
     hidden_all,
     slope_all,
     first_grads,
-    features,
-    first_sum,
-    attn_out,
-    grad_out,
-    mod,
+    features_out,
+    first_sum_out,
+    attn_out_out,
+    grad_out_out,
+    mod_out,
     load_buf,
     qkv_stage,
     up_stage,
@@ -1253,6 +1282,12 @@
     bin_land,
     mod_part,
     mod_land,
+    out_weight,
+    features,
+    first_sum,
+    attn_out,
+    grad_out,
+    mod,
     load_sems,
     token_sems,
     bin_sems,
@@ -1279,6 +1314,20 @@
     flips = (6, 7, 2, 4, 3, 5, 1, 0)
     greet([plane.to(flip) for flip in range(1, 8)] + [(mine, other) for other in others])
 
+    results = [
+        pltpu.make_async_copy(source, result, copy_sems.at[14 + number])
+        for number, (source, result) in enumerate(
+            (
+                (mod, mod_out),
+                (features, features_out),
+                (grad_out, grad_out_out),
+                (out_weight, out_weight_out),
+                (first_sum, first_sum_out),
+                (attn_out, attn_out_out),
+            )
+        )
+    ]
+
     token_copies = []
     my_rows = pl.ds(pl.multiple_of(place * piece, piece), piece)
     for number, (source, result) in enumerate(((block_input, features), (cotangent, grad_out))):
@@ -1462,6 +1511,7 @@
     mod[6:7, :] = jnp.full((1, width), 1.0, jnp.float32) * live
     mod[7:8, :] = jnp.zeros((1, width), jnp.float32)
     mod[7:8, :128] = bin_row[0:1, :]
+    results[0].start()
 
     def mod_row(number):
         return mod[number : number + 1, :]
@@ -1474,6 +1524,7 @@
                 copy.wait_recv()
 
     tokens_arrived(0)
+    results[1].start()
 
     def first_norm(band):
         source = plain(features, band)
@@ -1493,6 +1544,7 @@
         own_grad[band, :] = (mod_row(5) * scaled).astype(jnp.bfloat16)
 
     bands(rows, feed_grad)
+    results[2].start()
     grad_own = pltpu.make_async_copy(own_grad, grad_mlp_all.at[mine], copy_sems.at[0])
     grad_own.start()
     grad_gather = Gather(plane, own_grad, grad_mlp_all, gather_sems.at[1, 0], gather_sems.at[1, 1])
@@ -1532,6 +1584,7 @@
         out_weight[band, :] = load_buf[0, band, :].astype(jnp.bfloat16)
 
     bands(rows, cast_out)
+    results[3].start()
 
     weights_ready(qkv_stage, qkv_weight, 0, 3 * HD)
     load = pltpu.make_async_copy(qkv_weight, weight_buf, copy_sems.at[1])
@@ -1614,6 +1667,8 @@
         plane.gone(part_buf.at[slot], core_send.at[slot])
     next_gather = Gather(plane, own_next, h_all, gather_sems.at[2, 0], gather_sems.at[2, 1])
     next_gather.start()
+    results[4].start()
+    results[5].start()
     grad_gather.far()
     weights_ready(up_stage, up_weight, 1, feed // 2)
     load = pltpu.make_async_copy(up_weight, up_stage, copy_sems.at[1])
@@ -1655,7 +1710,7 @@
     )
     for gather in (grad_gather, next_gather):
         gather.finish()
-    for copy in keeps:
+    for copy in keeps + results:
         copy.wait()
     for copies in token_copies:
         for copy in copies[1:]:
@@ -1704,7 +1759,7 @@
             jax.ShapeDtypeStruct((8, width), full),
         ],
         in_specs=[scalars] * 2 + [inside] * 2 + [anywhere] * 5,
-        out_specs=[anywhere, inside] + [anywhere] * 10 + [inside] * 5,
+        out_specs=[anywhere] * 17,
         scratch_shapes=[
             pltpu.VMEM((2, rows, width), full),
             pltpu.VMEM((8, rows, columns), low),
@@ -1725,6 +1780,12 @@
             pltpu.VMEM((8, 8, 128), full),
             pltpu.VMEM((8, 8, width), full),
             pltpu.VMEM((8, 8, width), full),
+            pltpu.VMEM((rows, width), low),
+            pltpu.VMEM((rows, width), low),
+            pltpu.VMEM((rows, width), full),
+            pltpu.VMEM((rows, width), low),
+            pltpu.VMEM((rows, width), low),
+            pltpu.VMEM((8, width), full),
             dma((2, 3)),
             dma((2, 2, 4)),
             dma((2, 8)),
@@ -1738,7 +1799,7 @@
             dma((2,)),
             dma((4,)),
             dma((4,)),
-            dma((14,)),
+            dma((20,)),
         ],
         compiler_params=pltpu.CompilerParams(
             collective_id=5, has_side_effects=True, vmem_limit_bytes=63 * 1024 * 1024
@@ -1761,7 +1822,6 @@
     mlp_ref,
     attn_ref,
     rows_ref,
-    onehot_ref,
     noise_ref,
     weight_ref,
     out_ref,
@@ -1775,6 +1835,8 @@
     input_grad_ref,
     chosen,
     total,
+    flat_rows,
+    onehot_rows,
 ):
     step = pl.program_id(0)
     size = mlp_ref.shape[-1]
@@ -1789,17 +1851,22 @@
     block_out_ref[...] = out_ref[...]
     input_grad_ref[...] = grad_ref[...].astype(jnp.float32)
     noise = noise_ref[...]
-    onehot = onehot_ref[...]
     rise = 1.0 / (1.0 + jnp.exp(-noise))
+    part = weight_ref.shape[1]
 
     @pl.when(step == 0)
     def _():
+        width = rows_ref.shape[2]
+        for row in range(6):
+            flat_rows[:, row * width : (row + 1) * width] = rows_ref[:, row, :]
+        onehot = rows_ref[:, 7, : noise.shape[0]]
+        onehot_rows[...] = onehot
         chosen[...] = jnp.dot(
             onehot, noise * rise, precision=PRECISE, preferred_element_type=jnp.float32
         )
         total[...] = jnp.zeros_like(total)
 
-    grads = rows_ref[...]
+    grads = flat_rows[:, pl.ds(pl.multiple_of(step * part, 128), part)]
     bias_ref[...] = jnp.broadcast_to(jnp.sum(grads, axis=0, keepdims=True), bias_ref.shape)
     low = grads.astype(jnp.bfloat16)
     weight_grad_ref[...] = contract(chosen[...].astype(jnp.bfloat16), low, 0, 0)
@@ -1808,7 +1875,7 @@
     @pl.when(step == pl.num_programs(0) - 1)
     def _():
         table = lax.dot_general(
-            onehot,
+            onehot_rows[...],
             total[...],
             (((0,), (1,)), ((), ())),
             precision=PRECISE,
@@ -1817,7 +1884,7 @@
         noise_grad_ref[...] = table * (rise + noise * rise * (1.0 - rise))
 
 
-def tail_part(shares, image_rows, onehot, noise, weight, token_out, token_grad):
+def tail_part(shares, image_rows, noise, weight, token_out, token_grad):
     steps = 16
     rows = shares.shape[2]
     images = image_rows.shape[0]
@@ -1840,8 +1907,7 @@
         in_specs=[
             pl.BlockSpec((4, 1, rows, rows), lambda step: (1 - step // 8, step % 8, 0, 0)),
             pl.BlockSpec((1, 2, rows, rows), lambda step: (EARLY + step // 4, step % 4, 0, 0)),
-            pl.BlockSpec((images, part), lambda step: (0, step)),
-            pl.BlockSpec(onehot.shape, lambda step: (0, 0)),
+            pl.BlockSpec(image_rows.shape, lambda step: (0, 0, 0)),
             pl.BlockSpec(noise.shape, lambda step: (0, 0)),
             pl.BlockSpec((depth, part), lambda step: (0, step)),
             token_spec,
@@ -1859,10 +1925,12 @@
         scratch_shapes=[
             pltpu.VMEM((images, depth), jnp.float32),
             pltpu.VMEM((depth, images), jnp.float32),
+            pltpu.VMEM((images, columns), jnp.float32),
+            pltpu.VMEM((images, noise.shape[0]), jnp.float32),
         ],
         compiler_params=pltpu.CompilerParams(vmem_limit_bytes=VMEM_BYTES),
         name="tail_part",
-    )(shares, shares, image_rows, onehot, noise, weight, token_out, token_grad)
+    )(shares, shares, image_rows, noise, weight, token_out, token_grad)
 
 
 def plane_body(
@@ -1878,7 +1946,6 @@
 ):
     model_width = block_input.shape[2]
     rows = attn_weight.shape[0]
-    bins = noise_table.shape[0]
     bias_piece = mod_bias.shape[0]
     mine = lax.axis_index("fsdp")
     (
@@ -1933,8 +2000,6 @@
         grad_out,
         mod_rows,
     )
-    mod_out = mod_out.reshape(8, 4, 8, model_width)
-    onehot_all = mod_out[:, :, 7, :bins].reshape(-1, bins)
     (
         mlp_weight_grad,
         attn_weight_grad,
@@ -1945,8 +2010,7 @@
         input_grad,
     ) = tail_part(
         shares,
-        mod_out[:, :, :6].reshape(-1, 6 * model_width),
-        onehot_all,
+        mod_out.reshape(-1, 8, model_width),
         noise_table,
         mod_weight,
         token_out,

time: 677 us -> 668 us (0.987)
  no operation moved by 1% of the time
where the time goes in v6:
time: 668 us; the launch traced here: 664 us
  Pallas kernels  660 us (99%)
    pallas_call x1, Pallas kernels, back_part(): pl.pallas_call(back_kernel, out_shape=[jax.ShapeDtypeStruct((CHUNKS, 8, r...  406 us
    pallas_call x1, Pallas kernels, front_part(): pl.pallas_call(front_kernel, out_shape=[jax.ShapeDtypeStruct((8, rows, co...  224 us
    pallas_call x1, Pallas kernels, tail_part(): pl.pallas_call(tail_kernel, grid=(steps,), out_shape=[jax.ShapeDtypeStruc...  30 us

profile of v6, /device:TPU:0, one launch (start us, length us, event | category | flops | bytes accessed | tf_op | source)
XLA Modules:
  0.0 663.8 jit_solution(11908324763180198804)
XLA Ops:
  0.6 1.3 reshape.27.mod_bias
  2.6 223.7 %front_part.1 = (bf16[8,256,768]{2,1,0:T(8,128)(2,1)}, bf16[256,2048]{1,0:T(8,128)(2,1)}, bf16[8,256,1024]{2,1,0:T(8,128)(2,1)}, bf16[8,256,1024]{2,1,0:T(8,128)...) custom-call(s32[4]{0:T(128)} %bin_ids.1, ...), custom_call_target="tpu_custom_call" | custom-call | tf_op jit(solution)/shard_map/front_part/pallas_call | solution.py:1740
  226.3 405.8 %back_part.1 = (bf16[12,8,256,256]{3,2,1,0:T(8,128)(2,1)}, bf16[4,64,2048]{2,1,0:T(8,128)(2,1)}, bf16[4,64,2048]{2,1,0:T(8,128)(2,1)}, f32[8,32,2048]{2,1,0:T(8,...) custom-call(bf16[8,256,1024]{2,1,0:T(8,128)(2,1)} %get-tuple-element, ...), custom_call_target="tpu_custom_call" | custom-call | tf_op jit(solution)/shard_map/back_part/pallas_call | solution.py:1099
  632.1 30.0 %tail_part.1 = (f32[256,16384]{1,0:T(8,128)}, f32[256,8192]{1,0:T(8,128)}, f32[256,12288]{1,0:T(8,128)}, f32[64,256]{1,0:T(8,128)}, f32[8,12288]{1,0:T(8,128)}, ...) custom-call(bf16[12,8,256,256]{3,2,1,0:T(8,128)(2,1)} %get-tuple-element.52.mlp_ref.attn_ref, ...), custom_call_target="tpu_custom_call" | custom-call | tf_op jit(solution)/shard_map/tail_part/pallas_call | solution.py:1895
  662.1 1.0 slice.3
  663.1 0.6 dynamic-slice_reduce_fusion

commit v7 on v6

--- a/solution.py
+++ b/solution.py
@@ -587,7 +587,7 @@
         load = pltpu.make_async_copy(land_b.at[k], half_in, zload_sems.at[2])
         plane.got(land_b.at[k], z_sems.at[1, 1, k])
         load.start()
-        if k >= 2:
+        if k >= 2 and k - 2 != EARLY:
             plane.gone(half_buf.at[slot, pl.ds(0, 7)], x_sems.at[0, k - 2])
         load.wait()
 
@@ -595,7 +595,7 @@
         def _(block):
             half_buf[slot, block] = sum_buf[slot, block, my_half, :] + half_in[block]
 
-        if k == CHUNKS - 1:
+        if k == EARLY:
             pltpu.make_async_copy(
                 half_buf.at[slot], shares.at[k, :, my_half], x_sems.at[1, k]
             ).start()
@@ -1002,27 +1002,33 @@
 
     for block in range(8):
         in_buf[block] = out_sum[:, block * rows : (block + 1) * rows].astype(jnp.bfloat16)
-    out_copy = pltpu.make_async_copy(in_buf, more.at[7], load_sems.at[0])
+    out_copy = pltpu.make_async_copy(in_buf, more.at[4], load_sems.at[0])
     out_copy.start()
+    out_copy.wait()
+    send_outward(EARLY, EARLY + 1)
+    tick(16)
+    def late_hook(block):
+        @pl.when(block == 3)
+        def _():
+            tick(17)
+
     column_products(
         h_all,
         saved_grad.at[:, pl.ds(0, columns)],
         cols_buf,
         staged_buf,
-        more.at[pl.ds(4, 3)],
+        more.at[pl.ds(5, 3)],
         load_sems.at[pl.ds(3, 2)],
         load_sems.at[pl.ds(11, 2)],
         [[(3 * head + number) * HD for head in range(third // HD)] for number in range(3)],
+        late_hook,
     )
 
     def finish_input(where, value):
         total = back_norm(plain(features, where), value, "scale_one", "shift_one")
         own_pair[0, where, :] = (total + grad_first[where, :]).astype(jnp.bfloat16)
 
-    out_copy.wait()
-    send_outward(EARLY, CHUNKS)
-    tick(16)
-    tick(17)
+    send_outward(EARLY + 1, CHUNKS)
     for step, _ in enumerate(own_flow(2, finish_input)):
         for now in ((18, 19), (20,), (21,))[step]:
             tick(now)
@@ -1072,7 +1078,8 @@
     def _():
         for k in (CHUNKS - 2, CHUNKS - 1):
             plane.gone(sum_buf.at[k % 2, :, other_half], z_sems.at[0, 1, k])
-        plane.gone(half_buf.at[0, pl.ds(0, 7)], x_sems.at[0, CHUNKS - 2])
+        for k in (CHUNKS - 2, CHUNKS - 1):
+            plane.gone(half_buf.at[k % 2, pl.ds(0, 7)], x_sems.at[0, k])
         for k in range(CHUNKS):
             plane.gone(shares.at[k, :, my_half], z_sems.at[0, 2, k])
             plane.gone(shares.at[k, :, my_half], z_sems.at[0, 3, k])
@@ -1906,7 +1913,7 @@
         ],
         in_specs=[
             pl.BlockSpec((4, 1, rows, rows), lambda step: (1 - step // 8, step % 8, 0, 0)),
-            pl.BlockSpec((1, 2, rows, rows), lambda step: (EARLY + step // 4, step % 4, 0, 0)),
+            pl.BlockSpec((1, 2, rows, rows), lambda step: (EARLY + (step // 4 + 1) % 4, step % 4, 0, 0)),
             pl.BlockSpec(image_rows.shape, lambda step: (0, 0, 0)),
             pl.BlockSpec(noise.shape, lambda step: (0, 0)),
             pl.BlockSpec((depth, part), lambda step: (0, step)),

time: 668 us -> 664 us (level)
  no operation moved by 1% of the time
where the time goes in v7:
time: 664 us; the launch traced here: 661 us
  Pallas kernels  657 us (99%)
    pallas_call x1, Pallas kernels, back_part(): pl.pallas_call(back_kernel, out_shape=[jax.ShapeDtypeStruct((CHUNKS, 8, r...  403 us
    pallas_call x1, Pallas kernels, front_part(): pl.pallas_call(front_kernel, out_shape=[jax.ShapeDtypeStruct((8, rows, co...  224 us
    pallas_call x1, Pallas kernels, tail_part(): pl.pallas_call(tail_kernel, grid=(steps,), out_shape=[jax.ShapeDtypeStruc...  30 us

profile of v7, /device:TPU:0, one launch (start us, length us, event | category | flops | bytes accessed | tf_op | source)
XLA Modules:
  0.0 660.8 jit_solution(8379833906438741086)
XLA Ops:
  0.6 1.3 reshape.27.mod_bias
  2.6 223.7 %front_part.1 = (bf16[8,256,768]{2,1,0:T(8,128)(2,1)}, bf16[256,2048]{1,0:T(8,128)(2,1)}, bf16[8,256,1024]{2,1,0:T(8,128)(2,1)}, bf16[8,256,1024]{2,1,0:T(8,128)...) custom-call(s32[4]{0:T(128)} %bin_ids.1, ...), custom_call_target="tpu_custom_call" | custom-call | tf_op jit(solution)/shard_map/front_part/pallas_call | solution.py:1747
  226.3 402.9 %back_part.1 = (bf16[12,8,256,256]{3,2,1,0:T(8,128)(2,1)}, bf16[4,64,2048]{2,1,0:T(8,128)(2,1)}, bf16[4,64,2048]{2,1,0:T(8,128)(2,1)}, f32[8,32,2048]{2,1,0:T(8,...) custom-call(bf16[8,256,1024]{2,1,0:T(8,128)(2,1)} %get-tuple-element, ...), custom_call_target="tpu_custom_call" | custom-call | tf_op jit(solution)/shard_map/back_part/pallas_call | solution.py:1106
  629.2 30.0 %tail_part.1 = (f32[256,16384]{1,0:T(8,128)}, f32[256,8192]{1,0:T(8,128)}, f32[256,12288]{1,0:T(8,128)}, f32[64,256]{1,0:T(8,128)}, f32[8,12288]{1,0:T(8,128)}, ...) custom-call(bf16[12,8,256,256]{3,2,1,0:T(8,128)(2,1)} %get-tuple-element.52.mlp_ref.attn_ref, ...), custom_call_target="tpu_custom_call" | custom-call | tf_op jit(solution)/shard_map/tail_part/pallas_call | solution.py:1902
  659.2 1.0 slice.3
  660.2 0.6 dynamic-slice_reduce_fusion

commit v8 on v7

--- a/solution.py
+++ b/solution.py
@@ -1847,11 +1847,11 @@
 ):
     step = pl.program_id(0)
     size = mlp_ref.shape[-1]
+    for number in range(8):
+        mlp_grad_ref[:, number * size : (number + 1) * size] = mlp_ref[
+            number % 4, number // 4
+        ].astype(jnp.float32)
     for number in range(4):
-        mlp_grad_ref[:, number * size : (number + 1) * size] = mlp_ref[number, 0].astype(
-            jnp.float32
-        )
-    for number in range(2):
         attn_grad_ref[:, number * size : (number + 1) * size] = attn_ref[0, number].astype(
             jnp.float32
         )
@@ -1892,13 +1892,13 @@
 
 
 def tail_part(shares, image_rows, noise, weight, token_out, token_grad):
-    steps = 16
+    steps = 8
     rows = shares.shape[2]
     images = image_rows.shape[0]
     depth, columns = weight.shape
     part = columns // steps
     slots, local_tok, width = token_out.shape
-    token_spec = pl.BlockSpec((1, local_tok, width // 4), lambda step: (step // 4, 0, step % 4))
+    token_spec = pl.BlockSpec((1, local_tok, width // 2), lambda step: (step // 2, 0, step % 2))
     return pl.pallas_call(
         tail_kernel,
         grid=(steps,),
@@ -1912,8 +1912,8 @@
             jax.ShapeDtypeStruct(token_grad.shape, jnp.float32),
         ],
         in_specs=[
-            pl.BlockSpec((4, 1, rows, rows), lambda step: (1 - step // 8, step % 8, 0, 0)),
-            pl.BlockSpec((1, 2, rows, rows), lambda step: (EARLY + (step // 4 + 1) % 4, step % 4, 0, 0)),
+            pl.BlockSpec((4, 2, rows, rows), lambda step: (1 - step // 4, step % 4, 0, 0)),
+            pl.BlockSpec((1, 4, rows, rows), lambda step: (EARLY + (step // 2 + 1) % 4, step % 2, 0, 0)),
             pl.BlockSpec(image_rows.shape, lambda step: (0, 0, 0)),
             pl.BlockSpec(noise.shape, lambda step: (0, 0)),
             pl.BlockSpec((depth, part), lambda step: (0, step)),
@@ -1921,8 +1921,8 @@
             token_spec,
         ],
         out_specs=[
+            pl.BlockSpec((rows, 8 * rows), lambda step: (0, step)),
             pl.BlockSpec((rows, 4 * rows), lambda step: (0, step)),
-            pl.BlockSpec((rows, 2 * rows), lambda step: (0, step)),
             pl.BlockSpec((depth, part), lambda step: (0, step)),
             pl.BlockSpec(noise.shape, lambda step: (0, 0)),
             pl.BlockSpec((8, part), lambda step: (0, step)),

time: 664 us -> 660 us (level)
  no operation moved by 1% of the time
where the time goes in v8:
time: 660 us; the launch traced here: 657 us
  Pallas kernels  653 us (99%)
    pallas_call x1, Pallas kernels, back_part(): pl.pallas_call(back_kernel, out_shape=[jax.ShapeDtypeStruct((CHUNKS, 8, r...  403 us
    pallas_call x1, Pallas kernels, front_part(): pl.pallas_call(front_kernel, out_shape=[jax.ShapeDtypeStruct((8, rows, co...  224 us
    pallas_call x1, Pallas kernels, tail_part(): pl.pallas_call(tail_kernel, grid=(steps,), out_shape=[jax.ShapeDtypeStruc...  26 us

profile of v8, /device:TPU:0, one launch (start us, length us, event | category | flops | bytes accessed | tf_op | source)
XLA Modules:
  0.0 656.9 jit_solution(8383118597424378019)
XLA Ops:
  0.6 1.3 reshape.27.mod_bias
  2.6 223.7 %front_part.1 = (bf16[8,256,768]{2,1,0:T(8,128)(2,1)}, bf16[256,2048]{1,0:T(8,128)(2,1)}, bf16[8,256,1024]{2,1,0:T(8,128)(2,1)}, bf16[8,256,1024]{2,1,0:T(8,128)...) custom-call(s32[4]{0:T(128)} %bin_ids.1, ...), custom_call_target="tpu_custom_call" | custom-call | tf_op jit(solution)/shard_map/front_part/pallas_call | solution.py:1747
  226.3 402.9 %back_part.1 = (bf16[12,8,256,256]{3,2,1,0:T(8,128)(2,1)}, bf16[4,64,2048]{2,1,0:T(8,128)(2,1)}, bf16[4,64,2048]{2,1,0:T(8,128)(2,1)}, f32[8,32,2048]{2,1,0:T(8,...) custom-call(bf16[8,256,1024]{2,1,0:T(8,128)(2,1)} %get-tuple-element, ...), custom_call_target="tpu_custom_call" | custom-call | tf_op jit(solution)/shard_map/back_part/pallas_call | solution.py:1106
  629.2 26.0 %tail_part.1 = (f32[256,16384]{1,0:T(8,128)}, f32[256,8192]{1,0:T(8,128)}, f32[256,12288]{1,0:T(8,128)}, f32[64,256]{1,0:T(8,128)}, f32[8,12288]{1,0:T(8,128)}, ...) custom-call(bf16[12,8,256,256]{3,2,1,0:T(8,128)(2,1)} %get-tuple-element.52.mlp_ref.attn_ref, ...), custom_call_target="tpu_custom_call" | custom-call | tf_op jit(solution)/shard_map/tail_part/pallas_call | solution.py:1902
  655.2 1.0 slice.3
  656.2 0.6 dynamic-slice_reduce_fusion
